TPU v7x, 32 devices: a whole 2x2x4 slice. The times are simulated.
32 devices in a mesh: seq: 8 (over z, y), batch: 4 (over x, core).
Axes of the slice: x: 2, y: 2, z: 4, core: 2. Of those that a mesh axis runs over, the one named last changes fastest.
Arguments:
- layer_entries: bfloat16 [1024, 8, 2048], P('seq', 'batch'), may hold values from -6 to 6
- incoming_adjoint: bfloat16 [1024, 8, 2048], P('seq', 'batch'), may hold values from -6 to 6
- mixing_rescale_scalers: bfloat16 [2048], P(('seq', 'batch')), may hold values from 0.5 to 1.5
- triple_projector_matrix: bfloat16 [2048, 6144], P(('seq', 'batch')), may hold values from -0.1875 to 0.1875
- context_exit_matrix: bfloat16 [2048, 2048], P(('seq', 'batch')), may hold values from -0.5 to 0.5
- dense_center_scaler: bfloat16 [2048], P(('seq', 'batch')), may hold values from 0.5 to 1.5
- dense_center_offset: bfloat16 [2048], P(('seq', 'batch')), may hold values from -1.5 to 1.5
- expand_matrix: bfloat16 [2048, 8192], P(('seq', 'batch')), may hold values from -0.125 to 0.125
- shrink_matrix: bfloat16 [8192, 2048], P(('seq', 'batch')), may hold values from -0.0625 to 0.0625
- span_chooser_initial: bfloat16 [2048, 256], P(('seq', 'batch')), may hold values from -0.125 to 0.125
- span_chooser_final: bfloat16 [256, 4], P(('seq', 'batch')), may hold values from -0.375 to 0.375
- heat_divisor: float32 [1], replicated, may hold values from 0.7 to 1.4
- sample_channel_fourths: int32 [8], P('batch'), may hold values from 1 to 4
- element_preset_span: int32 [1024, 8], P('seq', 'batch'), may hold values from 0 to 4, as said below
- spot_group_table: int32 [8], replicated, may hold values from 0 to 7, each once
Outputs:
- output: bfloat16 [1024, 8, 2048], P('seq', 'batch')
- grad_tokens: bfloat16 [1024, 8, 2048], P('seq', 'batch')
- grad_gain_attn: float32 [2048], P(('seq', 'batch'))
- grad_w_qkv: float32 [2048, 6144], P(('seq', 'batch'))
- grad_w_out: float32 [2048, 2048], P(('seq', 'batch'))
- grad_gain_ffn: float32 [2048], P(('seq', 'batch'))
- grad_bias_ffn: float32 [2048], P(('seq', 'batch'))
- grad_w_up: float32 [2048, 8192], P(('seq', 'batch'))
- grad_w_down: float32 [8192, 2048], P(('seq', 'batch'))
- grad_router_in: float32 [2048, 256], P(('seq', 'batch'))
- grad_router_out: float32 [256, 4], P(('seq', 'batch'))
Inputs may be any that keep to these rules, and one draw needn't show every extreme that they name: A permutation: index j of seq holds block spot_group_table[j] of the positions of every sequence. `element_preset_span`: 0 lets the router mix the widths; k > 0 gives the token the k-th nested width, its first k * 2048 hidden units.
All inputs are finite; a program needn't handle non-finite values.
Results may differ from a plain program's by a relative error of at most 0.02.
Values may be sent and summed in bfloat16 or wider, within the bound.
No kernel may reach another device: no remote copies, remote signals or barrier semaphores. Data moves between devices by JAX's collectives and lax.ppermute only.
A program may use at most 576 MiB of HBM per device.

v0:
```python
import math

import jax
import jax.numpy as jnp
from jax import lax
from jax.sharding import PartitionSpec as P

H = 16
HD = 128
FF = 8192


epsilon = 1e-05
theta_base = 10000.0
neg_large = -1e30


def from_behind(block, axis, distance):
    devices = range(lax.axis_size(axis))
    route = [((i - distance) % len(devices), i) for i in devices]
    return lax.ppermute(block, axis, route)


def contract_rows(left_mat, right_mat):
    return lax.dot_general(
        left_mat, right_mat, (((0,), (0,)), ((), ())), preferred_element_type=jnp.float32
    )


def contract_cols(left_mat, right_mat):
    return lax.dot_general(
        left_mat, right_mat, (((1,), (1,)), ((), ())), preferred_element_type=jnp.float32
    )


def order_lookup(spot_group_table, shard_index):
    slot_ids = jnp.arange(spot_group_table.shape[0], dtype=jnp.int32)
    return jnp.sum(jnp.where(slot_ids == shard_index, spot_group_table, 0))


def rotary_tables(positions, head_dim):
    half_dim = head_dim // 2
    inverse = theta_base ** (-(jnp.arange(half_dim, dtype=jnp.float32) * (2.0 / head_dim)))
    angles = positions.astype(jnp.float32)[:, None] * inverse[None, :]
    cosine_table = jnp.concatenate([jnp.cos(angles), jnp.cos(angles)], axis=1)
    sine_table = jnp.concatenate([jnp.sin(angles), jnp.sin(angles)], axis=1)
    return (cosine_table[:, None, None, :], sine_table[:, None, None, :])


def rotate_half(values):
    lead_half, tail_half = jnp.split(values, 2, axis=-1)
    return jnp.concatenate([-tail_half, lead_half], axis=-1)


def rotate_back(values):
    lead_half, tail_half = jnp.split(values, 2, axis=-1)
    return jnp.concatenate([tail_half, -lead_half], axis=-1)


def backward_block(
    query_part,
    grad_part,
    log_part,
    dot_part,
    query_places,
    key_part,
    value_part,
    key_places,
    score_scale,
):
    scores = (
        jnp.einsum("qshd,kshd->shqk", query_part, key_part, preferred_element_type=jnp.float32)
        * score_scale
    )
    allowed = key_places[None, :] <= query_places[:, None]
    prob_vals = jnp.where(allowed, jnp.exp(scores - log_part[..., None]), 0.0)
    grad_value = jnp.einsum(
        "shqk,qshd->kshd",
        prob_vals.astype(jnp.bfloat16),
        grad_part,
        preferred_element_type=jnp.float32,
    )
    grad_prob = jnp.einsum(
        "qshd,kshd->shqk", grad_part, value_part, preferred_element_type=jnp.float32
    )
    grad_score = (prob_vals * (grad_prob - dot_part[..., None])).astype(jnp.bfloat16)
    grad_query = (
        jnp.einsum("shqk,kshd->qshd", grad_score, key_part, preferred_element_type=jnp.float32)
        * score_scale
    )
    grad_key = (
        jnp.einsum("shqk,qshd->kshd", grad_score, query_part, preferred_element_type=jnp.float32)
        * score_scale
    )
    return (grad_query, grad_key, grad_value)


def per_device(
    layer_entries,
    incoming_adjoint,
    mixing_rescale_scalers,
    triple_projector_matrix,
    context_exit_matrix,
    dense_center_scaler,
    dense_center_offset,
    expand_matrix,
    shrink_matrix,
    span_chooser_initial,
    span_chooser_final,
    heat_divisor,
    sample_channel_fourths,
    element_preset_span,
    spot_group_table,
):
    block_len, seq_count, model_width = layer_entries.shape
    tok_rows = block_len * seq_count
    head_count = H
    head_dim = HD
    band_width = FF // 4
    score_scale = 1.0 / math.sqrt(HD)
    circle_size = lax.axis_size("seq")
    circle_index = lax.axis_index("seq")
    offsets = jnp.arange(block_len, dtype=jnp.int32)

    def block_places(shard_index):
        return order_lookup(spot_group_table, shard_index) * block_len + offsets

    query_places = block_places(circle_index)
    cosine_table, sine_table = rotary_tables(query_places, head_dim)
    active = (
        (jnp.arange(head_count, dtype=jnp.int32) // (head_count // 4))[None, :]
        < sample_channel_fourths[:, None]
    ).astype(jnp.float32)
    head_mask = active[None, :, :, None]

    def split_heads(values):
        return values.reshape(block_len, seq_count, head_count, head_dim)

    qkv_full, out_full, gain_one = (
        lax.all_gather(triple_projector_matrix, ("seq", "batch"), axis=0, tiled=True),
        lax.all_gather(context_exit_matrix, ("seq", "batch"), axis=0, tiled=True),
        lax.all_gather(mixing_rescale_scalers, ("seq", "batch"), axis=0, tiled=True),
    )
    up_full, down_full, gain_two, bias_two, route_in, route_out = (
        lax.all_gather(expand_matrix, ("seq", "batch"), axis=0, tiled=True),
        lax.all_gather(shrink_matrix, ("seq", "batch"), axis=0, tiled=True),
        lax.all_gather(dense_center_scaler, ("seq", "batch"), axis=0, tiled=True),
        lax.all_gather(dense_center_offset, ("seq", "batch"), axis=0, tiled=True),
        lax.all_gather(span_chooser_initial, ("seq", "batch"), axis=0, tiled=True),
        lax.all_gather(span_chooser_final, ("seq", "batch"), axis=0, tiled=True),
    )
    inputs = layer_entries.astype(jnp.float32).reshape(tok_rows, model_width)
    inv_rms = lax.rsqrt(jnp.mean(inputs * inputs, axis=1, keepdims=True) + epsilon)
    scaled = inputs * inv_rms
    normed = (scaled * gain_one.astype(jnp.float32)).astype(jnp.bfloat16)
    joint_proj = jnp.dot(normed, qkv_full, preferred_element_type=jnp.float32)
    query_raw, key_raw, value_raw = jnp.split(joint_proj, 3, axis=1)
    queries = (
        split_heads(query_raw) * cosine_table + rotate_half(split_heads(query_raw)) * sine_table
    ).astype(jnp.bfloat16)
    key_heads = (
        split_heads(key_raw) * cosine_table + rotate_half(split_heads(key_raw)) * sine_table
    ).astype(jnp.bfloat16)
    value_heads = split_heads(value_raw).astype(jnp.bfloat16)
    key_rows = key_heads.reshape(block_len, seq_count, model_width)
    value_rows = value_heads.reshape(block_len, seq_count, model_width)
    start_state = (
        jnp.full((seq_count, head_count, block_len), neg_large, jnp.float32),
        jnp.zeros((seq_count, head_count, block_len), jnp.float32),
        jnp.zeros((block_len, seq_count, head_count, head_dim), jnp.float32),
    )
    carried = start_state
    piece_keys = lax.all_gather(key_rows, "seq", axis=0, tiled=True)
    piece_values = lax.all_gather(value_rows, "seq", axis=0, tiled=True)
    block_total = piece_keys.shape[0] // block_len
    key_blocks = piece_keys.reshape(block_total, block_len, seq_count, head_count, head_dim)
    value_blocks = piece_values.reshape(block_total, block_len, seq_count, head_count, head_dim)
    shard_ids = jnp.arange(block_total, dtype=jnp.int32)

    def absorb(running, block_item):
        maxima, totals, accumulated = running
        blk_keys, blk_values, shard_index = block_item
        key_places = block_places(shard_index)
        scores = (
            jnp.einsum("qshd,kshd->shqk", queries, blk_keys, preferred_element_type=jnp.float32)
            * score_scale
        )
        allowed = key_places[None, :] <= query_places[:, None]
        top_score = jnp.maximum(maxima, jnp.max(jnp.where(allowed, scores, neg_large), axis=-1))
        weights = jnp.where(allowed, jnp.exp(scores - top_score[..., None]), 0.0)
        factor = jnp.exp(maxima - top_score)
        totals = totals * factor + jnp.sum(weights, axis=-1)
        accumulated = accumulated * jnp.transpose(factor, (2, 0, 1))[..., None] + jnp.einsum(
            "shqk,kshd->qshd",
            weights.astype(jnp.bfloat16),
            blk_values,
            preferred_element_type=jnp.float32,
        )
        return ((top_score, totals, accumulated), None)

    carried, unused = lax.scan(absorb, carried, (key_blocks, value_blocks, shard_ids))
    maxima, totals, accumulated = carried
    heads_out = accumulated / jnp.transpose(totals, (2, 0, 1))[..., None]
    log_norm = maxima + jnp.log(totals)
    attended = (heads_out * head_mask).astype(jnp.bfloat16).reshape(tok_rows, model_width)
    hidden = inputs + jnp.dot(attended, out_full, preferred_element_type=jnp.float32)
    centre = jnp.mean(hidden, axis=1, keepdims=True)
    centered = hidden - centre
    variance = jnp.mean(centered * centered, axis=1, keepdims=True)
    inv_std = lax.rsqrt(variance + epsilon)
    normal = centered * inv_std
    ffn_in = (normal * gain_two.astype(jnp.float32) + bias_two.astype(jnp.float32)).astype(
        jnp.bfloat16
    )
    squashed = jnp.tanh(jnp.dot(ffn_in, route_in, preferred_element_type=jnp.float32))
    squashed_low = squashed.astype(jnp.bfloat16)
    logits = jnp.dot(squashed_low, route_out, preferred_element_type=jnp.float32)
    smoothing_coefficient = heat_divisor[0]
    routed = jax.nn.softmax(logits / smoothing_coefficient, axis=1)
    forced = element_preset_span.reshape(tok_rows)
    is_forced = (forced > 0)[:, None]
    chosen = (forced[:, None] - 1 == jnp.arange(4, dtype=jnp.int32)[None, :]).astype(jnp.float32)
    width_mix = jnp.where(is_forced, chosen, routed)
    upper_ones = (jnp.arange(4)[:, None] >= jnp.arange(4)[None, :]).astype(jnp.float32)
    band_scale = jnp.dot(
        width_mix, upper_ones, precision=lax.Precision.HIGHEST, preferred_element_type=jnp.float32
    )
    up_proj = jnp.dot(ffn_in, up_full, preferred_element_type=jnp.float32)
    rectified = jnp.maximum(up_proj, 0.0)
    activated = (rectified * rectified).reshape(tok_rows, 4, band_width)
    gated_act = (activated * band_scale[:, :, None]).astype(jnp.bfloat16).reshape(tok_rows, FF)
    output = hidden + jnp.dot(gated_act, down_full, preferred_element_type=jnp.float32)
    result = output.astype(jnp.bfloat16).reshape(block_len, seq_count, model_width)
    grad_out = incoming_adjoint.reshape(tok_rows, model_width)
    grad_down = contract_rows(gated_act, grad_out)
    grad_gated = contract_cols(grad_out, down_full).reshape(tok_rows, 4, band_width)
    grad_band = jnp.sum(grad_gated * activated, axis=2)
    grad_mix = jnp.dot(
        grad_band, upper_ones.T, precision=lax.Precision.HIGHEST, preferred_element_type=jnp.float32
    )
    grad_up = (grad_gated * band_scale[:, :, None]).reshape(tok_rows, FF) * (2.0 * rectified)
    grad_up_low = grad_up.astype(jnp.bfloat16)
    grad_wup = contract_rows(ffn_in, grad_up_low)
    grad_ffn_in = contract_cols(grad_up_low, up_full)
    grad_logits = jnp.where(
        is_forced,
        0.0,
        routed
        * (grad_mix - jnp.sum(routed * grad_mix, axis=1, keepdims=True))
        / smoothing_coefficient,
    )
    grad_logits_low = grad_logits.astype(jnp.bfloat16)
    grad_route_out = contract_rows(squashed_low, grad_logits_low)
    grad_squash = contract_cols(grad_logits_low, route_out)
    grad_pre_low = (grad_squash * (1.0 - squashed * squashed)).astype(jnp.bfloat16)
    grad_route_in = contract_rows(ffn_in, grad_pre_low)
    grad_ffn_in = grad_ffn_in + contract_cols(grad_pre_low, route_in)
    grad_gain_two = jnp.sum(grad_ffn_in * normal, axis=0)
    grad_bias_two = jnp.sum(grad_ffn_in, axis=0)
    grad_normal = grad_ffn_in * gain_two.astype(jnp.float32)
    grad_hidden = grad_out.astype(jnp.float32) + inv_std * (
        grad_normal
        - jnp.mean(grad_normal, axis=1, keepdims=True)
        - normal * jnp.mean(grad_normal * normal, axis=1, keepdims=True)
    )
    ffn_grads = (
        lax.psum_scatter(grad_wup, ("seq", "batch"), scatter_dimension=0, tiled=True),
        lax.psum_scatter(grad_down, ("seq", "batch"), scatter_dimension=0, tiled=True),
        lax.psum_scatter(grad_gain_two, ("seq", "batch"), scatter_dimension=0, tiled=True),
        lax.psum_scatter(grad_bias_two, ("seq", "batch"), scatter_dimension=0, tiled=True),
        lax.psum_scatter(grad_route_in, ("seq", "batch"), scatter_dimension=0, tiled=True),
        lax.psum_scatter(grad_route_out, ("seq", "batch"), scatter_dimension=0, tiled=True),
    )
    grad_attn = grad_hidden.astype(jnp.bfloat16)
    grad_wout = contract_rows(attended, grad_attn)
    grad_heads = (split_heads(contract_cols(grad_attn, out_full)) * head_mask).astype(jnp.bfloat16)
    grad_dot = jnp.transpose(
        jnp.sum(grad_heads.astype(jnp.float32) * heads_out, axis=-1), (1, 2, 0)
    )

    def pass_keys(pair_rows):
        return from_behind((pair_rows[0], pair_rows[1]), "seq", 1)

    def pass_key_grads(pair_grads):
        return (
            from_behind(pair_grads[0].astype(jnp.bfloat16), "seq", 1).astype(jnp.float32),
            from_behind(pair_grads[1].astype(jnp.bfloat16), "seq", 1).astype(jnp.float32),
        )

    grad_query, key_grad_part, value_grad_part = backward_block(
        queries,
        grad_heads,
        log_norm,
        grad_dot,
        query_places,
        key_heads,
        value_heads,
        query_places,
        score_scale,
    )

    def circle_turn(turn_index, carried):
        moving_keys, moving_values, moving_dkey, moving_dvalue, query_total = carried
        moving_keys, moving_values = pass_keys((moving_keys, moving_values))
        moving_dkey, moving_dvalue = pass_key_grads((moving_dkey, moving_dvalue))
        anchor_places = block_places((circle_index - turn_index) % circle_size)
        query_new, key_new, value_new = backward_block(
            queries,
            grad_heads,
            log_norm,
            grad_dot,
            query_places,
            moving_keys,
            moving_values,
            anchor_places,
            score_scale,
        )
        return (
            moving_keys,
            moving_values,
            moving_dkey + key_new,
            moving_dvalue + value_new,
            query_total + query_new,
        )

    carried = lax.fori_loop(
        1,
        circle_size,
        circle_turn,
        (key_heads, value_heads, key_grad_part, value_grad_part, grad_query),
    )
    grad_key, grad_value = pass_key_grads((carried[2], carried[3]))
    grad_query = carried[4]
    grad_query_raw = grad_query * cosine_table + rotate_back(grad_query * sine_table)
    grad_key_raw = grad_key * cosine_table + rotate_back(grad_key * sine_table)
    grad_joint = jnp.concatenate(
        [
            grad_query_raw.reshape(tok_rows, model_width),
            grad_key_raw.reshape(tok_rows, model_width),
            grad_value.reshape(tok_rows, model_width),
        ],
        axis=1,
    ).astype(jnp.bfloat16)
    grad_wqkv = contract_rows(normed, grad_joint)
    grad_normed = contract_cols(grad_joint, qkv_full)
    grad_gain_one = jnp.sum(grad_normed * scaled, axis=0)
    grad_scaled = grad_normed * gain_one.astype(jnp.float32)
    grad_inputs = grad_hidden + inv_rms * (
        grad_scaled - scaled * jnp.mean(grad_scaled * scaled, axis=1, keepdims=True)
    )
    attn_grads = (
        lax.psum_scatter(grad_wqkv, ("seq", "batch"), scatter_dimension=0, tiled=True),
        lax.psum_scatter(grad_wout, ("seq", "batch"), scatter_dimension=0, tiled=True),
        lax.psum_scatter(grad_gain_one, ("seq", "batch"), scatter_dimension=0, tiled=True),
    )
    grad_tokens = grad_inputs.astype(jnp.bfloat16).reshape(block_len, seq_count, model_width)
    return (
        result,
        grad_tokens,
        attn_grads[2],
        attn_grads[0],
        attn_grads[1],
        ffn_grads[2],
        ffn_grads[3],
        ffn_grads[0],
        ffn_grads[1],
        ffn_grads[4],
        ffn_grads[5],
    )


def solution(mesh):
    placed = (
        P("seq", "batch", None),
        P("seq", "batch", None),
        P(("seq", "batch")),
        P(("seq", "batch"), None),
        P(("seq", "batch"), None),
        P(("seq", "batch")),
        P(("seq", "batch")),
        P(("seq", "batch"), None),
        P(("seq", "batch"), None),
        P(("seq", "batch"), None),
        P(("seq", "batch"), None),
        P(),
        P("batch"),
        P("seq", "batch"),
        P(),
    )
    return jax.shard_map(
        per_device,
        mesh=mesh,
        in_specs=placed,
        out_specs=(
            P("seq", "batch", None),
            P("seq", "batch", None),
            P(("seq", "batch")),
            P(("seq", "batch"), None),
            P(("seq", "batch"), None),
            P(("seq", "batch")),
            P(("seq", "batch")),
            P(("seq", "batch"), None),
            P(("seq", "batch"), None),
            P(("seq", "batch"), None),
            P(("seq", "batch"), None),
        ),
        check_vma=False,
    )
```

profile of v0, /device:TPU:0, one launch (start us, length us, event | category | flops | bytes accessed | tf_op | source)
XLA Modules:
  0.0 3807.3 jit_solution(1703116361642868371)
XLA Ops:
  10.5 43.5 %all-reduce.8 = (bf16[2048]{0:T(1024)(128)(2,1)S(1)}, bf16[2048]{0:T(1024)(128)(2,1)S(1)}, bf16[2048]{0:T(1024)(128)(2,1)S(1)}) all-reduce(bf16[2048]{0:T(1024)(128)(2,1)S(1)} %dynamic-update-slice, bf16[2048]{0:T(1024)(128)(2,1)S(1)} %dynamic-update-slice.2, ...), channel_id=1, replica_groups=mesh['seq'=8,'batch'=4] {'seq','batch'}, use_global_device_ids=true, to_apply=%add | all-reduce | flops 6144 | bytes 24576
  56.7 112.8 %all-gather.9.cloned.1.call-done = bf16[2048,6144]{1,0:T(8,128)(2,1)} async-done(((bf16[64,6144]{1,0:T(8,128)(2,1)}), bf16[2048,6144]{1,0:T(8,128)(2,1)}) %all-gather.9.cloned.1.call-update) | async-done | bytes 25165840 | tf_op jit(solution)/shard_map/all_gather | solution.py:140
  224.8 39.2 %all-gather = bf16[32,8,4]{1,2,0:T(4,128)(2,1)S(1)} all-gather(bf16[1,8,4]{1,2,0:T(4,128)(2,1)S(1)} %bitcast.232), channel_id=1, replica_groups=mesh['seq'=8,'batch'=4] {'seq','batch'}, dimensions={0}, use_global_device_ids=true | all-gather | bytes 2112 | tf_op jit(solution)/shard_map/all_gather | solution.py:150
  265.3 44.2 %all-gather.13.cloned.1.call-done = bf16[1024,2,2048]{2,0,1:T(8,128)(2,1)} async-done(((bf16[128,2,2048]{2,0,1:T(8,128)(2,1)}), bf16[1024,2,2048]{2,0,1:T(8,128)(2,1)}) %all-gather.13.cloned.1.call-update) | async-done | bytes 8388624 | tf_op jit(solution)/shard_map/all_gather | solution.py:174
  319.7 116.1 %all-gather.11.cloned.1.call-done = bf16[1024,2,2048]{0,2,1:T(8,128)(2,1)} async-done(((bf16[128,2,2048]{0,2,1:T(8,128)(2,1)}), bf16[1024,2,2048]{0,2,1:T(8,128)(2,1)}) %all-gather.11.cloned.1.call-update) | async-done | bytes 8388624 | tf_op jit(solution)/shard_map/all_gather | solution.py:173
  457.1 89.5 %while.40 = (s32[]{:T(128)}, f32[2,16,128]{2,1,0:T(8,128)S(1)}, f32[2,16,128]{2,1,0:T(8,128)S(1)}, f32[128,2,16,128]{0,3,2,1:T(8,128)}, s32[8]{0:T(128)S(1)}, /*...) while((s32[]{:T(128)}, f32[2,16,128]{2,1,0:T(8,128)S(1)}, ...), condition=%wide.region_6.7_spmd.clone, body=%wide.region_2.6_spmd.clone.sunk | while | flops 275816736 | bytes 34933016 | solution.py:201
  571.4 194.3 %all-gather.17.cloned.1.call-done = bf16[2048,8192]{1,0:T(8,128)(2,1)} async-done(((bf16[64,8192]{1,0:T(8,128)(2,1)}), bf16[2048,8192]{1,0:T(8,128)(2,1)}) %all-gather.17.cloned.1.call-update) | async-done | bytes 33554448 | tf_op jit(solution)/shard_map/all_gather | solution.py:145
  785.6 175.9 %all-gather.21.cloned.1.call-done = bf16[8192,2048]{1,0:T(8,128)(2,1)} async-done(((bf16[256,2048]{1,0:T(8,128)(2,1)}), bf16[8192,2048]{1,0:T(8,128)(2,1)}) %all-gather.21.cloned.1.call-update) | async-done | bytes 33554448 | tf_op jit(solution)/shard_map/all_gather | solution.py:146
  1090.5 773.2 %while.39 = (s32[]{:T(128)}, bf16[128,2,16,128]{3,0,2,1:T(8,128)(2,1)}, bf16[128,2,16,128]{3,0,2,1:T(8,128)(2,1)}, bf16[128,2,16,128]{3,0,2,1:T(8,128)(2,1)}, bf...) while((s32[]{:T(128)}, ...), condition=%wide.region_18.19_spmd.clone, body=%wide.region_16.18_spmd.clone.sunk | while | flops 679493888 | bytes 62982700 | solution.py:326
  1097.1 24.0 collective-permute-done.1
  1122.1 22.8 collective-permute-done
  1149.3 32.4 collective-permute-done.3
  1185.5 27.4 collective-permute-done.2
  1225.1 37.1 collective-permute-done.1
  1263.2 32.3 collective-permute-done
  1299.9 29.3 collective-permute-done.3
  1333.1 27.2 collective-permute-done.2
  1370.5 37.9 collective-permute-done.1
  1409.4 21.6 collective-permute-done
  1481.5 25.8 collective-permute-done.1
  1508.3 21.6 collective-permute-done
  1579.6 25.5 collective-permute-done.1
  1606.0 21.6 collective-permute-done
  1676.7 25.2 collective-permute-done.1
  1772.9 24.9 collective-permute-done.1
  1868.4 26.8 collective-permute-done.4
  1937.4 31.1 fusion.72
  1969.8 42.1 %fusion.71 = f32[2048,8192]{1,0:T(8,128)} fusion(bf16[256,2048]{1,0:T(8,128)(2,1)S(1)} %copy-done.16, bf16[256,8192]{1,0:T(8,128)(2,1)} %get-tuple-element.605), kind=kOutput, calls=%fused_computation.166 | convolution fusion | flops 8589934592 | bytes 72351744 | tf_op jit(solution)/shard_map/dot_general | solution.py:25
  2047.1 59.1 %all-reduce.7 = (f32[2048]{0:T(1024)S(1)}, f32[2048]{0:T(1024)S(1)}, f32[2048]{0:T(1024)S(1)}, f32[256,4]{0,1:T(4,128)S(1)}) all-reduce(f32[2048]{0:T(1024)S(1)} %get-tuple-element.538, f32[2048]{0:T(1024)S(1)} %copy-done.48, f32[2048]{0:T(1024)S(1)} %copy-done.49, ...), channel_id=2, replica_groups=mesh['seq'=8,'batch'=4] {'seq','batch'}, use_global_device_ids=true, to_apply=%region_21.22.clone | all-reduce | flops 7168 | bytes 57344
  2112.9 269.6 %reduce-scatter.7.cloned.1.call-done = f32[64,6144]{1,0:T(8,128)} async-done(((f32[2048,6144]{1,0:T(8,128)}), f32[64,6144]{1,0:T(8,128)}) %reduce-scatter.7.cloned.1.call-update) | async-done | bytes 1572880 | tf_op jit(solution)/shard_map/reduce_scatter | solution.py:352
  2382.4 704.6 %reduce-scatter.13.cloned.1.call-done = f32[256,2048]{1,0:T(8,128)} async-done(((f32[8192,2048]{1,0:T(8,128)}), f32[256,2048]{1,0:T(8,128)}) %reduce-scatter.13.cloned.1.call-update) | async-done | bytes 2097168 | tf_op jit(solution)/shard_map/reduce_scatter | solution.py:268
  3087.1 713.2 %reduce-scatter.11.cloned.1.call-done = f32[64,8192]{1,0:T(8,128)} async-done(((f32[2048,8192]{1,0:T(8,128)}), f32[64,8192]{1,0:T(8,128)}) %reduce-scatter.11.cloned.1.call-update) | async-done | bytes 2097168 | tf_op jit(solution)/shard_map/reduce_scatter | solution.py:267
  (575 shorter events, 770.6 us)
Async XLA Ops:
  7.2 162.4 %all-gather.9.cloned.1.call-start = ((), (), s32[]{:S(2)}) async-start(), calls=%async_computation.5 | async-start | bytes 25952256 | tf_op jit(solution)/shard_map/all_gather | solution.py:140
  7.9 301.6 %all-gather.13.cloned.1.call-start = ((), (), s32[]{:S(2)}) async-start(), calls=%async_computation.7 | async-start | bytes 9437184 | tf_op jit(solution)/shard_map/all_gather | solution.py:174
  186.1 249.6 %all-gather.11.cloned.1.call-start = ((), (), s32[]{:S(2)}) async-start(), calls=%async_computation.6 | async-start | bytes 9437184 | tf_op jit(solution)/shard_map/all_gather | solution.py:173
  218.7 331.5 %all-gather.15.cloned.1.call-start = ((), (), s32[]{:S(2)}) async-start(), calls=%async_computation.8 | async-start | bytes 8650752 | tf_op jit(solution)/shard_map/all_gather | solution.py:141
  219.3 349.9 %all-gather.19.cloned.1.call-start = ((), (), s32[]{:S(2)}) async-start(), calls=%async_computation.10 | async-start | bytes 1081344 | tf_op jit(solution)/shard_map/all_gather | solution.py:149
  219.9 545.8 %all-gather.17.cloned.1.call-start = ((), (), s32[]{:S(2)}) async-start(), calls=%async_computation.9 | async-start | bytes 34603008 | tf_op jit(solution)/shard_map/all_gather | solution.py:145
  220.4 741.0 %all-gather.21.cloned.1.call-start = ((), (), s32[]{:S(2)}) async-start(), calls=%async_computation.11 | async-start | bytes 34603008 | tf_op jit(solution)/shard_map/all_gather | solution.py:146
  221.2 1891.7 %reduce-scatter.15.cloned.1.call-start = ((), (), s32[]{:S(2)}) async-start(), calls=%async_computation.16 | async-start | bytes 2162688 | tf_op jit(solution)/shard_map/reduce_scatter | solution.py:271
  993.4 1119.4 %reduce-scatter.9.cloned.1.call-start = ((), (), s32[]{:S(2)}) async-start(), calls=%async_computation.13 | async-start | bytes 17301504 | tf_op jit(solution)/shard_map/reduce_scatter | solution.py:353
  1046.7 1335.7 %reduce-scatter.7.cloned.1.call-start = ((), (), s32[]{:S(2)}) async-start(), calls=%async_computation.12 | async-start | bytes 51904512 | tf_op jit(solution)/shard_map/reduce_scatter | solution.py:352
  1092.1 52.8 %collective-permute-start = (bf16[128,2,16,128]{3,0,2,1:T(8,128)(2,1)}, bf16[128,2,16,128]{3,0,2,1:T(8,128)(2,1)}, u32[]{:S(2)}, u32[]{:S(2)}) collective-permute-start(bf16[128,2,16,128]{3,0,2,1:T(8,128)(2,1)} %get-tuple-element.852), channel_id=1, source_target_pairs={{28,0},{0,4},{4,8},{8,12},{12,16},{16,20},{20,24},{24,28},{29,1},{... | collective-permute-start | bytes 3145736 | tf_op jit(solution)/shard_map/while/body/eval_jaxpr/ppermute | solution.py:21
  1092.2 89.5 %collective-permute-start.3 = (bf16[128,2,16,128]{3,0,2,1:T(8,128)(2,1)}, bf16[128,2,16,128]{3,0,2,1:T(8,128)(2,1)}, u32[]{:S(2)}, u32[]{:S(2)}) collective-permute-start(bf16[128,2,16,128]{3,0,2,1:T(8,128)(2,1)} %get-tuple-element.855), channel_id=1, source_target_pairs={{28,0},{0,4},{4,8},{8,12},{12,16},{16,20},{20,24},{24,28},{29,1},{... | collective-permute-start | bytes 3145736 | tf_op jit(solution)/shard_map/while/body/eval_jaxpr/ppermute | solution.py:21
  1093.3 119.6 %collective-permute-start.2 = (bf16[128,2,16,128]{3,0,2,1:T(8,128)(2,1)}, bf16[128,2,16,128]{3,0,2,1:T(8,128)(2,1)}, u32[]{:S(2)}, u32[]{:S(2)}) collective-permute-start(bf16[128,2,16,128]{3,0,2,1:T(8,128)(2,1)} %get-tuple-element.854), channel_id=1, source_target_pairs={{28,0},{0,4},{4,8},{8,12},{12,16},{16,20},{20,24},{24,28},{29,1},{... | collective-permute-start | bytes 3145736 | tf_op jit(solution)/shard_map/while/body/eval_jaxpr/ppermute | solution.py:21
  1222.1 73.4 %collective-permute-start = (bf16[128,2,16,128]{3,0,2,1:T(8,128)(2,1)}, bf16[128,2,16,128]{3,0,2,1:T(8,128)(2,1)}, u32[]{:S(2)}, u32[]{:S(2)}) collective-permute-start(bf16[128,2,16,128]{3,0,2,1:T(8,128)(2,1)} %get-tuple-element.852), channel_id=1, source_target_pairs={{28,0},{0,4},{4,8},{8,12},{12,16},{16,20},{20,24},{24,28},{29,1},{... | collective-permute-start | bytes 3145736 | tf_op jit(solution)/shard_map/while/body/eval_jaxpr/ppermute | solution.py:21
  1222.1 107.0 %collective-permute-start.3 = (bf16[128,2,16,128]{3,0,2,1:T(8,128)(2,1)}, bf16[128,2,16,128]{3,0,2,1:T(8,128)(2,1)}, u32[]{:S(2)}, u32[]{:S(2)}) collective-permute-start(bf16[128,2,16,128]{3,0,2,1:T(8,128)(2,1)} %get-tuple-element.855), channel_id=1, source_target_pairs={{28,0},{0,4},{4,8},{8,12},{12,16},{16,20},{20,24},{24,28},{29,1},{... | collective-permute-start | bytes 3145736 | tf_op jit(solution)/shard_map/while/body/eval_jaxpr/ppermute | solution.py:21
  1222.2 138.1 %collective-permute-start.2 = (bf16[128,2,16,128]{3,0,2,1:T(8,128)(2,1)}, bf16[128,2,16,128]{3,0,2,1:T(8,128)(2,1)}, u32[]{:S(2)}, u32[]{:S(2)}) collective-permute-start(bf16[128,2,16,128]{3,0,2,1:T(8,128)(2,1)} %get-tuple-element.854), channel_id=1, source_target_pairs={{28,0},{0,4},{4,8},{8,12},{12,16},{16,20},{20,24},{24,28},{29,1},{... | collective-permute-start | bytes 3145736 | tf_op jit(solution)/shard_map/while/body/eval_jaxpr/ppermute | solution.py:21
  1366.4 64.7 %collective-permute-start = (bf16[128,2,16,128]{3,0,2,1:T(8,128)(2,1)}, bf16[128,2,16,128]{3,0,2,1:T(8,128)(2,1)}, u32[]{:S(2)}, u32[]{:S(2)}) collective-permute-start(bf16[128,2,16,128]{3,0,2,1:T(8,128)(2,1)} %get-tuple-element.852), channel_id=1, source_target_pairs={{28,0},{0,4},{4,8},{8,12},{12,16},{16,20},{20,24},{24,28},{29,1},{... | collective-permute-start | bytes 3145736 | tf_op jit(solution)/shard_map/while/body/eval_jaxpr/ppermute | solution.py:21
  1366.4 87.1 %collective-permute-start.3 = (bf16[128,2,16,128]{3,0,2,1:T(8,128)(2,1)}, bf16[128,2,16,128]{3,0,2,1:T(8,128)(2,1)}, u32[]{:S(2)}, u32[]{:S(2)}) collective-permute-start(bf16[128,2,16,128]{3,0,2,1:T(8,128)(2,1)} %get-tuple-element.855), channel_id=1, source_target_pairs={{28,0},{0,4},{4,8},{8,12},{12,16},{16,20},{20,24},{24,28},{29,1},{... | collective-permute-start | bytes 3145736 | tf_op jit(solution)/shard_map/while/body/eval_jaxpr/ppermute | solution.py:21
  1368.5 103.7 %collective-permute-start.2 = (bf16[128,2,16,128]{3,0,2,1:T(8,128)(2,1)}, bf16[128,2,16,128]{3,0,2,1:T(8,128)(2,1)}, u32[]{:S(2)}, u32[]{:S(2)}) collective-permute-start(bf16[128,2,16,128]{3,0,2,1:T(8,128)(2,1)} %get-tuple-element.854), channel_id=1, source_target_pairs={{28,0},{0,4},{4,8},{8,12},{12,16},{16,20},{20,24},{24,28},{29,1},{... | collective-permute-start | bytes 3145736 | tf_op jit(solution)/shard_map/while/body/eval_jaxpr/ppermute | solution.py:21
  1478.3 51.6 %collective-permute-start = (bf16[128,2,16,128]{3,0,2,1:T(8,128)(2,1)}, bf16[128,2,16,128]{3,0,2,1:T(8,128)(2,1)}, u32[]{:S(2)}, u32[]{:S(2)}) collective-permute-start(bf16[128,2,16,128]{3,0,2,1:T(8,128)(2,1)} %get-tuple-element.852), channel_id=1, source_target_pairs={{28,0},{0,4},{4,8},{8,12},{12,16},{16,20},{20,24},{24,28},{29,1},{... | collective-permute-start | bytes 3145736 | tf_op jit(solution)/shard_map/while/body/eval_jaxpr/ppermute | solution.py:21
  1478.3 74.0 %collective-permute-start.3 = (bf16[128,2,16,128]{3,0,2,1:T(8,128)(2,1)}, bf16[128,2,16,128]{3,0,2,1:T(8,128)(2,1)}, u32[]{:S(2)}, u32[]{:S(2)}) collective-permute-start(bf16[128,2,16,128]{3,0,2,1:T(8,128)(2,1)} %get-tuple-element.855), channel_id=1, source_target_pairs={{28,0},{0,4},{4,8},{8,12},{12,16},{16,20},{20,24},{24,28},{29,1},{... | collective-permute-start | bytes 3145736 | tf_op jit(solution)/shard_map/while/body/eval_jaxpr/ppermute | solution.py:21
  1478.3 91.7 %collective-permute-start.2 = (bf16[128,2,16,128]{3,0,2,1:T(8,128)(2,1)}, bf16[128,2,16,128]{3,0,2,1:T(8,128)(2,1)}, u32[]{:S(2)}, u32[]{:S(2)}) collective-permute-start(bf16[128,2,16,128]{3,0,2,1:T(8,128)(2,1)} %get-tuple-element.854), channel_id=1, source_target_pairs={{28,0},{0,4},{4,8},{8,12},{12,16},{16,20},{20,24},{24,28},{29,1},{... | collective-permute-start | bytes 3145736 | tf_op jit(solution)/shard_map/while/body/eval_jaxpr/ppermute | solution.py:21
  1576.0 51.6 %collective-permute-start = (bf16[128,2,16,128]{3,0,2,1:T(8,128)(2,1)}, bf16[128,2,16,128]{3,0,2,1:T(8,128)(2,1)}, u32[]{:S(2)}, u32[]{:S(2)}) collective-permute-start(bf16[128,2,16,128]{3,0,2,1:T(8,128)(2,1)} %get-tuple-element.852), channel_id=1, source_target_pairs={{28,0},{0,4},{4,8},{8,12},{12,16},{16,20},{20,24},{24,28},{29,1},{... | collective-permute-start | bytes 3145736 | tf_op jit(solution)/shard_map/while/body/eval_jaxpr/ppermute | solution.py:21
  1576.0 74.0 %collective-permute-start.3 = (bf16[128,2,16,128]{3,0,2,1:T(8,128)(2,1)}, bf16[128,2,16,128]{3,0,2,1:T(8,128)(2,1)}, u32[]{:S(2)}, u32[]{:S(2)}) collective-permute-start(bf16[128,2,16,128]{3,0,2,1:T(8,128)(2,1)} %get-tuple-element.855), channel_id=1, source_target_pairs={{28,0},{0,4},{4,8},{8,12},{12,16},{16,20},{20,24},{24,28},{29,1},{... | collective-permute-start | bytes 3145736 | tf_op jit(solution)/shard_map/while/body/eval_jaxpr/ppermute | solution.py:21
  1576.0 90.8 %collective-permute-start.2 = (bf16[128,2,16,128]{3,0,2,1:T(8,128)(2,1)}, bf16[128,2,16,128]{3,0,2,1:T(8,128)(2,1)}, u32[]{:S(2)}, u32[]{:S(2)}) collective-permute-start(bf16[128,2,16,128]{3,0,2,1:T(8,128)(2,1)} %get-tuple-element.854), channel_id=1, source_target_pairs={{28,0},{0,4},{4,8},{8,12},{12,16},{16,20},{20,24},{24,28},{29,1},{... | collective-permute-start | bytes 3145736 | tf_op jit(solution)/shard_map/while/body/eval_jaxpr/ppermute | solution.py:21
  1672.9 74.0 %collective-permute-start.3 = (bf16[128,2,16,128]{3,0,2,1:T(8,128)(2,1)}, bf16[128,2,16,128]{3,0,2,1:T(8,128)(2,1)}, u32[]{:S(2)}, u32[]{:S(2)}) collective-permute-start(bf16[128,2,16,128]{3,0,2,1:T(8,128)(2,1)} %get-tuple-element.855), channel_id=1, source_target_pairs={{28,0},{0,4},{4,8},{8,12},{12,16},{16,20},{20,24},{24,28},{29,1},{... | collective-permute-start | bytes 3145736 | tf_op jit(solution)/shard_map/while/body/eval_jaxpr/ppermute | solution.py:21
  1672.9 89.8 %collective-permute-start.2 = (bf16[128,2,16,128]{3,0,2,1:T(8,128)(2,1)}, bf16[128,2,16,128]{3,0,2,1:T(8,128)(2,1)}, u32[]{:S(2)}, u32[]{:S(2)}) collective-permute-start(bf16[128,2,16,128]{3,0,2,1:T(8,128)(2,1)} %get-tuple-element.854), channel_id=1, source_target_pairs={{28,0},{0,4},{4,8},{8,12},{12,16},{16,20},{20,24},{24,28},{29,1},{... | collective-permute-start | bytes 3145736 | tf_op jit(solution)/shard_map/while/body/eval_jaxpr/ppermute | solution.py:21
  1768.8 51.6 %collective-permute-start = (bf16[128,2,16,128]{3,0,2,1:T(8,128)(2,1)}, bf16[128,2,16,128]{3,0,2,1:T(8,128)(2,1)}, u32[]{:S(2)}, u32[]{:S(2)}) collective-permute-start(bf16[128,2,16,128]{3,0,2,1:T(8,128)(2,1)} %get-tuple-element.852), channel_id=1, source_target_pairs={{28,0},{0,4},{4,8},{8,12},{12,16},{16,20},{20,24},{24,28},{29,1},{... | collective-permute-start | bytes 3145736 | tf_op jit(solution)/shard_map/while/body/eval_jaxpr/ppermute | solution.py:21
  1768.8 74.0 %collective-permute-start.3 = (bf16[128,2,16,128]{3,0,2,1:T(8,128)(2,1)}, bf16[128,2,16,128]{3,0,2,1:T(8,128)(2,1)}, u32[]{:S(2)}, u32[]{:S(2)}) collective-permute-start(bf16[128,2,16,128]{3,0,2,1:T(8,128)(2,1)} %get-tuple-element.855), channel_id=1, source_target_pairs={{28,0},{0,4},{4,8},{8,12},{12,16},{16,20},{20,24},{24,28},{29,1},{... | collective-permute-start | bytes 3145736 | tf_op jit(solution)/shard_map/while/body/eval_jaxpr/ppermute | solution.py:21
  1768.8 88.9 %collective-permute-start.2 = (bf16[128,2,16,128]{3,0,2,1:T(8,128)(2,1)}, bf16[128,2,16,128]{3,0,2,1:T(8,128)(2,1)}, u32[]{:S(2)}, u32[]{:S(2)}) collective-permute-start(bf16[128,2,16,128]{3,0,2,1:T(8,128)(2,1)} %get-tuple-element.854), channel_id=1, source_target_pairs={{28,0},{0,4},{4,8},{8,12},{12,16},{16,20},{20,24},{24,28},{29,1},{... | collective-permute-start | bytes 3145736 | tf_op jit(solution)/shard_map/while/body/eval_jaxpr/ppermute | solution.py:21
  1936.2 1150.9 %reduce-scatter.13.cloned.1.call-start = ((), (), s32[]{:S(2)}) async-start(), calls=%async_computation.15 | async-start | bytes 69206016 | tf_op jit(solution)/shard_map/reduce_scatter | solution.py:268
  1968.5 1831.8 %reduce-scatter.11.cloned.1.call-start = ((), (), s32[]{:S(2)}) async-start(), calls=%async_computation.14 | async-start | bytes 69206016 | tf_op jit(solution)/shard_map/reduce_scatter | solution.py:267
  (112 other events, 3970.8 us)
Sparse Core Ops, SparseCore 0:
  10.9 158.6 all-gather.8
  186.3 123.2 all-gather.12
  312.2 123.5 all-gather.10
  438.4 75.6 all-gather.14
  516.8 52.2 all-gather.18
  571.9 193.7 all-gather.16
  768.5 192.9 all-gather.20
  993.6 137.9 reduce-scatter.14
  1134.5 269.5 reduce-scatter.8
  1936.3 446.1 reduce-scatter.6
  2385.5 701.5 reduce-scatter.12
  3090.0 710.2 reduce-scatter.10
where the time goes:
time: 3820 us; the launch traced here: 3810 us
  waiting for transfers between devices  3010 us (79%)
  matrix products  336 us (9%)
  local copies, waits for them, and re-layouts  210 us (5%)
  blocking collectives  142 us (4%)
  other arithmetic  56 us (1%)
    reduce_scatter x1, waiting for transfers between devices, per_device(): lax.psum_scatter(grad_wup, ('seq', 'batch'), scatter_dimension=0, tiled=T...  713 us
    reduce_scatter x1, waiting for transfers between devices, per_device(): lax.psum_scatter(grad_down, ('seq', 'batch'), scatter_dimension=0, tiled=...  705 us
    ppermute x30, waiting for transfers between devices, from_behind(): return lax.ppermute(block, axis, route)  669 us
    reduce_scatter x1, waiting for transfers between devices, per_device(): lax.psum_scatter(grad_wqkv, ('seq', 'batch'), scatter_dimension=0, tiled=...  270 us
    all_gather x1, waiting for transfers between devices, per_device(): lax.all_gather(expand_matrix, ('seq', 'batch'), axis=0, tiled=True)  194 us
    all_gather x1, waiting for transfers between devices, per_device(): lax.all_gather(shrink_matrix, ('seq', 'batch'), axis=0, tiled=True)  176 us
    all_gather x1, waiting for transfers between devices, per_device(): piece_keys = lax.all_gather(key_rows, 'seq', axis=0, tiled=True)  116 us
    all_gather x1, waiting for transfers between devices, per_device(): lax.all_gather(triple_projector_matrix, ('seq', 'batch'), axis=0, tiled=T...  113 us
  transfers between devices with their start and end apart: 42, of which 39 were waited for; matrix products, arithmetic and copies ran while one was open for 13% of the time, Pallas kernels for 0%

commit v1 on v0

v1 whole, which is shorter than its diff:
```python
import functools
import math

import jax
import jax.numpy as jnp
from jax import lax
from jax.experimental import pallas as pl
from jax.experimental.pallas import tpu as pltpu
from jax.sharding import Mesh, PartitionSpec as P

H = 16
HD = 128
FF = 8192
RH = 256
RING = 4
SEQS = 2
GROUP_HEADS = H // RING
GROUP_WIDTH = GROUP_HEADS * HD
SCALE = 1.0 / math.sqrt(HD)
VMEM_LIMIT = 48 * 1024 * 1024

epsilon = 1e-05
theta_base = 10000.0
neg_large = -1e30
bf16 = jnp.bfloat16
f32 = jnp.float32
PLANE = ("yb", "bx", "bc")
EVERY = ("za",) + PLANE
SWAP = [(0, 1), (1, 0)]


def dot(left_mat, right_mat):
    return lax.dot_general(
        left_mat, right_mat, (((1,), (0,)), ((), ())), preferred_element_type=f32
    )


def dot_rows(left_mat, right_mat):
    return lax.dot_general(
        left_mat, right_mat, (((0,), (0,)), ((), ())), preferred_element_type=f32
    )


def dot_cols(left_mat, right_mat):
    return lax.dot_general(
        left_mat, right_mat, (((1,), (1,)), ((), ())), preferred_element_type=f32
    )


def onward(block, axis):
    size = lax.axis_size(axis)
    return lax.ppermute(block, axis, [(i, (i + 1) % size) for i in range(size)])


def add_low(left, right):
    return (left.astype(f32) + right.astype(f32)).astype(left.dtype)


def ring_gather(block, axis):
    slots = [block]
    for _ in range(1, lax.axis_size(axis)):
        slots.append(onward(slots[-1], axis))
    return slots


def ring_scatter(parts, axis):
    running = parts[1]()
    for slot in range(2, lax.axis_size(axis)):
        moved = onward(running, axis)
        running = add_low(parts[slot](), moved)
    moved = onward(running, axis)
    return parts[0]().astype(f32) + moved.astype(f32)


EARLY = [(0, 0, 0), (0, 1, 0), (1, 0, 0), (1, 0, 1)]
LATE = [(0, 0, 1), (0, 1, 1), (1, 1, 0), (1, 1, 1)]
CHUNKS = [(h, x, y, c) for c in (0, 1) for h, x, y in EARLY + LATE]


def swap(block, axis):
    return lax.ppermute(block, axis, SWAP)


def plane_gather(block):
    half = block.shape[0] // 2
    first, second = block[:half], block[half:]
    early = jnp.concatenate(
        [first, swap(first, "bx"), second, swap(second, "yb")], axis=0
    )
    late = jnp.concatenate(
        [swap(early[: 2 * half], "yb"), swap(early[2 * half :], "bx")], axis=0
    )
    return jnp.concatenate([early, late, swap(early, "bc"), swap(late, "bc")], axis=0)


def plane_scatter(chunks):
    both = add_low(chunks[:8], swap(chunks[8:], "bc"))
    first = add_low(both[0:2], swap(both[4:6], "yb"))
    second = add_low(both[2:4], swap(both[6:8], "bx"))
    first_sum = first[0].astype(f32) + swap(first[1], "bx").astype(f32)
    second_sum = second[0].astype(f32) + swap(second[1], "yb").astype(f32)
    return jnp.stack([first_sum, second_sum])


def rope_kernel(joint_ref, cos_ref, sin_ref, query_ref, key_ref, value_ref):
    cosine, sine = cos_ref[0], sin_ref[0]
    for head in range(GROUP_HEADS):
        for part, out_ref in ((0, query_ref), (1, key_ref)):
            at = part * GROUP_WIDTH + head * HD
            raw = joint_ref[0, 0, :, at : at + HD]
            turned = raw * cosine + pltpu.roll(raw, HD // 2, 1) * sine
            out_ref[0, 0, :, head * HD : (head + 1) * HD] = turned.astype(bf16)
    value_ref[0, 0] = joint_ref[0, 0, :, 2 * GROUP_WIDTH :].astype(bf16)


def rope(joint, cosine, sine):
    slots, seqs, block_len, width = joint.shape
    rows = lambda w: pl.BlockSpec((1, 1, block_len, w), lambda s, b: (s, b, 0, 0))
    table = pl.BlockSpec((1, block_len, HD), lambda s, b: (s, 0, 0))
    out = jax.ShapeDtypeStruct((slots, seqs, block_len, GROUP_WIDTH), bf16)
    return pl.pallas_call(
        rope_kernel,
        grid=(slots, seqs),
        in_specs=[rows(width), table, table],
        out_specs=[rows(GROUP_WIDTH)] * 3,
        out_shape=[out] * 3,
        compiler_params=pltpu.CompilerParams(vmem_limit_bytes=VMEM_LIMIT),
        name="rope",
    )(joint, cosine, sine)


def rope_back_kernel(*refs):
    dq_ref, dk_ref, dv_ref, mk_ref, mv_ref, cos_ref, sin_ref, out_ref = refs
    cosine, sine = cos_ref[0], sin_ref[0]
    for head in range(GROUP_HEADS):
        at = slice(head * HD, (head + 1) * HD)
        grad_query = dq_ref[0, 0, :, at]
        grad_key = dk_ref[0, 0, :, at].astype(f32) + mk_ref[0, 0, :, at].astype(f32)
        for part, grad in ((0, grad_query), (1, grad_key)):
            turned = grad * cosine - pltpu.roll(grad, HD // 2, 1) * sine
            start = part * GROUP_WIDTH + head * HD
            out_ref[0, 0, :, start : start + HD] = turned.astype(bf16)
    out_ref[0, 0, :, 2 * GROUP_WIDTH :] = (
        dv_ref[0, 0].astype(f32) + mv_ref[0, 0].astype(f32)
    ).astype(bf16)


def rope_back(grads, cosine, sine):
    slots, seqs, block_len, _ = grads[0].shape
    rows = lambda w: pl.BlockSpec((1, 1, block_len, w), lambda s, b: (s, b, 0, 0))
    table = pl.BlockSpec((1, block_len, HD), lambda s, b: (s, 0, 0))
    return pl.pallas_call(
        rope_back_kernel,
        grid=(slots, seqs),
        in_specs=[rows(GROUP_WIDTH)] * 5 + [table, table],
        out_specs=rows(3 * GROUP_WIDTH),
        out_shape=jax.ShapeDtypeStruct(
            (slots, seqs, block_len, 3 * GROUP_WIDTH), bf16
        ),
        compiler_params=pltpu.CompilerParams(vmem_limit_bytes=VMEM_LIMIT),
        name="rope_back",
    )(*grads, cosine, sine)


def flat(ref):
    slots, _, block_len, width = ref.shape
    return ref[:, 0].reshape(slots * block_len, width)


def attend_kernel(pieces, *refs):
    active_ref, query_ref = refs[:2]
    key_refs, value_refs = refs[2 : 2 + pieces], refs[2 + pieces : 2 + 2 * pieces]
    qplace_ref, kplace_ref, out_ref, low_ref, log_ref = refs[2 + 2 * pieces :]
    queries = flat(query_ref)
    query_places = qplace_ref[...]
    masked = []
    for piece, key_ref in enumerate(key_refs):
        scores = dot_cols(queries, flat(key_ref)) * SCALE
        allowed = kplace_ref[piece] <= query_places
        masked.append(jnp.where(allowed, scores, neg_large))
    top = functools.reduce(
        jnp.maximum, [jnp.max(m, axis=1, keepdims=True) for m in masked]
    )
    total, gathered = 0.0, 0.0
    for scores, value_ref in zip(masked, value_refs):
        weights = jnp.exp(scores - top)
        total = total + jnp.sum(weights, axis=1, keepdims=True)
        gathered = gathered + dot(weights.astype(bf16), flat(value_ref))
    result = gathered / total
    out_ref[:, 0] = result.reshape(out_ref.shape[0], out_ref.shape[2], HD)
    kept = active_ref[pl.program_id(0)]
    low_ref[:, 0] = (
        (result * kept).astype(bf16).reshape(out_ref.shape[0], out_ref.shape[2], HD)
    )
    log_ref[0, 0] = top + jnp.log(total)


def attend(active, queries, keys, values, query_places, key_places):
    slots, seqs, block_len, width = queries.shape
    rows = slots * block_len
    heads = width // HD
    pieces = len(keys)
    tile = pl.BlockSpec((slots, 1, block_len, HD), lambda s, h: (0, s, 0, h))
    return pl.pallas_call(
        functools.partial(attend_kernel, pieces),
        grid=(seqs, heads),
        in_specs=[pl.BlockSpec(memory_space=pltpu.SMEM)]
        + [tile] * (1 + 2 * pieces)
        + [
            pl.BlockSpec((rows, 1), lambda s, h: (0, 0)),
            pl.BlockSpec((pieces, 1, rows), lambda s, h: (0, 0, 0)),
        ],
        out_specs=[
            tile,
            tile,
            pl.BlockSpec((1, 1, rows, 1), lambda s, h: (s, h, 0, 0)),
        ],
        out_shape=[
            jax.ShapeDtypeStruct(queries.shape, f32),
            jax.ShapeDtypeStruct(queries.shape, bf16),
            jax.ShapeDtypeStruct((seqs, heads, rows, 1), f32),
        ],
        compiler_params=pltpu.CompilerParams(vmem_limit_bytes=VMEM_LIMIT),
        name="attend",
    )(active, queries, *keys, *values, query_places, key_places)


def attend_back_kernel(pieces, *refs):
    query_ref = refs[0]
    key_refs, value_refs = refs[1 : 1 + pieces], refs[1 + pieces : 1 + 2 * pieces]
    rest = refs[1 + 2 * pieces :]
    grad_ref, out_ref, log_ref, qplace_ref, kplace_ref, dq_ref = rest[:6]
    dk_refs, dv_refs = rest[6 : 6 + pieces], rest[6 + pieces :]
    queries, grads = flat(query_ref), flat(grad_ref)
    query_places = qplace_ref[...]
    dots = jnp.sum(grads.astype(f32) * flat(out_ref), axis=1, keepdims=True)
    log_norm = log_ref[0, 0]
    grad_query = 0.0
    shape = (query_ref.shape[0], query_ref.shape[2], HD)
    for piece in range(pieces):
        keys, values = flat(key_refs[piece]), flat(value_refs[piece])
        scores = dot_cols(queries, keys) * SCALE
        allowed = kplace_ref[piece] <= query_places
        probs = jnp.exp(jnp.where(allowed, scores - log_norm, neg_large))
        grad_probs = dot_cols(grads, values)
        dv_refs[piece][:, 0] = (
            dot_rows(probs.astype(bf16), grads)
            .astype(dv_refs[piece].dtype)
            .reshape(shape)
        )
        grad_scores = (probs * (grad_probs - dots)).astype(bf16)
        dk_refs[piece][:, 0] = (
            (dot_rows(grad_scores, queries) * SCALE)
            .astype(dk_refs[piece].dtype)
            .reshape(shape)
        )
        grad_query = grad_query + dot(grad_scores, keys)
    dq_ref[:, 0] = (grad_query * SCALE).reshape(shape)


def attend_back(queries, keys, values, grads, out, logs, query_places, key_places):
    slots, seqs, block_len, width = queries.shape
    rows = slots * block_len
    heads = width // HD
    pieces = len(keys)
    tile = pl.BlockSpec((slots, 1, block_len, HD), lambda s, h: (0, s, 0, h))
    wide = jax.ShapeDtypeStruct(queries.shape, f32)
    low = jax.ShapeDtypeStruct(queries.shape, bf16)
    found = pl.pallas_call(
        functools.partial(attend_back_kernel, pieces),
        grid=(seqs, heads),
        in_specs=[tile] * (3 + 2 * pieces)
        + [
            pl.BlockSpec((1, 1, rows, 1), lambda s, h: (s, h, 0, 0)),
            pl.BlockSpec((rows, 1), lambda s, h: (0, 0)),
            pl.BlockSpec((pieces, 1, rows), lambda s, h: (0, 0, 0)),
        ],
        out_specs=[tile] * (1 + 2 * pieces),
        out_shape=[wide] + ([wide] + [low] * (pieces - 1)) * 2,
        compiler_params=pltpu.CompilerParams(vmem_limit_bytes=VMEM_LIMIT),
        name="attend_back",
    )(queries, *keys, *values, grads, out, logs, query_places, key_places)
    return found[0], found[1 : 1 + pieces], found[1 + pieces :]


def per_device(
    layer_entries,
    incoming_adjoint,
    mixing_rescale_scalers,
    triple_projector_matrix,
    context_exit_matrix,
    dense_center_scaler,
    dense_center_offset,
    expand_matrix,
    shrink_matrix,
    span_chooser_initial,
    span_chooser_final,
    heat_divisor,
    sample_channel_fourths,
    element_preset_span,
    spot_group_table,
):
    block_len, seqs, width = layer_entries.shape
    tokens = block_len * seqs
    ring, plane = lax.axis_size("za"), lax.axis_size("yb")
    cores = lax.axis_size("bc")
    group = plane * lax.axis_size("bx") * cores
    devices = ring * group
    paired = plane == 2 and lax.axis_size("bx") == 2 and cores == 2
    za, yb = lax.axis_index("za"), lax.axis_index("yb")
    bx, bc = lax.axis_index("bx"), lax.axis_index("bc")
    rows = width // devices
    hidden_rows = FF // devices
    out_rows = span_chooser_final.shape[0] * 4

    def home(array):
        return jnp.transpose(array, (1, 0, 2)).reshape(tokens, width)

    def back(array):
        return jnp.transpose(array.reshape(seqs, block_len, width), (1, 0, 2))

    entries, adjoint = home(layer_entries), home(incoming_adjoint)

    vector = jnp.concatenate(
        [
            mixing_rescale_scalers,
            dense_center_scaler,
            dense_center_offset,
            span_chooser_final.reshape(-1),
            jnp.zeros((RH - 3 * rows - out_rows,), bf16),
        ]
    )
    forced_home = jnp.transpose(element_preset_span, (1, 0)).reshape(tokens)
    pad_rows = -(rows + 2) % 16
    pack_rows = rows + 2 + pad_rows
    pack = jnp.concatenate(
        [
            span_chooser_initial,
            vector[None],
            forced_home.astype(bf16).reshape(1, RH),
            jnp.zeros((pad_rows, RH), bf16),
        ],
        axis=0,
    )
    packs = lax.all_gather(pack, EVERY, axis=0, tiled=False)
    route_in = packs[:, :rows].reshape(width, RH)
    vectors = packs[:, rows]
    gain_one = vectors[:, :rows].reshape(1, width).astype(f32)
    gain_two = vectors[:, rows : 2 * rows].reshape(1, width).astype(f32)
    bias_two = vectors[:, 2 * rows : 3 * rows].reshape(1, width).astype(f32)
    route_out = vectors[:, 3 * rows : 3 * rows + out_rows].reshape(RH, 4)
    forced_all = packs[:, rows + 1]

    qkv_cut = jnp.transpose(
        triple_projector_matrix.reshape(rows, 3, ring, GROUP_WIDTH), (2, 0, 1, 3)
    ).reshape(ring, rows, 3 * GROUP_WIDTH)
    qkv_cut = lax.all_to_all(qkv_cut, "za", 0, 0, tiled=True)
    qkv_own = lax.all_gather(qkv_cut, PLANE, axis=1, tiled=False).reshape(
        width, 3 * GROUP_WIDTH
    )
    out_own = lax.all_gather(context_exit_matrix, PLANE, axis=0, tiled=True)
    up_cut = jnp.transpose(
        expand_matrix.reshape(rows, ring, group, hidden_rows), (2, 0, 1, 3)
    ).reshape(group, rows, ring * hidden_rows)
    up_cut = lax.all_to_all(up_cut, PLANE, 0, 0, tiled=True)
    up_own = lax.all_gather(
        up_cut.reshape(group * rows, ring * hidden_rows), "za", axis=0, tiled=True
    )
    down_own = lax.all_gather(shrink_matrix, "za", axis=0, tiled=True)

    slot_ids = jnp.arange(ring, dtype=jnp.int32)
    table_ids = jnp.arange(spot_group_table.shape[0], dtype=jnp.int32)

    def places_of(piece):
        index = ((za - slot_ids) % ring) * plane + (yb - piece) % plane
        spots = jnp.sum(
            jnp.where(index[:, None] == table_ids[None, :], spot_group_table, 0), axis=1
        )
        return spots[:, None] * block_len + jnp.arange(block_len, dtype=jnp.int32)

    all_places = [places_of(piece) for piece in range(plane)]
    query_places = all_places[0].reshape(ring * block_len, 1)
    key_places = jnp.stack(all_places).reshape(plane, 1, ring * block_len)
    half = HD // 2
    inverse = theta_base ** (-(jnp.arange(half, dtype=f32) * (2.0 / HD)))
    angles = all_places[0].astype(f32)[:, :, None] * inverse
    cosine = jnp.concatenate([jnp.cos(angles), jnp.cos(angles)], axis=-1)
    sine = jnp.concatenate([-jnp.sin(angles), jnp.sin(angles)], axis=-1)
    active = (za < sample_channel_fourths).astype(f32)
    active_rows = jnp.broadcast_to(
        active[None, :, None, None], (ring, seqs, block_len, 1)
    ).reshape(ring * tokens, 1)

    entry_slots = jnp.concatenate(ring_gather(entries, "za"), axis=0).astype(f32)
    inv_rms = lax.rsqrt(
        jnp.mean(entry_slots * entry_slots, axis=1, keepdims=True) + epsilon
    )
    scaled_slots = entry_slots * inv_rms
    normed = (scaled_slots * gain_one).astype(bf16)
    joint = dot(normed, qkv_own).reshape(ring, seqs, block_len, 3 * GROUP_WIDTH)
    queries, keys, values = rope(joint, cosine, sine)
    all_keys = ring_gather(keys, "yb")
    all_values = ring_gather(values, "yb")
    heads_out, attended, logs = attend(
        active, queries, all_keys, all_values, query_places, key_places
    )
    attended = attended.reshape(ring * tokens, GROUP_WIDTH)
    inputs = entries.astype(f32)
    hidden = inputs + ring_scatter(
        [
            lambda s=s: dot(attended[s * tokens : (s + 1) * tokens], out_own).astype(
                bf16
            )
            for s in range(ring)
        ],
        "za",
    )

    centre = jnp.mean(hidden, axis=1, keepdims=True)
    centered = hidden - centre
    variance = jnp.mean(centered * centered, axis=1, keepdims=True)
    inv_std = lax.rsqrt(variance + epsilon)
    normal = centered * inv_std
    ffn_in = (normal * gain_two + bias_two).astype(bf16)

    if paired:
        spread, gather_back = (
            plane_gather,
            lambda terms: plane_scatter(
                terms.reshape((16, block_len) + terms.shape[1:])
            ).reshape((tokens,) + terms.shape[1:]),
        )
        at = jnp.stack(
            [
                (
                    (za * group + ((yb ^ y) * 2 + (bx ^ x)) * 2 + (bc ^ c)) * seqs + h
                ).astype(jnp.int32)
                for h, x, y, c in CHUNKS
            ]
        )
    else:
        spread = lambda block: lax.all_gather(block, PLANE, axis=0, tiled=True)
        gather_back = lambda terms: lax.psum_scatter(
            terms, PLANE, scatter_dimension=0, tiled=True
        ).astype(f32)
        at = za * group * seqs + jnp.arange(group * seqs, dtype=jnp.int32)
    wide_in, wide_adjoint = spread(ffn_in), spread(adjoint)
    wide_tokens = wide_in.shape[0]
    picks = (at[:, None] == jnp.arange(devices * seqs)[None, :]).astype(bf16)
    wide_forced = dot(picks, forced_all.reshape(devices * seqs, block_len)).reshape(
        wide_tokens
    )

    temperature = heat_divisor[0]

    def router(block, forced):
        squashed = jnp.tanh(dot(block, route_in))
        logits = dot(squashed.astype(bf16), route_out)
        routed = jax.nn.softmax(logits / temperature, axis=1)
        is_forced = (forced > 0)[:, None]
        chosen = forced[:, None] - 1 == jnp.arange(4, dtype=forced.dtype)[None, :]
        mix = jnp.where(is_forced, chosen.astype(f32), routed)
        scale = jnp.stack(
            [
                mix[:, 0] + mix[:, 1] + mix[:, 2] + mix[:, 3],
                mix[:, 1] + mix[:, 2] + mix[:, 3],
                mix[:, 2] + mix[:, 3],
                mix[:, 3],
            ],
            axis=1,
        )
        return squashed, routed, is_forced, scale

    band_scale = router(wide_in, wide_forced)[3]
    scale_wide = jnp.broadcast_to(
        band_scale[:, :, None], (wide_tokens, 4, hidden_rows)
    ).reshape(wide_tokens, 4 * hidden_rows)

    rectified = jnp.maximum(dot(wide_in, up_own), 0.0)
    activated = rectified * rectified
    gated = (activated * scale_wide).astype(bf16)
    grad_gated = dot_cols(wide_adjoint, down_own)
    grad_up = (grad_gated * scale_wide * (2.0 * rectified)).astype(bf16)
    grad_band = jnp.sum(
        (grad_gated * activated).reshape(wide_tokens, 4, hidden_rows), axis=2
    )
    grad_in_terms = dot_cols(grad_up, up_own).astype(bf16)
    grad_ffn_in = gather_back(grad_in_terms)
    grad_band_home = gather_back(grad_band)
    output = hidden + gather_back(dot(gated, down_own).astype(bf16))
    result = back(output.astype(bf16))
    down_terms = dot_rows(gated, wide_adjoint).astype(bf16)
    up_terms = dot_rows(wide_in, grad_up).astype(bf16)
    grad_down = lax.psum_scatter(
        down_terms, "za", scatter_dimension=0, tiled=True
    ).astype(f32)
    up_terms = lax.psum_scatter(up_terms, "za", scatter_dimension=0, tiled=True)
    up_terms = lax.all_to_all(
        up_terms.reshape(group, rows, ring * hidden_rows), PLANE, 0, 0, tiled=True
    )
    grad_wup = (
        jnp.transpose(up_terms.reshape(group, rows, ring, hidden_rows), (1, 2, 0, 3))
        .reshape(rows, FF)
        .astype(f32)
    )

    squashed, routed, is_forced, _ = router(ffn_in, forced_home)
    grad_mix = jnp.cumsum(grad_band_home, axis=1)
    grad_logits = jnp.where(
        is_forced,
        0.0,
        routed
        * (grad_mix - jnp.sum(routed * grad_mix, axis=1, keepdims=True))
        / temperature,
    ).astype(bf16)
    grad_route_out = dot_rows(squashed.astype(bf16), grad_logits)
    grad_pre = (dot_cols(grad_logits, route_out) * (1.0 - squashed * squashed)).astype(
        bf16
    )
    grad_route_in = dot_rows(ffn_in, grad_pre)
    grad_ffn_in = grad_ffn_in + dot_cols(grad_pre, route_in)
    grad_gain_two = jnp.sum(grad_ffn_in * normal, axis=0)
    grad_bias_two = jnp.sum(grad_ffn_in, axis=0)
    grad_normal = grad_ffn_in * gain_two
    grad_hidden = adjoint.astype(f32) + inv_std * (
        grad_normal
        - jnp.mean(grad_normal, axis=1, keepdims=True)
        - normal * jnp.mean(grad_normal * normal, axis=1, keepdims=True)
    )
    small = jnp.concatenate(
        [
            grad_gain_two.reshape(devices, rows),
            grad_bias_two.reshape(devices, rows),
            grad_route_out.reshape(devices, out_rows),
            jnp.zeros((devices, RH - 2 * rows - out_rows), f32),
        ],
        axis=1,
    )
    small_rows = rows + 1 + (-(rows + 1) % 8)
    small_pack = jnp.concatenate(
        [
            grad_route_in.reshape(devices, rows, RH),
            small[:, None],
            jnp.zeros((devices, small_rows - rows - 1, RH), f32),
        ],
        axis=1,
    )
    small_sum = lax.psum_scatter(
        small_pack.reshape(devices * small_rows, RH),
        EVERY,
        scatter_dimension=0,
        tiled=True,
    )

    grad_attn = jnp.concatenate(ring_gather(grad_hidden.astype(bf16), "za"), axis=0)
    grad_heads = (
        (dot_cols(grad_attn, out_own) * active_rows)
        .astype(bf16)
        .reshape(ring, seqs, block_len, GROUP_WIDTH)
    )
    grad_query, grad_keys, grad_values = attend_back(
        queries,
        all_keys,
        all_values,
        grad_heads,
        heads_out,
        logs,
        query_places,
        key_places,
    )

    def from_others(grads):
        if plane == 1:
            return jnp.zeros_like(grads[0])
        running = grads[1]
        for slot in range(2, plane):
            running = add_low(grads[slot], onward(running, "yb"))
        return onward(running, "yb")

    grad_joint = rope_back(
        (
            grad_query,
            grad_keys[0],
            grad_values[0],
            from_others(grad_keys),
            from_others(grad_values),
        ),
        cosine,
        sine,
    ).reshape(ring * tokens, 3 * GROUP_WIDTH)
    grad_out_terms = dot_rows(attended, grad_attn).astype(bf16)
    grad_wout = lax.psum_scatter(
        grad_out_terms, PLANE, scatter_dimension=0, tiled=True
    ).astype(f32)
    normed_terms = dot_cols(grad_joint, qkv_own)
    grad_gain_terms = jnp.sum(normed_terms * scaled_slots, axis=0)
    gain_high = grad_gain_terms.astype(bf16)
    gain_low = (grad_gain_terms - gain_high.astype(f32)).astype(bf16)
    qkv_terms = jnp.concatenate(
        [
            dot_rows(normed, grad_joint).astype(bf16),
            gain_high[:, None],
            gain_low[:, None],
            jnp.zeros((width, HD - 2), bf16),
        ],
        axis=1,
    )
    wide_cols = 3 * GROUP_WIDTH + HD
    qkv_terms = lax.psum_scatter(
        qkv_terms.reshape(ring, group, rows, wide_cols),
        PLANE,
        scatter_dimension=1,
        tiled=False,
    )
    qkv_terms = lax.all_to_all(qkv_terms, "za", 0, 0, tiled=True).astype(f32)
    grad_wqkv = jnp.transpose(
        qkv_terms[:, :, : 3 * GROUP_WIDTH].reshape(ring, rows, 3, GROUP_WIDTH),
        (1, 2, 0, 3),
    ).reshape(rows, 3 * width)
    grad_gain_one = jnp.sum(
        qkv_terms[:, :, 3 * GROUP_WIDTH] + qkv_terms[:, :, 3 * GROUP_WIDTH + 1], axis=0
    )
    low_terms = normed_terms.astype(bf16)
    grad_normed = ring_scatter(
        [lambda s=s: low_terms[s * tokens : (s + 1) * tokens] for s in range(ring)],
        "za",
    )
    inv_home = lax.rsqrt(jnp.mean(inputs * inputs, axis=1, keepdims=True) + epsilon)
    scaled = inputs * inv_home
    grad_scaled = grad_normed * gain_one
    grad_inputs = grad_hidden + inv_home * (
        grad_scaled - scaled * jnp.mean(grad_scaled * scaled, axis=1, keepdims=True)
    )
    grad_tokens = back(grad_inputs.astype(bf16))
    return (
        result,
        grad_tokens,
        grad_gain_one,
        grad_wqkv,
        grad_wout,
        small_sum[rows, :rows],
        small_sum[rows, rows : 2 * rows],
        grad_wup,
        grad_down,
        small_sum[:rows],
        small_sum[rows, 2 * rows : 2 * rows + out_rows].reshape(out_rows // 4, 4),
    )


def solution(mesh):
    seq, batch = mesh.shape["seq"], mesh.shape["batch"]
    inner = Mesh(
        mesh.devices.reshape(RING, seq // RING, batch // 2, 2),
        ("za", "yb", "bx", "bc"),
    )
    along, across = ("za", "yb"), ("bx", "bc")
    tokens = P(along, across, None)
    vector = P(along + across)
    matrix = P(along + across, None)
    return jax.shard_map(
        per_device,
        mesh=inner,
        in_specs=(
            tokens,
            tokens,
            vector,
            matrix,
            matrix,
            vector,
            vector,
            matrix,
            matrix,
            matrix,
            matrix,
            P(),
            P(across),
            P(along, across),
            P(),
        ),
        out_specs=(
            tokens,
            tokens,
            vector,
            matrix,
            matrix,
            vector,
            vector,
            matrix,
            matrix,
            matrix,
            matrix,
        ),
        check_vma=False,
    )
```

time: 3820 us -> 1020 us (0.27)
  waiting for transfers between devices: 3010 us -> 529 us
  matrix products: 336 us -> 144 us
  blocking collectives: 142 us -> 27.2 us
  local copies, waits for them, and re-layouts: 210 us -> 107 us
  Pallas kernels: 0 us -> 50 us
  starting transfers between devices: 23.1 us -> 65.5 us
    reduce_scatter x5, waiting for transfers between devices: 1690 us -> 59.4 us  [the longest x1 31.1 us: per_device(): lax.psum_scatter(grad_out_terms, PLANE, scatter_dimension=0, tiled=True)]
    all_gather x7 -> x5, waiting for transfers between devices: 654 us -> 0.07 us  [the longest x1 0.02 us: per_device(): lax.all_gather(qkv_cut, PLANE, axis=1, tiled=False)]
    ppermute x30 -> x43, waiting for transfers between devices: 669 us -> 469 us  [the longest x16 398 us: onward(): return lax.ppermute(block, axis, [(i, (i + 1) % size) for i in range(size)])]
    dot_general x76 -> x23, matrix products: 336 us -> 144 us  [the longest x11 56 us: dot(): lax.dot_general(left_mat, right_mat, (((1,), (0,)), ((), ())), preferred_...]
    unnamed x2 -> x0, blocking collectives: 103 us -> none
    unnamed x175 -> x174, local copies, waits for them, and re-layouts: 92.7 us -> 33 us
    while x84 -> x0, local copies, waits for them, and re-layouts: 55.8 us -> none
    pallas_call x0 -> x4, Pallas kernels: none -> 50 us  [the longest x1 20.3 us: attend_back(): pl.pallas_call(functools.partial(attend_back_kernel, pieces), grid=(seqs,...]
  transfers between devices with their start and end apart: 42 -> 56, of which waited for: 39 -> 29; matrix products, arithmetic and copies ran while one was open for 13% -> 26% of each run, Pallas kernels for 0% -> 5%
where the time goes in v1:
time: 1020 us; the launch traced here: 1010 us
  waiting for transfers between devices  529 us (52%)
  matrix products  144 us (14%)
  local copies, waits for them, and re-layouts  107 us (10%)
  other arithmetic  73.1 us (7%)
  starting transfers between devices  65.5 us (6%)
  Pallas kernels  50 us (5%)
  blocking collectives  27.2 us (3%)
  between operations  16.5 us (2%)
    ppermute x16, waiting for transfers between devices, onward(): return lax.ppermute(block, axis, [(i, (i + 1) % size) for i in range(size)])  398 us
    ppermute x27, waiting for transfers between devices, swap(): return lax.ppermute(block, axis, SWAP)  71 us
    dot_general x11, matrix products, dot(): lax.dot_general(left_mat, right_mat, (((1,), (0,)), ((), ())), preferred_...  56 us
    dot_general x6, matrix products, dot_cols(): lax.dot_general(left_mat, right_mat, (((1,), (1,)), ((), ())), preferred_...  47.4 us
    dot_general x6, matrix products, dot_rows(): lax.dot_general(left_mat, right_mat, (((0,), (0,)), ((), ())), preferred_...  40.5 us
    unnamed x174, local copies, waits for them, and re-layouts  33 us
    reduce_scatter x1, waiting for transfers between devices, per_device(): lax.psum_scatter(grad_out_terms, PLANE, scatter_dimension=0, tiled=True)  31.1 us
    ppermute x16, starting transfers between devices, onward(): return lax.ppermute(block, axis, [(i, (i + 1) % size) for i in range(size)])  28.9 us
  transfers between devices with their start and end apart: 56, of which 29 were waited for; matrix products, arithmetic and copies ran while one was open for 26% of the time, Pallas kernels for 5%

profile of v1, /device:TPU:0, one launch (start us, length us, event | category | flops | bytes accessed | tf_op | source)
XLA Modules:
  0.0 1012.5 jit_solution(3073613742802093444)
XLA Ops:
  16.4 27.2 %all_to_all.20 = bf16[4,64,1536]{2,1,0:T(8,128)(2,1)} all-to-all(bf16[4,64,1536]{2,1,0:T(8,128)(2,1)S(1)} %reshape.501), channel_id=1, replica_groups=mesh['za'=4,'yb'=2,'bx'=2,'bc'=2] {'za'}, dimensions={0} | all-to-all | bytes 1572864 | tf_op jit(solution)/shard_map/all_to_all | solution.py:357
  52.9 22.4 %collective-permute-done = bf16[256,2048]{1,0:T(8,128)(2,1)S(1)} collective-permute-done((bf16[256,2048]{1,0:T(8,128)(2,1)S(1)}, bf16[256,2048]{1,0:T(8,128)(2,1)S(1)}, u32[]{:S(2)}, u32[]{:S(2)}) %collective-permute-start) | collective-permute-done | bytes 1048608 | tf_op jit(solution)/shard_map/ppermute | solution.py:52
  75.6 24.3 %collective-permute-done.1 = bf16[256,2048]{1,0:T(8,128)(2,1)S(1)} collective-permute-done((bf16[256,2048]{1,0:T(8,128)(2,1)S(1)}, bf16[256,2048]{1,0:T(8,128)(2,1)S(1)}, u32[]{:S(2)}, u32[]{:S(2)}) %collective-permute-start.1) | collective-permute-done | bytes 1048608 | tf_op jit(solution)/shard_map/ppermute | solution.py:52
  103.5 20.3 %collective-permute-done.2 = bf16[256,2048]{1,0:T(8,128)(2,1)} collective-permute-done((bf16[256,2048]{1,0:T(8,128)(2,1)S(1)}, bf16[256,2048]{1,0:T(8,128)(2,1)}, u32[]{:S(2)}, u32[]{:S(2)}) %collective-permute-start.2) | collective-permute-done | bytes 1048608 | tf_op jit(solution)/shard_map/ppermute | solution.py:52
  134.2 11.8 %fusion.65.joint_ref = f32[4,2,128,1536]{3,2,1,0:T(8,128)} fusion(bf16[4,2,128,2048]{3,2,1,0:T(8,128)(2,1)} %bitcast.263, bf16[2048,1536,1,1]{1,0,3,2:T(8,128)(2,1)} %bitcast.298), kind=kOutput, calls=%fused_computation.220 | convolution fusion | flops 6442450944 | bytes 16777216 | tf_op jit(solution)/shard_map/dot_general | solution.py:33
  154.9 23.8 %collective-permute-done.3.refs_3_.refs_2_ = bf16[4,2,128,512]{3,2,1,0:T(8,128)(2,1)} collective-permute-done((bf16[4,2,128,512]{3,2,1,0:T(8,128)(2,1)S(1)}, bf16[4,2,128,512]{3,2,1,0:T(8,128)(2,1)}, u32[]{:S(2)}, u32[]{:S(2)}) %collective-permute-start.3) | collective-permute-done | bytes 1048608 | tf_op jit(solution)/shard_map/ppermute | solution.py:52
  178.7 18.5 %collective-permute-done.4.refs_5_.refs_4_ = bf16[4,2,128,512]{3,2,1,0:T(8,128)(2,1)} collective-permute-done((bf16[4,2,128,512]{3,2,1,0:T(8,128)(2,1)S(1)}, bf16[4,2,128,512]{3,2,1,0:T(8,128)(2,1)}, u32[]{:S(2)}, u32[]{:S(2)}) %collective-permute-start.4) | collective-permute-done | bytes 1048608 | tf_op jit(solution)/shard_map/ppermute | solution.py:52
  197.2 15.0 %attend.1 = (f32[4,2,128,512]{3,2,1,0:T(8,128)}, bf16[4,2,128,512]{3,2,1,0:T(8,128)(2,1)S(1)}, f32[2,4,512,1]{3,2,1,0:T(8,128)}) custom-call(f32[2]{0:T(128)S(1)} %compare_convert_fusion.refs_0_, bf16[4,2,128,512]{3,2,1,0:T(8,128)(2,1)S(1)} %get-tuple-element.22.refs_1_.refs_0_, bf16[4,2,128,512]{3,2,1,0:T(8,128)(2,1)S(1)} %get-tuple-element.23.refs_2_.refs_1_, ...), custom_call_target="tpu_custom_call" | custom-call | tf_op jit(solution)/shard_map/attend/pallas_call | solution.py:204
  224.6 38.4 %collective-permute-done.5 = bf16[256,2048]{1,0:T(8,128)(2,1)} collective-permute-done((bf16[256,2048]{1,0:T(8,128)(2,1)}, bf16[256,2048]{1,0:T(8,128)(2,1)}, u32[]{:S(2)}, u32[]{:S(2)}) %collective-permute-start.5) | collective-permute-done | bytes 1048608 | tf_op jit(solution)/shard_map/ppermute | solution.py:52
  278.7 36.4 %collective-permute-done.6 = bf16[256,2048]{1,0:T(8,128)(2,1)} collective-permute-done((bf16[256,2048]{1,0:T(8,128)(2,1)}, bf16[256,2048]{1,0:T(8,128)(2,1)}, u32[]{:S(2)}, u32[]{:S(2)}) %collective-permute-start.6) | collective-permute-done | bytes 1048608 | tf_op jit(solution)/shard_map/ppermute | solution.py:52
  318.0 10.6 %collective-permute-start.7 = (bf16[256,2048]{1,0:T(8,128)(2,1)}, bf16[256,2048]{1,0:T(8,128)(2,1)}, u32[]{:S(2)}, u32[]{:S(2)}) collective-permute-start(bf16[256,2048]{1,0:T(8,128)(2,1)} %fusion.14), channel_id=1, source_target_pairs={{0,8},{8,16},{16,24},{24,0},{1,9},{9,17},{17,25},{25,1},{2,10},{10... | collective-permute-start | bytes 3145736 | tf_op jit(solution)/shard_map/ppermute | solution.py:52
  335.1 43.8 %collective-permute-done.7 = bf16[256,2048]{1,0:T(8,128)(2,1)} collective-permute-done((bf16[256,2048]{1,0:T(8,128)(2,1)}, bf16[256,2048]{1,0:T(8,128)(2,1)}, u32[]{:S(2)}, u32[]{:S(2)}) %collective-permute-start.7) | collective-permute-done | bytes 1048608 | tf_op jit(solution)/shard_map/ppermute | solution.py:52
  433.1 14.9 %fusion.66 = f32[2048,1024]{0,1:T(8,128)} fusion(bf16[2048,2048]{1,0:T(8,128)(2,1)} %copy-done.51, bf16[2048,1024]{1,0:T(8,128)(2,1)} %all-gather.10.cloned.1.call-done), kind=kOutput, calls=%fused_computation.221 | convolution fusion | flops 8589934592 | bytes 20971520 | tf_op jit(solution)/shard_map/dot_general | solution.py:33
  448.1 17.6 %fusion.7 = (bf16[2048,1024]{0,1:T(8,128)(2,1)S(1)}, bf16[2048,1024]{0,1:T(8,128)(2,1)}, f32[2048,1024]{0,1:T(8,128)}) fusion(f32[2048,1024]{0,1:T(8,128)} %fusion.66, f32[2048,4]{0,1:T(4,128)S(1)} %pad_maximum_fusion.16, bf16[2048,2048]{1,0:T(8,128)(2,1)} %constant_dynamic-update-slice_fusion.8, bf16[1024,2048]{1,0:T(8,128)(2,1)} %all-gather.12.cloned.1.call-done), kind=kOutput, calls=%fused_computation.11 | convolution fusion | flops 8606711808 | bytes 37781504 | tf_op jit(solution)/shard_map/dot_general | solution.py:45
  467.6 11.1 %convolution_convert_fusion.4 = bf16[2048,1024]{1,0:T(8,128)(2,1)} fusion(bf16[2048,2048]{1,0:T(8,128)(2,1)S(1)} %copy-done.52, bf16[2048,1024]{0,1:T(8,128)(2,1)S(1)} %get-tuple-element.120), kind=kOutput, calls=%fused_computation.24 | convolution fusion | flops 8592031744 | bytes 16777216 | tf_op jit(solution)/shard_map/dot_general | solution.py:39
  487.2 9.8 convolution_convert_fusion.1
  518.3 12.6 %convolution_convert_fusion.3 = bf16[1024,2048]{1,0:T(8,128)(2,1)} fusion(bf16[2048,1024]{0,1:T(8,128)(2,1)S(1)} %copy-done.41, bf16[2048,2048]{1,0:T(8,128)(2,1)} %constant_dynamic-update-slice_fusion.8), kind=kOutput, calls=%fused_computation.23 | convolution fusion | flops 8592031744 | bytes 16777216 | tf_op jit(solution)/shard_map/dot_general | solution.py:39
  554.2 17.6 %collective-permute-done.26 = bf16[2,128,2048]{2,1,0:T(8,128)(2,1)S(1)} collective-permute-done((bf16[2,128,2048]{2,1,0:T(8,128)(2,1)S(1)}, bf16[2,128,2048]{2,1,0:T(8,128)(2,1)S(1)}, u32[]{:S(2)}, u32[]{:S(2)}) %collective-permute-start.26) | collective-permute-done | bytes 1048608 | tf_op jit(solution)/shard_map/ppermute | solution.py:81
  575.9 18.4 %collective-permute-done.15 = bf16[2,128,2048]{2,1,0:T(8,128)(2,1)S(1)} collective-permute-done((bf16[2,128,2048]{2,1,0:T(8,128)(2,1)S(1)}, bf16[2,128,2048]{2,1,0:T(8,128)(2,1)S(1)}, u32[]{:S(2)}, u32[]{:S(2)}) %collective-permute-start.15) | collective-permute-done | bytes 1048608 | tf_op jit(solution)/shard_map/ppermute | solution.py:81
  617.8 46.2 %collective-permute-done.35 = bf16[256,2048]{1,0:T(8,128)(2,1)S(1)} collective-permute-done((bf16[256,2048]{1,0:T(8,128)(2,1)S(1)}, bf16[256,2048]{1,0:T(8,128)(2,1)S(1)}, u32[]{:S(2)}, u32[]{:S(2)}) %collective-permute-start.35) | collective-permute-done | bytes 1048608 | tf_op jit(solution)/shard_map/ppermute | solution.py:52
  664.0 25.9 %collective-permute-done.36 = bf16[256,2048]{1,0:T(8,128)(2,1)S(1)} collective-permute-done((bf16[256,2048]{1,0:T(8,128)(2,1)S(1)}, bf16[256,2048]{1,0:T(8,128)(2,1)S(1)}, u32[]{:S(2)}, u32[]{:S(2)}) %collective-permute-start.36) | collective-permute-done | bytes 1048608 | tf_op jit(solution)/shard_map/ppermute | solution.py:52
  690.0 11.5 %collective-permute-start.37 = (bf16[256,2048]{1,0:T(8,128)(2,1)S(1)}, bf16[256,2048]{1,0:T(8,128)(2,1)S(1)}, u32[]{:S(2)}, u32[]{:S(2)}) collective-permute-start(bf16[256,2048]{1,0:T(8,128)(2,1)S(1)} %collective-permute-done.36), channel_id=1, source_target_pairs={{0,8},{8,16},{16,24},{24,0},{1,9},{9,17},{17,25},{25,1},{2,10},{10... | collective-permute-start | bytes 3145736 | tf_op jit(solution)/shard_map/ppermute | solution.py:52
  702.7 23.8 %collective-permute-done.37 = bf16[256,2048]{1,0:T(8,128)(2,1)S(1)} collective-permute-done((bf16[256,2048]{1,0:T(8,128)(2,1)S(1)}, bf16[256,2048]{1,0:T(8,128)(2,1)S(1)}, u32[]{:S(2)}, u32[]{:S(2)}) %collective-permute-start.37) | collective-permute-done | bytes 1048608 | tf_op jit(solution)/shard_map/ppermute | solution.py:52
  732.7 20.3 %attend_back.1 = (f32[4,2,128,512]{3,2,1,0:T(8,128)}, f32[4,2,128,512]{3,2,1,0:T(8,128)}, bf16[4,2,128,512]{3,2,1,0:T(8,128)(2,1)}, f32[4,2,128,512]{3,2,1,0:T(8,128)}, bf16[4,2,128,512]{3,2,1,0:T(8,128)(2,1)}) custom-call(bf16[4,2,128,512]{3,2,1,0:T(8,128)(2,1)S(1)} %get-tuple-element.22.refs_1_.refs_0_, ...), custom_call_target="tpu_custom_call" | custom-call | tf_op jit(solution)/shard_map/attend_back/pallas_call | solution.py:269
  763.0 16.4 %collective-permute-done.38.refs_3_ = bf16[4,2,128,512]{3,2,1,0:T(8,128)(2,1)} collective-permute-done((bf16[4,2,128,512]{3,2,1,0:T(8,128)(2,1)}, bf16[4,2,128,512]{3,2,1,0:T(8,128)(2,1)}, u32[]{:S(2)}, u32[]{:S(2)}) %collective-permute-start.38) | collective-permute-done | bytes 1048608 | tf_op jit(solution)/shard_map/ppermute | solution.py:52
  779.4 18.7 %collective-permute-done.39.refs_4_ = bf16[4,2,128,512]{3,2,1,0:T(8,128)(2,1)} collective-permute-done((bf16[4,2,128,512]{3,2,1,0:T(8,128)(2,1)}, bf16[4,2,128,512]{3,2,1,0:T(8,128)(2,1)}, u32[]{:S(2)}, u32[]{:S(2)}) %collective-permute-start.39) | collective-permute-done | bytes 1048608 | tf_op jit(solution)/shard_map/ppermute | solution.py:52
  821.1 11.0 %fusion.3 = (f32[2048]{0:T(1024)S(1)}, bf16[1024,2048]{1,0:T(8,128)(2,1)}) fusion(f32[1024]{0:T(1024)S(1)} %copy-done.60, bf16[256,2048]{1,0:T(8,128)(2,1)} %collective-permute-done.2, bf16[256,2048]{1,0:T(8,128)(2,1)S(1)} %copy-done.32, bf16[256,2048]{1,0:T(8,128)(2,1)S(1)} %copy-done.30, bf16[256,2048]{1,0:T(8,128)(2,1)S(1)} %bitcast.246, ...), kind=kOutput, calls=%fused_computation.7 | convolution fusion | flops 6467614720 | bytes 17838080 | tf_op jit(solution)/shard_map/dot_general | solution.py:45
  833.1 11.1 %concatenate.80 = bf16[4,8,64,1664]{3,2,0,1:T(8,128)(2,1)} concatenate(bf16[4,8,64,1536]{3,2,0,1:T(8,128)(2,1)} %copy.146, bf16[4,8,64,1]{3,2,0,1:T(8,128)(2,1)S(1)} %copy.147, bf16[4,8,64,1]{3,2,0,1:T(8,128)(2,1)S(1)} %copy.148, bf16[4,8,64,126]{3,2,0,1:T(8,128)(2,1)S(1)} %broadcast_in_dim.61), dimensions={3} | concatenate | bytes 13631488 | tf_op jit(solution)/shard_map/concatenate | solution.py:599
  852.4 19.4 %collective-permute-done.40 = bf16[256,2048]{1,0:T(8,128)(2,1)} collective-permute-done((bf16[256,2048]{1,0:T(8,128)(2,1)}, bf16[256,2048]{1,0:T(8,128)(2,1)}, u32[]{:S(2)}, u32[]{:S(2)}) %collective-permute-start.40) | collective-permute-done | bytes 1048608 | tf_op jit(solution)/shard_map/ppermute | solution.py:52
  878.3 19.4 %collective-permute-done.41 = bf16[256,2048]{1,0:T(8,128)(2,1)} collective-permute-done((bf16[256,2048]{1,0:T(8,128)(2,1)}, bf16[256,2048]{1,0:T(8,128)(2,1)}, u32[]{:S(2)}, u32[]{:S(2)}) %collective-permute-start.41) | collective-permute-done | bytes 1048608 | tf_op jit(solution)/shard_map/ppermute | solution.py:52
  911.2 28.3 %reduce-scatter.6.cloned.1.call-done = bf16[4,1,64,1664]{3,2,0,1:T(8,128)(2,1)} async-done(((bf16[4,8,64,1664]{3,2,0,1:T(8,128)(2,1)}), bf16[4,1,64,1664]{3,2,0,1:T(8,128)(2,1)}) %reduce-scatter.6.cloned.1.call-update) | async-done | bytes 851984 | tf_op jit(solution)/shard_map/reduce_scatter | solution.py:609
  952.7 31.1 %reduce-scatter.8.cloned.1.call-done = bf16[64,2048]{1,0:T(8,128)(2,1)} async-done(((bf16[512,2048]{1,0:T(8,128)(2,1)}), bf16[64,2048]{1,0:T(8,128)(2,1)}) %reduce-scatter.8.cloned.1.call-update) | async-done | bytes 262160 | tf_op jit(solution)/shard_map/reduce_scatter | solution.py:592
  (437 shorter events, 318.4 us)
Async XLA Ops:
  7.2 95.0 %all-gather.14.cloned.1.call-start = ((), (), s32[]{:S(2)}) async-start(), calls=%async_computation.17 | async-start | bytes 1351680 | tf_op jit(solution)/shard_map/all_gather | solution.py:345
  12.5 121.7 %all-gather.16.cloned.1.call-start = ((), (), s32[]{:S(2)}) async-start(), calls=%async_computation.18 | async-start | bytes 7077888 | tf_op jit(solution)/shard_map/all_gather | solution.py:358
  43.6 171.1 %all-gather.8.cloned.1.call-start = ((), (), s32[]{:S(2)}) async-start(), calls=%async_computation.9 | async-start | bytes 2359296 | tf_op jit(solution)/shard_map/all_gather | solution.py:361
  44.8 30.5 %collective-permute-start = (bf16[256,2048]{1,0:T(8,128)(2,1)S(1)}, bf16[256,2048]{1,0:T(8,128)(2,1)S(1)}, u32[]{:S(2)}, u32[]{:S(2)}) collective-permute-start(bf16[256,2048]{1,0:T(8,128)(2,1)S(1)} %bitcast.242), channel_id=1, source_target_pairs={{0,8},{8,16},{16,24},{24,0},{1,9},{9,17},{17,25},{25,1},{2,10},{10... | collective-permute-start | bytes 3145736 | tf_op jit(solution)/shard_map/ppermute | solution.py:52
  52.8 380.3 %all-gather.10.cloned.1.call-start = ((), (), s32[]{:S(2)}) async-start(), calls=%async_computation.10 | async-start | bytes 5242880 | tf_op jit(solution)/shard_map/all_gather | solution.py:366
  75.5 372.5 %all-gather.12.cloned.1.call-start = ((), (), s32[]{:S(2)}) async-start(), calls=%async_computation.11 | async-start | bytes 5242880 | tf_op jit(solution)/shard_map/all_gather | solution.py:369
  154.5 42.7 %collective-permute-start.4 = (bf16[4,2,128,512]{3,2,1,0:T(8,128)(2,1)S(1)}, bf16[4,2,128,512]{3,2,1,0:T(8,128)(2,1)}, u32[]{:S(2)}, u32[]{:S(2)}) collective-permute-start(bf16[4,2,128,512]{3,2,1,0:T(8,128)(2,1)S(1)} %get-tuple-element.24.refs_4_.refs_3_), channel_id=1, source_target_pairs={{0,4},{4,0},{1,5},{5,1},{2,6},{6,2},{3,7},{7,3},{8,12},{12,8},{9,1... | collective-permute-start | bytes 3145736 | tf_op jit(solution)/shard_map/ppermute | solution.py:52
  218.2 44.8 %collective-permute-start.5 = (bf16[256,2048]{1,0:T(8,128)(2,1)}, bf16[256,2048]{1,0:T(8,128)(2,1)}, u32[]{:S(2)}, u32[]{:S(2)}) collective-permute-start(bf16[256,2048]{1,0:T(8,128)(2,1)} %convolution_convert_fusion.6), channel_id=1, source_target_pairs={{0,8},{8,16},{16,24},{24,0},{1,9},{9,17},{17,25},{25,1},{2,10},{10... | collective-permute-start | bytes 3145736 | tf_op jit(solution)/shard_map/ppermute | solution.py:52
  222.4 45.5 %collective-permute-start.19 = (bf16[128,2048]{1,0:T(8,128)(2,1)}, bf16[128,2048]{1,0:T(8,128)(2,1)}, u32[]{:S(2)}, u32[]{:S(2)}) collective-permute-start(bf16[128,2048]{1,0:T(8,128)(2,1)} %get-tuple-element.142), channel_id=1, source_target_pairs={{0,2},{2,0},{1,3},{3,1},{4,6},{6,4},{5,7},{7,5},{8,10},{10,8},{9,1... | collective-permute-start | bytes 1572872 | tf_op jit(solution)/shard_map/ppermute | solution.py:81
  222.5 48.4 %collective-permute-start.20 = (bf16[128,2048]{1,0:T(8,128)(2,1)}, bf16[128,2048]{1,0:T(8,128)(2,1)}, u32[]{:S(2)}, u32[]{:S(2)}) collective-permute-start(bf16[128,2048]{1,0:T(8,128)(2,1)} %get-tuple-element.141), channel_id=1, source_target_pairs={{0,4},{4,0},{1,5},{5,1},{2,6},{6,2},{3,7},{7,3},{8,12},{12,8},{9,1... | collective-permute-start | bytes 1572872 | tf_op jit(solution)/shard_map/ppermute | solution.py:81
  223.5 651.2 %reduce-scatter.12.cloned.1.call-start = ((), (), s32[]{:S(2)}) async-start(), calls=%async_computation.15 | async-start | bytes 5242880 | tf_op jit(solution)/shard_map/reduce_scatter | solution.py:497
  266.6 48.5 %collective-permute-start.6 = (bf16[256,2048]{1,0:T(8,128)(2,1)}, bf16[256,2048]{1,0:T(8,128)(2,1)}, u32[]{:S(2)}, u32[]{:S(2)}) collective-permute-start(bf16[256,2048]{1,0:T(8,128)(2,1)} %fusion.17), channel_id=1, source_target_pairs={{0,8},{8,16},{16,24},{24,0},{1,9},{9,17},{17,25},{25,1},{2,10},{10... | collective-permute-start | bytes 3145736 | tf_op jit(solution)/shard_map/ppermute | solution.py:52
  269.3 62.0 %collective-permute-start.21 = (bf16[256,2048]{1,0:T(8,128)(2,1)S(1)}, bf16[256,2048]{1,0:T(8,128)(2,1)S(1)}, u32[]{:S(2)}, u32[]{:S(2)}) collective-permute-start(bf16[256,2048]{1,0:T(8,128)(2,1)S(1)} %pad_maximum_fusion.10), channel_id=1, source_target_pairs={{0,4},{4,0},{1,5},{5,1},{2,6},{6,2},{3,7},{7,3},{8,12},{12,8},{9,1... | collective-permute-start | bytes 3145736 | tf_op jit(solution)/shard_map/ppermute | solution.py:81
  272.2 59.1 %collective-permute-start.22 = (bf16[256,2048]{1,0:T(8,128)(2,1)S(1)}, bf16[256,2048]{1,0:T(8,128)(2,1)S(1)}, u32[]{:S(2)}, u32[]{:S(2)}) collective-permute-start(bf16[256,2048]{1,0:T(8,128)(2,1)S(1)} %pad_maximum_fusion.11), channel_id=1, source_target_pairs={{0,2},{2,0},{1,3},{3,1},{4,6},{6,4},{5,7},{7,5},{8,10},{10,8},{9,1... | collective-permute-start | bytes 3145736 | tf_op jit(solution)/shard_map/ppermute | solution.py:81
  276.8 126.3 %collective-permute-start.23 = (bf16[512,2048]{1,0:T(8,128)(2,1)}, bf16[512,2048]{1,0:T(8,128)(2,1)}, u32[]{:S(2)}, u32[]{:S(2)}) collective-permute-start(bf16[512,2048]{1,0:T(8,128)(2,1)} %pad_maximum_fusion.5), channel_id=1, source_target_pairs={{0,1},{1,0},{2,3},{3,2},{4,5},{5,4},{6,7},{7,6},{8,9},{9,8},{10,11... | collective-permute-start | bytes 6291464 | tf_op jit(solution)/shard_map/ppermute | solution.py:81
  318.0 60.9 %collective-permute-start.7 = (bf16[256,2048]{1,0:T(8,128)(2,1)}, bf16[256,2048]{1,0:T(8,128)(2,1)}, u32[]{:S(2)}, u32[]{:S(2)}) collective-permute-start(bf16[256,2048]{1,0:T(8,128)(2,1)} %fusion.14), channel_id=1, source_target_pairs={{0,8},{8,16},{16,24},{24,0},{1,9},{9,17},{17,25},{25,1},{2,10},{10... | collective-permute-start | bytes 3145736 | tf_op jit(solution)/shard_map/ppermute | solution.py:52
  333.9 72.6 %collective-permute-start.24 = (bf16[512,2048]{1,0:T(8,128)(2,1)}, bf16[512,2048]{1,0:T(8,128)(2,1)}, u32[]{:S(2)}, u32[]{:S(2)}) collective-permute-start(bf16[512,2048]{1,0:T(8,128)(2,1)} %pad_maximum_fusion.6), channel_id=1, source_target_pairs={{0,1},{1,0},{2,3},{3,2},{4,5},{5,4},{6,7},{7,6},{8,9},{9,8},{10,11... | collective-permute-start | bytes 6291464 | tf_op jit(solution)/shard_map/ppermute | solution.py:81
  478.8 426.7 %reduce-scatter.14.cloned.1.call-start = ((), (), s32[]{:S(2)}) async-start(), calls=%async_computation.16 | async-start | bytes 5242880 | tf_op jit(solution)/shard_map/reduce_scatter | solution.py:494
  501.5 38.5 %collective-permute-start.25 = (bf16[8,128,2048]{2,1,0:T(8,128)(2,1)}, bf16[8,128,2048]{2,1,0:T(8,128)(2,1)}, u32[]{:S(2)}, u32[]{:S(2)}) collective-permute-start(bf16[8,128,2048]{2,1,0:T(8,128)(2,1)} %bitcast.56), channel_id=1, source_target_pairs={{0,1},{1,0},{2,3},{3,2},{4,5},{5,4},{6,7},{7,6},{8,9},{9,8},{10,11... | collective-permute-start | bytes 12582920 | tf_op jit(solution)/shard_map/ppermute | solution.py:81
  531.0 377.3 %reduce-scatter.10.cloned.1.call-start = ((), (), s32[]{:S(2)}) async-start(), calls=%async_computation.14 | async-start | bytes 2433024 | tf_op jit(solution)/shard_map/reduce_scatter | solution.py:548
  551.9 42.4 %collective-permute-start.15 = (bf16[2,128,2048]{2,1,0:T(8,128)(2,1)S(1)}, bf16[2,128,2048]{2,1,0:T(8,128)(2,1)S(1)}, u32[]{:S(2)}, u32[]{:S(2)}) collective-permute-start(bf16[2,128,2048]{2,1,0:T(8,128)(2,1)S(1)} %get-tuple-element.134), channel_id=1, source_target_pairs={{0,4},{4,0},{1,5},{5,1},{2,6},{6,2},{3,7},{7,3},{8,12},{12,8},{9,1... | collective-permute-start | bytes 3145736 | tf_op jit(solution)/shard_map/ppermute | solution.py:81
  553.2 41.8 %collective-permute-start.17 = (bf16[2,128,2048]{2,1,0:T(8,128)(2,1)S(1)}, bf16[2,128,2048]{2,1,0:T(8,128)(2,1)S(1)}, u32[]{:S(2)}, u32[]{:S(2)}) collective-permute-start(bf16[2,128,2048]{2,1,0:T(8,128)(2,1)S(1)} %get-tuple-element.135), channel_id=1, source_target_pairs={{0,2},{2,0},{1,3},{3,1},{4,6},{6,4},{5,7},{7,5},{8,10},{10,8},{9,1... | collective-permute-start | bytes 3145736 | tf_op jit(solution)/shard_map/ppermute | solution.py:81
  573.3 32.8 %collective-permute-start.27 = (bf16[128,2048]{1,0:T(8,128)(2,1)S(1)}, bf16[128,2048]{1,0:T(8,128)(2,1)S(1)}, u32[]{:S(2)}, u32[]{:S(2)}) collective-permute-start(bf16[128,2048]{1,0:T(8,128)(2,1)S(1)} %slice_bitcast_fusion.2), channel_id=1, source_target_pairs={{0,2},{2,0},{1,3},{3,1},{4,6},{6,4},{5,7},{7,5},{8,10},{10,8},{9,1... | collective-permute-start | bytes 1572872 | tf_op jit(solution)/shard_map/ppermute | solution.py:81
  573.9 32.4 %collective-permute-start.29 = (bf16[128,2048]{1,0:T(8,128)(2,1)S(1)}, bf16[128,2048]{1,0:T(8,128)(2,1)S(1)}, u32[]{:S(2)}, u32[]{:S(2)}) collective-permute-start(bf16[128,2048]{1,0:T(8,128)(2,1)S(1)} %slice_bitcast_fusion), channel_id=1, source_target_pairs={{0,4},{4,0},{1,5},{5,1},{2,6},{6,2},{3,7},{7,3},{8,12},{12,8},{9,1... | collective-permute-start | bytes 1572872 | tf_op jit(solution)/shard_map/ppermute | solution.py:81
  617.8 46.2 %collective-permute-start.35 = (bf16[256,2048]{1,0:T(8,128)(2,1)S(1)}, bf16[256,2048]{1,0:T(8,128)(2,1)S(1)}, u32[]{:S(2)}, u32[]{:S(2)}) collective-permute-start(bf16[256,2048]{1,0:T(8,128)(2,1)S(1)} %get-tuple-element.118), channel_id=1, source_target_pairs={{0,8},{8,16},{16,24},{24,0},{1,9},{9,17},{17,25},{25,1},{2,10},{10... | collective-permute-start | bytes 3145736 | tf_op jit(solution)/shard_map/ppermute | solution.py:52
  690.0 36.5 %collective-permute-start.37 = (bf16[256,2048]{1,0:T(8,128)(2,1)S(1)}, bf16[256,2048]{1,0:T(8,128)(2,1)S(1)}, u32[]{:S(2)}, u32[]{:S(2)}) collective-permute-start(bf16[256,2048]{1,0:T(8,128)(2,1)S(1)} %collective-permute-done.36), channel_id=1, source_target_pairs={{0,8},{8,16},{16,24},{24,0},{1,9},{9,17},{17,25},{25,1},{2,10},{10... | collective-permute-start | bytes 3145736 | tf_op jit(solution)/shard_map/ppermute | solution.py:52
  754.4 43.6 %collective-permute-start.39 = (bf16[4,2,128,512]{3,2,1,0:T(8,128)(2,1)}, bf16[4,2,128,512]{3,2,1,0:T(8,128)(2,1)}, u32[]{:S(2)}, u32[]{:S(2)}) collective-permute-start(bf16[4,2,128,512]{3,2,1,0:T(8,128)(2,1)} %get-tuple-element.32), channel_id=1, source_target_pairs={{0,4},{4,0},{1,5},{5,1},{2,6},{6,2},{3,7},{7,3},{8,12},{12,8},{9,1... | collective-permute-start | bytes 3145736 | tf_op jit(solution)/shard_map/ppermute | solution.py:52
  762.9 176.5 %reduce-scatter.6.cloned.1.call-start = ((), (), s32[]{:S(2)}) async-start(), calls=%async_computation.12 | async-start | bytes 7667712 | tf_op jit(solution)/shard_map/reduce_scatter | solution.py:609
  844.2 139.7 %reduce-scatter.8.cloned.1.call-start = ((), (), s32[]{:S(2)}) async-start(), calls=%async_computation.13 | async-start | bytes 2359296 | tf_op jit(solution)/shard_map/reduce_scatter | solution.py:592
  874.7 36.5 %all-to-all-start.3 = ((bf16[8,64,1024]{2,1,0:T(8,128)(2,1)}), bf16[8,64,1024]{2,1,0:T(8,128)(2,1)S(1)}, u32[]{:S(2)}, u32[]{:S(2)}) async-start(bf16[8,64,1024]{2,1,0:T(8,128)(2,1)} %bitcast.273), calls=%async_computation.7 | async-start | bytes 2097152 | tf_op jit(solution)/shard_map/all_to_all | solution.py:498
  900.7 85.0 %collective-permute-start.42 = (bf16[256,2048]{1,0:T(8,128)(2,1)}, bf16[256,2048]{1,0:T(8,128)(2,1)}, u32[]{:S(2)}, u32[]{:S(2)}) collective-permute-start(bf16[256,2048]{1,0:T(8,128)(2,1)} %add_convert_fusion), channel_id=1, source_target_pairs={{0,8},{8,16},{16,24},{24,0},{1,9},{9,17},{17,25},{25,1},{2,10},{10... | collective-permute-start | bytes 3145736 | tf_op jit(solution)/shard_map/ppermute | solution.py:52
  939.5 52.9 %all-to-all-start.2 = ((bf16[4,64,1664]{2,1,0:T(8,128)(2,1)}), bf16[4,64,1664]{2,1,0:T(8,128)(2,1)S(1)}, u32[]{:S(2)}, u32[]{:S(2)}) async-start(bf16[4,64,1664]{2,1,0:T(8,128)(2,1)} %bitcast.282), calls=%async_computation.3 | async-start | bytes 1703936 | tf_op jit(solution)/shard_map/all_to_all | solution.py:615
  (99 other events, 2555.9 us)
Sparse Core Ops, SparseCore 0:
  12.6 64.4 all-gather.13
  79.0 44.8 all-gather.15
  125.9 28.0 all-gather.7
  155.3 103.1 all-gather.9
  260.0 123.2 all-gather.11
  478.9 81.9 reduce-scatter.11
  563.3 96.2 reduce-scatter.13
  763.0 109.5 reduce-scatter.9
  876.5 62.9 reduce-scatter.5
  942.6 41.1 reduce-scatter.7

commit v2 on v1

v2 whole, which is shorter than its diff:
```python
import functools
import math

import jax
import jax.numpy as jnp
from jax import lax
from jax.experimental import pallas as pl
from jax.experimental.pallas import tpu as pltpu
from jax.sharding import Mesh, PartitionSpec as P

H = 16
HD = 128
FF = 8192
RH = 256
RING = 4
SEQS = 2
GROUP_HEADS = H // RING
GROUP_WIDTH = GROUP_HEADS * HD
SCALE = 1.0 / math.sqrt(HD)
VMEM_LIMIT = 48 * 1024 * 1024
TILE = 256
LANES = 128

epsilon = 1e-05
theta_base = 10000.0
neg_large = -1e30
bf16 = jnp.bfloat16
f32 = jnp.float32
PLANE = ("yb", "bx", "bc")
EVERY = ("za",) + PLANE
SWAP = [(0, 1), (1, 0)]


def dot(left_mat, right_mat):
    return lax.dot_general(
        left_mat, right_mat, (((1,), (0,)), ((), ())), preferred_element_type=f32
    )


def dot_rows(left_mat, right_mat):
    return lax.dot_general(
        left_mat, right_mat, (((0,), (0,)), ((), ())), preferred_element_type=f32
    )


def dot_cols(left_mat, right_mat):
    return lax.dot_general(
        left_mat, right_mat, (((1,), (1,)), ((), ())), preferred_element_type=f32
    )


def onward(block, axis):
    size = lax.axis_size(axis)
    return lax.ppermute(block, axis, [(i, (i + 1) % size) for i in range(size)])


def after(value, *others):
    return lax.optimization_barrier((value, others))[0]


def add_low(left, right):
    return (left.astype(f32) + right.astype(f32)).astype(left.dtype)


def ring_gather(block, axis):
    slots = [block]
    for _ in range(1, lax.axis_size(axis)):
        slots.append(onward(slots[-1], axis))
    return slots


def ring_scatter(parts, axis, hops=None):
    running = parts[1]()
    for slot in range(2, lax.axis_size(axis)):
        moved = onward(running, axis)
        if hops is not None:
            hops.append(moved)
        running = add_low(parts[slot](), moved)
    moved = onward(running, axis)
    return parts[0]().astype(f32) + moved.astype(f32)


def in_order(slots, axis):
    size = lax.axis_size(axis)
    run = slots[::-1] + slots[:0:-1]
    rows = slots[0].shape[0]
    start = (size - 1 - lax.axis_index(axis)) * rows
    return lax.dynamic_slice_in_dim(
        jnp.concatenate(run, axis=0), start, size * rows, axis=0
    )


def gather_in_order(block, axis):
    return in_order(ring_gather(block, axis), axis)


def rotate(pieces, axis):
    size, me = lax.axis_size(axis), lax.axis_index(axis)
    came = [pieces(me)]
    for far in range(1, size):
        route = [(i, (i + far) % size) for i in range(size)]
        came.append(lax.ppermute(pieces((me + far) % size), axis, route))
    return came


def exchange(pieces, axis):
    return in_order(
        rotate(lambda i: lax.dynamic_index_in_dim(pieces, i, 0), axis), axis
    )


EARLY = [(0, 0, 0), (0, 1, 0), (1, 0, 0), (1, 0, 1)]
LATE = [(0, 0, 1), (0, 1, 1), (1, 1, 0), (1, 1, 1)]
CHUNKS = [(h, x, y, c) for part in (EARLY, LATE) for c in (0, 1) for h, x, y in part]


def swap(block, axis):
    return lax.ppermute(block, axis, SWAP)


def plane_gather(block, between=lambda early: ()):
    half = block.shape[0] // 2
    first, second = block[:half], block[half:]
    early = jnp.concatenate(
        [first, swap(first, "bx"), second, swap(second, "yb")], axis=0
    )
    late = jnp.concatenate(
        [swap(early[: 2 * half], "yb"), swap(early[2 * half :], "bx")], axis=0
    )
    groups = [(early, swap(early, "bc"))]
    late = after(late, between(groups[0]))
    return groups + [(late, swap(late, "bc"))]


def plane_scatter_late(terms):
    late = add_low(terms[0], swap(terms[1], "bc"))
    half = late.shape[0] // 2
    return late, swap(late[:half], "yb"), swap(late[half:], "bx")


def plane_scatter(terms, came):
    rows = terms[0].shape[0] // 4
    early = add_low(terms[0], swap(terms[1], "bc"))
    first = add_low(early[: 2 * rows], came[1])
    second = add_low(early[2 * rows :], came[2])
    first_sum = first[:rows].astype(f32) + swap(first[rows:], "bx").astype(f32)
    second_sum = second[:rows].astype(f32) + swap(second[rows:], "yb").astype(f32)
    return jnp.concatenate([first_sum, second_sum], axis=0)


def keep_and_swap(blocks, axis, dim):
    me = lax.axis_index(axis)
    kept = lax.dynamic_index_in_dim(blocks, me, dim, keepdims=False)
    sent = lax.dynamic_index_in_dim(blocks, 1 - me, dim, keepdims=False)
    return add_low(kept, swap(sent, axis))


def plane_reduce(blocks, steps=None):
    both = keep_and_swap(blocks, "bc", 3)
    middle = blocks.shape[-1] // 2
    first = keep_and_swap(both[..., :middle], "yb", 1)
    second = keep_and_swap(both[..., middle:], "bx", 2)
    if steps is not None:
        steps.extend([both, (first, second)])
    first = keep_and_swap(first, "bx", 1)
    second = keep_and_swap(second, "yb", 1)
    if steps is not None:
        steps.append((first, second))
    return jnp.concatenate([first, second], axis=-1)


def rope_kernel(joint_ref, cos_ref, sin_ref, query_ref, both_ref):
    cosine, sine = cos_ref[...], sin_ref[...]
    for head in range(GROUP_HEADS):
        for part, out_ref in ((0, query_ref), (1, both_ref)):
            at = part * GROUP_WIDTH + head * HD
            raw = joint_ref[0, :, at : at + HD]
            turned = raw * cosine + pltpu.roll(raw, HD // 2, 1) * sine
            out_ref[0, :, head * HD : (head + 1) * HD] = turned.astype(bf16)
    both_ref[0, :, GROUP_WIDTH:] = joint_ref[0, :, 2 * GROUP_WIDTH :].astype(bf16)


def rope(joint, cosine, sine):
    seqs, block_len, width = joint.shape
    rows = lambda w: pl.BlockSpec((1, block_len, w), lambda b: (b, 0, 0))
    table = pl.BlockSpec((block_len, HD), lambda b: (0, 0))
    return pl.pallas_call(
        rope_kernel,
        grid=(seqs,),
        in_specs=[rows(3 * GROUP_WIDTH), table, table],
        out_specs=[rows(GROUP_WIDTH), rows(2 * GROUP_WIDTH)],
        out_shape=[
            jax.ShapeDtypeStruct((seqs, block_len, GROUP_WIDTH), bf16),
            jax.ShapeDtypeStruct((seqs, block_len, 2 * GROUP_WIDTH), bf16),
        ],
        compiler_params=pltpu.CompilerParams(vmem_limit_bytes=VMEM_LIMIT),
        name="rope",
    )(joint, cosine, sine)


def turn_back(grad, cosine, sine):
    return (grad * cosine - pltpu.roll(grad, HD // 2, 1) * sine).astype(bf16)


def query_back_kernel(terms, *refs):
    cos_ref, sin_ref, out_ref = refs[terms:]
    cosine, sine = cos_ref[0], sin_ref[0]
    for seq in range(out_ref.shape[1]):
        for head in range(GROUP_HEADS):
            at = slice(head * HD, (head + 1) * HD)
            grad = sum(ref[0, seq, :, at].astype(f32) for ref in refs[:terms])
            out_ref[0, seq, :, at] = turn_back(grad, cosine, sine)


def both_back_kernel(terms, *refs):
    key_refs, value_refs = refs[:terms], refs[terms : 2 * terms]
    cos_ref, sin_ref, _, out_ref = refs[2 * terms :]

    @pl.when(pl.program_id(1) == 0)
    def _():
        cosine, sine = cos_ref[0], sin_ref[0]
        for seq in range(out_ref.shape[1]):
            for head in range(GROUP_HEADS):
                at = slice(head * HD, (head + 1) * HD)
                grad = sum(ref[0, seq, :, at].astype(f32) for ref in key_refs)
                out_ref[0, seq, :, at] = turn_back(grad, cosine, sine)

    @pl.when(pl.program_id(1) == 1)
    def _():
        total = sum(ref[0].astype(f32) for ref in value_refs)
        out_ref[0] = total.astype(bf16)


def joint_shape(grad):
    return jax.ShapeDtypeStruct(grad.shape[:3] + (3 * GROUP_WIDTH,), bf16)


def query_back(grads, cosine, sine):
    slots, seqs, block_len, width = grads[0].shape
    rows = pl.BlockSpec((1, seqs, block_len, width), lambda s: (s, 0, 0, 0))
    table = pl.BlockSpec((1, block_len, HD), lambda s: (s, 0, 0))
    return pl.pallas_call(
        functools.partial(query_back_kernel, len(grads)),
        grid=(slots,),
        in_specs=[rows] * len(grads) + [table, table],
        out_specs=rows,
        out_shape=joint_shape(grads[0]),
        compiler_params=pltpu.CompilerParams(vmem_limit_bytes=VMEM_LIMIT),
        name="query_back",
    )(*grads, cosine, sine)


def both_back(keys, values, cosine, sine, joint):
    slots, seqs, block_len, width = keys[0].shape
    rows = pl.BlockSpec((1, seqs, block_len, width), lambda s, j: (s, 0, 0, 0))
    table = pl.BlockSpec((1, block_len, HD), lambda s, j: (s, 0, 0))
    terms = len(keys)
    return pl.pallas_call(
        functools.partial(both_back_kernel, terms),
        grid=(slots, 2),
        in_specs=[rows] * (2 * terms)
        + [table, table, pl.BlockSpec(memory_space=pl.ANY)],
        out_specs=pl.BlockSpec(
            (1, seqs, block_len, width), lambda s, j: (s, 0, 0, 1 + j)
        ),
        out_shape=joint_shape(keys[0]),
        input_output_aliases={2 * terms + 2: 0},
        compiler_params=pltpu.CompilerParams(vmem_limit_bytes=VMEM_LIMIT),
        name="both_back",
    )(*keys, *values, cosine, sine, joint)


def flat(ref):
    slots, _, block_len, width = ref.shape
    return ref[:, 0].reshape(slots * block_len, width)


def end_to_end(refs):
    return jnp.concatenate([ref[0] for ref in refs], axis=0)


def by_piece(refs, slots):
    return [refs[i : i + slots] for i in range(0, len(refs), slots)]


def attend_kernel(slots, pieces, *refs):
    active_ref, query_refs = refs[0], refs[1 : 1 + slots]
    rest = refs[1 + slots :]
    key_refs = by_piece(rest[: pieces * slots], slots)
    value_refs = by_piece(rest[pieces * slots : 2 * pieces * slots], slots)
    qplace_ref, kplace_ref, out_ref, low_ref, log_ref = rest[2 * pieces * slots :]
    queries = end_to_end(query_refs)
    query_places = qplace_ref[...]
    masked = []
    for piece in range(pieces):
        scores = dot_cols(queries, end_to_end(key_refs[piece])) * SCALE
        allowed = kplace_ref[piece] <= query_places
        masked.append(jnp.where(allowed, scores, neg_large))
    top = functools.reduce(
        jnp.maximum, [jnp.max(m, axis=1, keepdims=True) for m in masked]
    )
    total, gathered = 0.0, 0.0
    for piece in range(pieces):
        weights = jnp.exp(masked[piece] - top)
        total = total + jnp.sum(weights, axis=1, keepdims=True)
        gathered = gathered + dot(weights.astype(bf16), end_to_end(value_refs[piece]))
    result = gathered / total
    out_ref[:, 0] = result.reshape(out_ref.shape[0], out_ref.shape[2], HD)
    kept = active_ref[pl.program_id(0)]
    low_ref[:, 0] = (
        (result * kept).astype(bf16).reshape(out_ref.shape[0], out_ref.shape[2], HD)
    )
    log_ref[0, 0] = top + jnp.log(total)


def attend(active, queries, boths, query_places, key_places):
    slots, pieces = len(queries), len(boths)
    seqs, block_len, width = queries[0].shape
    rows = slots * block_len
    heads = width // HD
    own = pl.BlockSpec((1, block_len, HD), lambda s, h: (s, 0, h))
    value = pl.BlockSpec((1, block_len, HD), lambda s, h: (s, 0, heads + h))
    tile = pl.BlockSpec((slots, 1, block_len, HD), lambda s, h: (0, s, 0, h))
    every = [both for piece in boths for both in piece]
    shape = (slots, seqs, block_len, width)
    return pl.pallas_call(
        functools.partial(attend_kernel, slots, pieces),
        grid=(seqs, heads),
        in_specs=[pl.BlockSpec(memory_space=pltpu.SMEM)]
        + [own] * slots
        + [own] * len(every)
        + [value] * len(every)
        + [
            pl.BlockSpec((rows, 1), lambda s, h: (0, 0)),
            pl.BlockSpec((pieces, 1, rows), lambda s, h: (0, 0, 0)),
        ],
        out_specs=[
            tile,
            tile,
            pl.BlockSpec((1, 1, rows, 1), lambda s, h: (s, h, 0, 0)),
        ],
        out_shape=[
            jax.ShapeDtypeStruct(shape, f32),
            jax.ShapeDtypeStruct(shape, bf16),
            jax.ShapeDtypeStruct((seqs, heads, rows, 1), f32),
        ],
        compiler_params=pltpu.CompilerParams(vmem_limit_bytes=VMEM_LIMIT),
        name="attend",
    )(active, *queries, *every, *every, query_places, key_places)


def attend_back_kernel(slots, pieces, *refs):
    query_refs, rest = refs[:slots], refs[slots:]
    key_refs = by_piece(rest[: pieces * slots], slots)
    value_refs = by_piece(rest[pieces * slots : 2 * pieces * slots], slots)
    rest = rest[2 * pieces * slots :]
    grad_refs, rest = rest[:slots], rest[slots:]
    out_ref, log_ref, qplace_ref, kplace_ref, dq_ref = rest[:5]
    dk_refs, dv_refs = rest[5 : 5 + pieces], rest[5 + pieces :]
    queries, grads = end_to_end(query_refs), end_to_end(grad_refs)
    query_places = qplace_ref[...]
    dots = jnp.sum(grads.astype(f32) * flat(out_ref), axis=1, keepdims=True)
    log_norm = log_ref[0, 0]
    grad_query = 0.0
    shape = (slots, query_refs[0].shape[1], HD)
    for piece in range(pieces):
        keys, values = end_to_end(key_refs[piece]), end_to_end(value_refs[piece])
        scores = dot_cols(queries, keys) * SCALE
        allowed = kplace_ref[piece] <= query_places
        probs = jnp.exp(jnp.where(allowed, scores - log_norm, neg_large))
        grad_probs = dot_cols(grads, values)
        dv_refs[piece][:, 0] = (
            dot_rows(probs.astype(bf16), grads)
            .astype(dv_refs[piece].dtype)
            .reshape(shape)
        )
        grad_scores = (probs * (grad_probs - dots)).astype(bf16)
        dk_refs[piece][:, 0] = (
            (dot_rows(grad_scores, queries) * SCALE)
            .astype(dk_refs[piece].dtype)
            .reshape(shape)
        )
        grad_query = grad_query + dot(grad_scores, keys)
    dq_ref[:, 0] = (grad_query * SCALE).reshape(shape)


def attend_back(queries, boths, grads, out, logs, query_places, key_places, name):
    slots, pieces = len(queries), len(boths)
    seqs, block_len, width = queries[0].shape
    rows = slots * block_len
    heads = width // HD
    own = pl.BlockSpec((1, block_len, HD), lambda s, h: (s, 0, h))
    value = pl.BlockSpec((1, block_len, HD), lambda s, h: (s, 0, heads + h))
    tile = pl.BlockSpec((slots, 1, block_len, HD), lambda s, h: (0, s, 0, h))
    every = [both for piece in boths for both in piece]
    shape = (slots, seqs, block_len, width)
    wide = jax.ShapeDtypeStruct(shape, f32)
    low = jax.ShapeDtypeStruct(shape, bf16)
    found = pl.pallas_call(
        functools.partial(attend_back_kernel, slots, pieces),
        grid=(seqs, heads),
        in_specs=[own] * slots
        + [own] * len(every)
        + [value] * len(every)
        + [own] * slots
        + [
            tile,
            pl.BlockSpec((1, 1, rows, 1), lambda s, h: (s, h, 0, 0)),
            pl.BlockSpec((rows, 1), lambda s, h: (0, 0)),
            pl.BlockSpec((pieces, 1, rows), lambda s, h: (0, 0, 0)),
        ],
        out_specs=[tile] * (1 + 2 * pieces),
        out_shape=[wide] + [low] * (2 * pieces),
        compiler_params=pltpu.CompilerParams(vmem_limit_bytes=VMEM_LIMIT),
        name=name,
    )(*queries, *every, *every, *grads, out, logs, query_places, key_places)
    return found[0], found[1 : 1 + pieces], found[1 + pieces :]


def feed_up_kernel(steps, blocks, passed, *refs):
    in_refs, refs = refs[:blocks], refs[blocks:]
    heat_ref, forced_ref, route_in_ref, route_out_ref, up_ref = refs[:5]
    all_in_ref, gated_ref, scale_ref, rectified_ref = refs[5 + passed :]
    block = in_refs[0][...]
    for k in range(1, blocks):
        block = jnp.where(pl.program_id(0) < k * steps, block, in_refs[k][...])
    all_in_ref[...] = block
    units = up_ref.shape[1]
    band = units // 4

    squashed = jnp.tanh(dot(block, route_in_ref[...])).astype(bf16)
    logits = dot(squashed, route_out_ref[...]) / heat_ref[0]
    lane = lax.broadcasted_iota(jnp.int32, logits.shape, 1)
    logits = jnp.where(lane < 4, logits, neg_large)
    weights = jnp.exp(logits - jnp.max(logits, axis=1, keepdims=True))
    routed = weights / jnp.sum(weights, axis=1, keepdims=True)
    forced = forced_ref[...]
    chosen = jnp.where(lane.astype(f32) == forced - 1.0, 1.0, 0.0)
    mix = jnp.where(forced > 0.0, chosen, routed)
    scales = [mix[:, 3:4]]
    for k in (2, 1, 0):
        scales.insert(0, scales[0] + mix[:, k : k + 1])
    scale_ref[...] = by_lane(scales, scale_ref.shape)

    rectified = jnp.maximum(dot(block, up_ref[...]), 0.0)
    rectified_ref[...] = rectified
    gated_ref[...] = (rectified * rectified * by_band(scales, band, units)).astype(bf16)


def by_lane(columns, shape):
    lane = lax.broadcasted_iota(jnp.int32, shape, 1)
    found = jnp.zeros(shape, f32)
    for k, column in enumerate(columns):
        found = jnp.where(lane == k, column, found)
    return found


def by_band(columns, band, units):
    rows = columns[0].shape[0]
    if band % LANES == 0:
        return jnp.concatenate(
            [jnp.broadcast_to(column, (rows, band)) for column in columns], axis=1
        )
    at = lax.broadcasted_iota(jnp.int32, (rows, units), 1) // band
    found = jnp.broadcast_to(columns[3], (rows, units))
    for k in range(3):
        found = jnp.where(at == k, columns[k], found)
    return found


def band_sums(array, band):
    if band % LANES == 0:
        parts = [array[:, k * band : (k + 1) * band] for k in range(4)]
    else:
        at = lax.broadcasted_iota(jnp.int32, array.shape, 1) // band
        parts = [jnp.where(at == k, array, 0.0) for k in range(4)]
    return [jnp.sum(part, axis=1, keepdims=True) for part in parts]


def feed_down_kernel(count, steps, passed, *refs):
    adjoint_ref, scale_ref, rectified_ref, gated_ref, up_ref, down_ref = refs[:6]
    grad_up_ref, split_refs = refs[6 + passed], refs[7 + passed :]
    units = up_ref.shape[1]
    band = units // 4
    down = down_ref[...]
    rectified = rectified_ref[...]
    grad_gated = dot_cols(adjoint_ref[...], down)
    scales = [scale_ref[:, k : k + 1] for k in range(4)]
    twice = grad_gated * rectified
    grad_up = (twice * by_band(scales, band, units) * 2.0).astype(bf16)
    grad_up_ref[...] = grad_up
    sums = by_lane(band_sums(twice * rectified, band), split_refs[0].shape)
    grad_in = dot_cols(grad_up, up_ref[...]).astype(bf16)
    out = dot(gated_ref[...], down).astype(bf16)
    for k in range(count):

        @pl.when(pl.program_id(0) // steps == k)
        def _():
            for kind, value in enumerate((sums, grad_in, out)):
                split_refs[kind * count + k][...] = value


def tiles(width, at=0):
    return pl.BlockSpec((TILE, width), lambda i: (at + i, 0))


def fixed(array):
    return pl.BlockSpec(array.shape, lambda i: (0, 0), pipeline_mode=pl.Buffered(1))


def feed_up(blocks, heat, first, total, forced, route_in, route_out, up, passed):
    rows, width = blocks[0].shape
    tokens, count = rows * len(blocks), len(blocks)
    units = up.shape[1]
    at, steps = first // TILE, rows // TILE
    share = lambda k: pl.BlockSpec(
        (TILE, width), lambda i: (jnp.clip(i - k * steps, 0, steps - 1), 0)
    )
    before = count + 5
    return pl.pallas_call(
        functools.partial(feed_up_kernel, steps, count, len(passed)),
        grid=(tokens // TILE,),
        in_specs=[share(k) for k in range(count)]
        + [
            pl.BlockSpec(memory_space=pltpu.SMEM),
            tiles(1, at),
            fixed(route_in),
            fixed(route_out),
            fixed(up),
        ]
        + [pl.BlockSpec(memory_space=pl.ANY)] * len(passed),
        out_specs=[tiles(width, at), tiles(units, at), tiles(4), tiles(units)],
        out_shape=[
            jax.ShapeDtypeStruct((total, width), bf16),
            jax.ShapeDtypeStruct((total, units), bf16),
            jax.ShapeDtypeStruct((tokens, 4), f32),
            jax.ShapeDtypeStruct((tokens, units), f32),
        ],
        input_output_aliases={before + i: i for i in range(len(passed))},
        compiler_params=pltpu.CompilerParams(vmem_limit_bytes=VMEM_LIMIT),
        cost_estimate=pl.CostEstimate(
            flops=2 * tokens * width * units,
            bytes_accessed=2 * width * units + 6 * tokens * width,
            transcendentals=0,
        ),
        name="feed_up",
    )(*blocks, heat, forced, route_in, route_out, up, *passed)


def feed_down(adjoint, first, count, scale, rectified, gated, up, down, passed):
    total, width = adjoint.shape
    tokens, units = rectified.shape
    rows = tokens // count
    at, steps = first // TILE, rows // TILE
    share = lambda k, cols: pl.BlockSpec(
        (TILE, cols), lambda i: (jnp.clip(i - k * steps, 0, steps - 1), 0)
    )
    kinds = ((4, f32), (width, bf16), (width, bf16))
    found = pl.pallas_call(
        functools.partial(feed_down_kernel, count, steps, len(passed)),
        grid=(tokens // TILE,),
        in_specs=[
            tiles(width, at),
            tiles(4),
            tiles(units),
            tiles(units, at),
            fixed(up),
            fixed(down),
        ]
        + [pl.BlockSpec(memory_space=pl.ANY)] * len(passed),
        out_specs=[tiles(units, at)]
        + [share(k, cols) for cols, _ in kinds for k in range(count)],
        out_shape=[jax.ShapeDtypeStruct((total, units), bf16)]
        + [
            jax.ShapeDtypeStruct((rows, cols), dtype)
            for cols, dtype in kinds
            for _ in range(count)
        ],
        input_output_aliases={6 + i: i for i in range(len(passed))},
        compiler_params=pltpu.CompilerParams(vmem_limit_bytes=VMEM_LIMIT),
        cost_estimate=pl.CostEstimate(
            flops=6 * tokens * width * units,
            bytes_accessed=4 * width * units + 8 * tokens * width,
            transcendentals=0,
        ),
        name="feed_down",
    )(adjoint, scale, rectified, gated, up, down, *passed)
    return found[:1], *[found[1 + k * count : 1 + (k + 1) * count] for k in range(3)]


def per_device(
    layer_entries,
    incoming_adjoint,
    mixing_rescale_scalers,
    triple_projector_matrix,
    context_exit_matrix,
    dense_center_scaler,
    dense_center_offset,
    expand_matrix,
    shrink_matrix,
    span_chooser_initial,
    span_chooser_final,
    heat_divisor,
    sample_channel_fourths,
    element_preset_span,
    spot_group_table,
):
    block_len, seqs, width = layer_entries.shape
    tokens = block_len * seqs
    ring, plane = lax.axis_size("za"), lax.axis_size("yb")
    cores = lax.axis_size("bc")
    group = plane * lax.axis_size("bx") * cores
    devices = ring * group
    paired = plane == 2 and lax.axis_size("bx") == 2 and cores == 2
    za, yb = lax.axis_index("za"), lax.axis_index("yb")
    bx, bc = lax.axis_index("bx"), lax.axis_index("bc")
    rows = width // devices
    hidden_rows = FF // devices

    def home(array):
        return jnp.transpose(array, (1, 0, 2)).reshape(tokens, width)

    def back(array):
        return jnp.transpose(array.reshape(seqs, block_len, width), (1, 0, 2))

    entries, adjoint = home(layer_entries), home(incoming_adjoint)

    forced_home = jnp.transpose(element_preset_span, (1, 0)).reshape(tokens)
    forced_lanes = tokens // rows
    route_out_rows = span_chooser_final.shape[0]
    small_lanes = jnp.concatenate(
        [
            mixing_rescale_scalers[:, None],
            dense_center_scaler[:, None],
            dense_center_offset[:, None],
            jnp.pad(span_chooser_final, ((0, rows - route_out_rows), (0, 0))),
            forced_home.astype(bf16).reshape(rows, forced_lanes),
            jnp.zeros((rows, LANES - 7 - forced_lanes), bf16),
        ],
        axis=1,
    )
    qkv_cut = jnp.concatenate(
        [
            jnp.transpose(
                triple_projector_matrix.reshape(rows, 3, ring, GROUP_WIDTH),
                (2, 0, 1, 3),
            ).reshape(ring, rows, 3 * GROUP_WIDTH),
            jnp.broadcast_to(small_lanes, (ring, rows, LANES)),
            jnp.broadcast_to(span_chooser_initial, (ring, rows, RH)),
        ],
        axis=2,
    )
    units = ring * hidden_rows
    up_cut = jnp.transpose(
        expand_matrix.reshape(rows, ring, group, hidden_rows), (2, 0, 1, 3)
    ).reshape(group, rows, units)
    up_cut = lax.all_to_all(up_cut, PLANE, 0, 0, tiled=True).reshape(group * rows, units)
    qkv_cut = after(exchange(qkv_cut, "za"), up_cut)
    qkv_own = lax.all_gather(qkv_cut, PLANE, axis=1, tiled=False).reshape(width, 3 * GROUP_WIDTH + LANES + RH)
    small_lanes = qkv_own[:, 3 * GROUP_WIDTH : 3 * GROUP_WIDTH + LANES]
    route_in = qkv_own[:, 3 * GROUP_WIDTH + LANES :]
    gain_one, gain_two, bias_two = jnp.split(
        dot_cols(jnp.eye(8, LANES, dtype=bf16), small_lanes)[:3], 3, axis=0
    )
    by_device = small_lanes.reshape(devices, rows, LANES)
    route_out = by_device[:, :route_out_rows, 3:7].reshape(RH, 4)
    forced_all = by_device[:, :, 7 : 7 + forced_lanes].reshape(devices, tokens)
    out_own = lax.all_gather(context_exit_matrix, PLANE, axis=0, tiled=True)
    units = ring * hidden_rows
    entry_slots = ring_gather(entries, "za")
    up_own = lax.all_gather(
        after(up_cut, out_own, entry_slots[-1]), "za", axis=0, tiled=True
    )

    slot_ids = jnp.arange(ring, dtype=jnp.int32)
    table_ids = jnp.arange(spot_group_table.shape[0], dtype=jnp.int32)

    def places_of(piece):
        index = ((za - slot_ids) % ring) * plane + (yb - piece) % plane
        spots = jnp.sum(
            jnp.where(index[:, None] == table_ids[None, :], spot_group_table, 0), axis=1
        )
        return spots[:, None] * block_len + jnp.arange(block_len, dtype=jnp.int32)

    all_places = [places_of(piece) for piece in range(plane)]
    query_places = all_places[0].reshape(ring * block_len, 1)
    key_places = jnp.stack(all_places).reshape(plane, 1, ring * block_len)
    half = HD // 2
    inverse = theta_base ** (-(jnp.arange(half, dtype=f32) * (2.0 / HD)))
    angles = all_places[0].astype(f32)[:, :, None] * inverse
    cosine = jnp.concatenate([jnp.cos(angles), jnp.cos(angles)], axis=-1)
    sine = jnp.concatenate([-jnp.sin(angles), jnp.sin(angles)], axis=-1)
    active = (za < sample_channel_fourths).astype(f32)
    active_rows = jnp.broadcast_to(
        active[:, None, None], (seqs, block_len, 1)
    ).reshape(tokens, 1)

    if paired:
        spread = plane_gather
        at = jnp.stack(
            [
                (
                    (za * group + ((yb ^ y) * 2 + (bx ^ x)) * 2 + (bc ^ c)) * seqs + h
                ).astype(jnp.int32)
                for h, x, y, c in CHUNKS
            ]
        )
    else:
        spread = lambda block, between=None: [
            (lax.all_gather(block, PLANE, axis=0, tiled=True),)
        ]
        at = za * group * seqs + jnp.arange(group * seqs, dtype=jnp.int32)
    wide_adjoint = jnp.concatenate(sum(spread(adjoint), ()), axis=0)

    normed_slots, queries, boths = [], [], []
    for slot in range(ring):
        held = after(entry_slots[slot], entry_slots[min(slot + 2, ring - 1)])
        if slot > 0:
            held = after(held, boths[-1][0])
        held = held.astype(f32)
        inv_rms = lax.rsqrt(jnp.mean(held * held, axis=1, keepdims=True) + epsilon)
        normed_slots.append((held * inv_rms * gain_one).astype(bf16))
        joint = dot(normed_slots[slot], qkv_own)
        query, both = rope(
            joint.reshape(seqs, block_len, joint.shape[1]), cosine[slot], sine[slot]
        )
        queries.append(query)
        boths.append(ring_gather(both, "yb"))
    boths = [[slot[piece] for slot in boths] for piece in range(plane)]
    heads_out, attended, logs = attend(active, queries, boths, query_places, key_places)
    attended = after(attended, up_own).reshape(ring * tokens, GROUP_WIDTH)
    inputs = entries.astype(f32)
    hops = []
    parts = [
        lambda s=s: dot(attended[s * tokens : (s + 1) * tokens], out_own).astype(bf16)
        for s in range(ring)
    ]
    parts[0] = lambda: dot(after(attended[:tokens], wide_adjoint), out_own).astype(bf16)
    hidden = inputs + ring_scatter(parts, "za", hops)
    down_own = lax.all_gather(after(shrink_matrix, hops), "za", axis=0, tiled=True)

    centre = jnp.mean(hidden, axis=1, keepdims=True)
    centered = hidden - centre
    variance = jnp.mean(centered * centered, axis=1, keepdims=True)
    inv_std = lax.rsqrt(variance + epsilon)
    normal = centered * inv_std
    ffn_in = (normal * gain_two + bias_two).astype(bf16)

    picks = (at[:, None] == jnp.arange(devices * seqs)[None, :]).astype(bf16)
    wide_forced = dot(picks, forced_all.reshape(devices * seqs, block_len)).reshape(
        -1, 1
    )
    route_out_lanes = jnp.pad(route_out, ((0, 0), (0, LANES - 4)))

    def gather_back(groups, came=None):
        if paired:
            return plane_scatter(groups[0], came or plane_scatter_late(groups[1]))
        return lax.psum_scatter(
            groups[0][0], PLANE, scatter_dimension=0, tiled=True
        ).astype(f32)

    total = wide_adjoint.shape[0]
    kept, firsts, passed = [], [], ()

    def up_part(blocks):
        nonlocal passed
        firsts.append(sum(scale.shape[0] for scale, _ in kept))
        found = feed_up(
            blocks,
            heat_divisor,
            firsts[-1],
            total,
            wide_forced,
            route_in,
            route_out_lanes,
            up_own,
            passed,
        )
        passed = found[:2]
        kept.append(found[2:])
        return found[2]

    groups = spread(ffn_in, up_part)
    up_part(groups[-1])
    wide_in, gated = passed
    down_terms = dot_rows(gated, after(wide_adjoint, down_own)).astype(bf16)
    grad_down = lax.psum_scatter(down_terms, "za", scatter_dimension=0, tiled=True)
    late_adjoint = after(wide_adjoint, down_terms)
    count = len(groups)
    grad_bands, grad_ins, outs = [[None] * count for _ in range(3)]
    passed, came, band_came = (), None, None
    for turn in range(count)[::-1]:
        passed, grad_bands[turn], grad_ins[turn], outs[turn] = feed_down(
            late_adjoint,
            firsts[turn],
            len(groups[turn]),
            *kept[turn],
            gated,
            up_own,
            down_own,
            passed,
        )
        if paired and turn == 1:
            band_came = plane_scatter_late(grad_bands[1])
            came = plane_scatter_late(grad_ins[1])
            passed = after(passed, came[0], band_came)
    (grad_up,) = passed
    if paired:
        grad_ins[0] = after(grad_ins[0], came)
    grad_band_home = gather_back(grad_bands, band_came)
    grad_ffn_in = gather_back(grad_ins, came)

    temperature = heat_divisor[0]
    squashed = jnp.tanh(dot(ffn_in, route_in))
    routed = jax.nn.softmax(dot(squashed.astype(bf16), route_out) / temperature, axis=1)
    is_forced = (forced_home > 0)[:, None]
    grad_mix = jnp.cumsum(grad_band_home, axis=1)
    grad_logits = jnp.where(
        is_forced,
        0.0,
        routed
        * (grad_mix - jnp.sum(routed * grad_mix, axis=1, keepdims=True))
        / temperature,
    ).astype(bf16)
    grad_route_out = dot_rows(squashed.astype(bf16), grad_logits)
    grad_pre = (dot_cols(grad_logits, route_out) * (1.0 - squashed * squashed)).astype(
        bf16
    )
    grad_route_in = dot_rows(ffn_in, grad_pre)
    grad_ffn_in = grad_ffn_in + dot_cols(grad_pre, route_in)
    grad_gain_two = jnp.sum(grad_ffn_in * normal, axis=0)
    grad_bias_two = jnp.sum(grad_ffn_in, axis=0)
    grad_normal = grad_ffn_in * gain_two
    grad_hidden = adjoint.astype(f32) + inv_std * (
        grad_normal
        - jnp.mean(grad_normal, axis=1, keepdims=True)
        - normal * jnp.mean(grad_normal * normal, axis=1, keepdims=True)
    )
    small_terms = jnp.concatenate(
        [
            grad_route_in.reshape(devices, rows, RH),
            grad_gain_two.reshape(devices, rows, 1),
            grad_bias_two.reshape(devices, rows, 1),
            jnp.pad(
                grad_route_out.reshape(devices, route_out_rows, 4),
                ((0, 0), (0, rows - route_out_rows), (0, LANES - 6)),
            ),
        ],
        axis=2,
    ).astype(bf16)
    grad_low = after(grad_hidden.astype(bf16), grad_down)
    outs = after(outs, grad_low)
    came, steps = None, []
    if paired:
        came = plane_scatter_late(outs[1])
    out_sum = None
    if paired:
        early_outs = add_low(outs[0][0], swap(outs[0][1], "bc"))
        half_rows = early_outs.shape[0] // 2
        steps.append(add_low(early_outs[:half_rows], came[1]))
        steps.append(add_low(early_outs[half_rows:], came[2]))
    else:
        out_sum = gather_back(outs)
    grad_attn = [grad_low, onward(grad_low, "za")]
    up_terms = dot_rows(wide_in, after(grad_up, grad_low)).astype(bf16)
    grad_attn.append(onward(after(grad_attn[1], came, up_terms), "za"))
    grad_attn.append(onward(after(grad_attn[2], steps), "za"))
    up_terms = after(up_terms, grad_attn[3])
    up_terms = lax.psum_scatter(up_terms, "za", scatter_dimension=0, tiled=True)
    up_sums = up_terms
    up_terms = lax.all_to_all(
        up_terms.reshape(group, rows, units), PLANE, 0, 0, tiled=True
    )
    grad_wup = (
        jnp.transpose(up_terms.reshape(group, rows, ring, hidden_rows), (1, 2, 0, 3))
        .reshape(rows, FF)
        .astype(f32)
    )

    grad_heads = [
        (dot_cols(block, out_own) * active_rows)
        .astype(bf16)
        .reshape(seqs, block_len, GROUP_WIDTH)
        for block in grad_attn
    ]
    grad_queries, grad_keys, grad_values = [], [], []
    for name, chosen in (
        ("attend_back_far", range(1, plane)),
        ("attend_back", range(1)),
    ):
        if len(chosen) == 0:
            continue
        found = attend_back(
            queries,
            [boths[piece] for piece in chosen],
            grad_heads,
            heads_out,
            logs,
            query_places,
            key_places[jnp.array(chosen)],
            name,
        )
        if name == "attend_back_far":
            found, grad_heads = lax.optimization_barrier((found, grad_heads))
            steps, small_terms = after((steps, small_terms), found)

            def from_others(grads):
                running = grads[0]
                for term in grads[1:]:
                    running = add_low(term, onward(running, "yb"))
                return onward(running, "yb")

            grad_keys.append(from_others(found[1]))
            grad_values.append(from_others(found[2]))
        else:
            grad_keys.append(found[1][0])
            grad_values.append(found[2][0])
        grad_queries.append(found[0])
    if paired:
        half_rows = steps[0].shape[0] // 2
        out_sum = jnp.concatenate(
            [
                part[:half_rows].astype(f32) + swap(part[half_rows:], axis).astype(f32)
                for part, axis in zip(steps, ("bx", "yb"))
            ],
            axis=0,
        )
        small_terms = plane_reduce(
            small_terms.reshape(ring, plane, 2, cores, rows, RH + LANES)
        )
    else:
        small_terms = lax.psum_scatter(
            small_terms.reshape(ring, group, rows, RH + LANES),
            PLANE,
            scatter_dimension=1,
            tiled=False,
        )
    small_sum = sum(
        part.astype(f32)
        for part in rotate(
            lambda i: lax.dynamic_index_in_dim(small_terms, i, 0, keepdims=False), "za"
        )
    )
    result = back((hidden + out_sum).astype(bf16))
    joint = query_back(grad_queries, cosine, sine)
    attn_wide = jnp.concatenate(grad_attn, axis=0)
    normed_wide = jnp.concatenate(normed_slots, axis=0)

    def to_rows(terms, steps=None):
        cols = terms.shape[-1]
        if paired:
            terms = plane_reduce(
                terms.reshape(ring, plane, 2, cores, rows, cols), steps
            )
        else:
            terms = lax.psum_scatter(
                terms.reshape(ring, group, rows, cols),
                PLANE,
                scatter_dimension=1,
                tiled=False,
            )
        return exchange(terms, "za").astype(f32)

    flat_joint = lambda array: array.reshape(ring * tokens, 3 * GROUP_WIDTH)
    query_terms = dot_cols(
        flat_joint(after(joint, grad_keys, grad_values, result, small_sum))[:, :GROUP_WIDTH],
        qkv_own[:, :GROUP_WIDTH],
    )
    grad_out_terms = dot_rows(attended, attn_wide).astype(bf16)
    grad_wout = lax.psum_scatter(
        grad_out_terms, PLANE, scatter_dimension=0, tiled=True
    ).astype(f32)
    grad_keys = after(grad_keys, query_terms, grad_out_terms)
    joint = flat_joint(both_back(grad_keys, grad_values, cosine, sine, joint))
    both_own = qkv_own[:, GROUP_WIDTH : 3 * GROUP_WIDTH]
    low_terms = []
    for s in range(ring):
        at = slice(s * tokens, (s + 1) * tokens)
        terms = query_terms[at] + dot_cols(joint[at, GROUP_WIDTH:], both_own)
        low_terms.append(terms.astype(bf16))
    low_terms[1] = after(low_terms[1], up_sums)
    weight_terms = dot_rows(normed_wide, after(joint, low_terms[1])).astype(bf16)
    steps = []
    qkv_rows = to_rows(weight_terms, steps)
    low_terms[2] = after(low_terms[2], weight_terms)
    if steps:
        low_terms[2] = after(low_terms[2], steps[0])
        low_terms[3] = after(low_terms[3], steps[1], up_terms)
        low_terms[0] = after(low_terms[0], steps[2])
    grad_normed = ring_scatter([lambda s=s: low_terms[s] for s in range(ring)], "za")
    grad_wqkv = jnp.transpose(
        qkv_rows.reshape(ring, rows, 3, GROUP_WIDTH), (1, 2, 0, 3)
    ).reshape(rows, 3 * width)
    weight_rows = triple_projector_matrix.astype(f32)
    grad_gain_one = jnp.sum(grad_wqkv * weight_rows, axis=1) / (
        mixing_rescale_scalers.astype(f32)
    )
    inv_home = lax.rsqrt(jnp.mean(inputs * inputs, axis=1, keepdims=True) + epsilon)
    scaled = inputs * inv_home
    grad_scaled = grad_normed * gain_one
    grad_inputs = grad_hidden + inv_home * (
        grad_scaled - scaled * jnp.mean(grad_scaled * scaled, axis=1, keepdims=True)
    )
    grad_tokens = back(grad_inputs.astype(bf16))
    return (
        result,
        grad_tokens,
        grad_gain_one,
        grad_wqkv,
        grad_wout,
        small_sum[:, RH],
        small_sum[:, RH + 1],
        grad_wup,
        grad_down.astype(f32),
        small_sum[:, :RH],
        small_sum[:route_out_rows, RH + 2 : RH + 6],
    )


def solution(mesh):
    seq, batch = mesh.shape["seq"], mesh.shape["batch"]
    inner = Mesh(
        mesh.devices.reshape(RING, seq // RING, batch // 2, 2),
        ("za", "yb", "bx", "bc"),
    )
    along, across = ("za", "yb"), ("bx", "bc")
    tokens = P(along, across, None)
    vector = P(along + across)
    matrix = P(along + across, None)
    return jax.shard_map(
        per_device,
        mesh=inner,
        in_specs=(
            tokens,
            tokens,
            vector,
            matrix,
            matrix,
            vector,
            vector,
            matrix,
            matrix,
            matrix,
            matrix,
            P(),
            P(across),
            P(along, across),
            P(),
        ),
        out_specs=(
            tokens,
            tokens,
            vector,
            matrix,
            matrix,
            vector,
            vector,
            matrix,
            matrix,
            matrix,
            matrix,
        ),
        check_vma=False,
    )
```

time: 1020 us -> 885 us (0.87)
  waiting for transfers between devices: 529 us -> 372 us
  Pallas kernels: 50 us -> 118 us
  matrix products: 144 us -> 105 us
  blocking collectives: 27.2 us -> 0 us
  starting transfers between devices: 65.5 us -> 86.5 us
    ppermute x16 -> x18, waiting for transfers between devices: 398 us -> 203 us  [onward(): return lax.ppermute(block, axis, [(i, (i + 1) % size) for i in range(size)])]
    pallas_call x4 -> x13, Pallas kernels: 50 us -> 118 us  [the longest x2 43.4 us: feed_down(): pl.pallas_call(functools.partial(feed_down_kernel, count, steps, len(pass...]
    ppermute x0 -> x9, waiting for transfers between devices: none -> 48.6 us  [rotate(): came.append(lax.ppermute(pieces((me + far) % size), axis, route))]
    ppermute x27 -> x40, waiting for transfers between devices: 71 us -> 107 us  [swap(): return lax.ppermute(block, axis, SWAP)]
    dot_general x11, matrix products: 56 us -> 22.2 us  [dot(): lax.dot_general(left_mat, right_mat, (((1,), (0,)), ((), ())), preferred_...]
    reduce_scatter x1, waiting for transfers between devices: 31.1 us -> 0.01 us  [per_device(): lax.psum_scatter(grad_out_terms, PLANE, scatter_dimension=0, tiled=True)]
    reduce_scatter x2 -> x0, waiting for transfers between devices: 28.3 us -> none  [the longest x1 28.3 us: per_device(): lax.psum_scatter(qkv_terms.reshape(ring, group, rows, wide_cols), PLANE,...]
    all_to_all x1 -> x0, blocking collectives: 27.2 us -> none  [per_device(): qkv_cut = lax.all_to_all(qkv_cut, 'za', 0, 0, tiled=True)]
  transfers between devices with their start and end apart: 56 -> 76, of which waited for: 29 -> 41; matrix products, arithmetic and copies ran while one was open for 26% -> 26% of each run, Pallas kernels for 5% -> 11%
where the time goes in v2:
time: 885 us; the launch traced here: 876 us
  waiting for transfers between devices  372 us (42%)
  Pallas kernels  118 us (13%)
  matrix products  105 us (12%)
  local copies, waits for them, and re-layouts  97.4 us (11%)
  starting transfers between devices  86.5 us (10%)
  other arithmetic  79 us (9%)
  between operations  17.4 us (2%)
    ppermute x18, waiting for transfers between devices, onward(): return lax.ppermute(block, axis, [(i, (i + 1) % size) for i in range(size)])  203 us
    ppermute x40, waiting for transfers between devices, swap(): return lax.ppermute(block, axis, SWAP)  107 us
    ppermute x9, waiting for transfers between devices, rotate(): came.append(lax.ppermute(pieces((me + far) % size), axis, route))  48.6 us
    dot_general x6, matrix products, dot_rows(): lax.dot_general(left_mat, right_mat, (((0,), (0,)), ((), ())), preferred_...  44.6 us
    pallas_call x2, Pallas kernels, feed_down(): pl.pallas_call(functools.partial(feed_down_kernel, count, steps, len(pass...  43.4 us
    ppermute x40, starting transfers between devices, swap(): return lax.ppermute(block, axis, SWAP)  41.2 us
    dot_general x12, matrix products, dot_cols(): lax.dot_general(left_mat, right_mat, (((1,), (1,)), ((), ())), preferred_...  38.5 us
    unnamed x261, local copies, waits for them, and re-layouts  37 us
  transfers between devices with their start and end apart: 76, of which 41 were waited for; matrix products, arithmetic and copies ran while one was open for 26% of the time, Pallas kernels for 11%

profile of v2, /device:TPU:0, one launch (start us, length us, event | category | flops | bytes accessed | tf_op | source)
XLA Modules:
  0.0 875.7 jit_solution(6181012291142614018)
XLA Ops:
  29.0 14.2 %collective-permute-done.3 = bf16[1,64,1920]{2,1,0:T(8,128)(2,1)} collective-permute-done((bf16[1,64,1920]{2,1,0:T(8,128)(2,1)}, bf16[1,64,1920]{2,1,0:T(8,128)(2,1)}, u32[]{:S(2)}, u32[]{:S(2)}) %collective-permute-start.3) | collective-permute-done | bytes 245792 | tf_op jit(solution)/shard_map/ppermute | solution.py:102
  57.6 16.9 %collective-permute-done = bf16[256,2048]{1,0:T(8,128)(2,1)S(1)} collective-permute-done((bf16[256,2048]{1,0:T(8,128)(2,1)S(1)}, bf16[256,2048]{1,0:T(8,128)(2,1)S(1)}, u32[]{:S(2)}, u32[]{:S(2)}) %collective-permute-start) | collective-permute-done | bytes 1048608 | tf_op jit(solution)/shard_map/ppermute | solution.py:54
  78.1 19.8 %collective-permute-done.1 = bf16[256,2048]{1,0:T(8,128)(2,1)S(1)} collective-permute-done((bf16[256,2048]{1,0:T(8,128)(2,1)S(1)}, bf16[256,2048]{1,0:T(8,128)(2,1)S(1)}, u32[]{:S(2)}, u32[]{:S(2)}) %collective-permute-start.1) | collective-permute-done | bytes 1048608 | tf_op jit(solution)/shard_map/ppermute | solution.py:54
  99.2 21.3 %collective-permute-done.5 = bf16[256,2048]{1,0:T(8,128)(2,1)} collective-permute-done((bf16[256,2048]{1,0:T(8,128)(2,1)S(1)}, bf16[256,2048]{1,0:T(8,128)(2,1)}, u32[]{:S(2)}, u32[]{:S(2)}) %collective-permute-start.5) | collective-permute-done | bytes 1048608 | tf_op jit(solution)/shard_map/ppermute | solution.py:54
  152.5 7.6 collective-permute-start.14
  168.7 11.2 %collective-permute-done.9.refs_12_.refs_20_.refs_7_.refs_11_ = bf16[2,128,1024]{2,1,0:T(8,128)(2,1)} collective-permute-done((bf16[2,128,1024]{2,1,0:T(8,128)(2,1)S(1)}, bf16[2,128,1024]{2,1,0:T(8,128)(2,1)}, u32[]{:S(2)}, u32[]{:S(2)}) %collective-permute-start.9) | collective-permute-done | bytes 524320 | tf_op jit(solution)/shard_map/ppermute | solution.py:54
  179.9 15.8 %attend.1 = (f32[4,2,128,512]{3,2,1,0:T(8,128)}, bf16[4,2,128,512]{3,2,1,0:T(8,128)(2,1)}, f32[2,4,512,1]{3,2,1,0:T(8,128)}) custom-call(f32[2]{0:T(128)S(1)} %compare_convert_fusion.refs_0_, bf16[2,128,512]{2,1,0:T(8,128)(2,1)S(1)} %copy-done.3, bf16[2,128,512]{2,1,0:T(8,128)(2,1)S(1)} %copy-done.7, bf16[2,128,512]{2,1,0:T(8,128)(2,1)S(1)} %copy-done.11, ...), custom_call_target="tpu_custom_call" | custom-call | tf_op jit(solution)/shard_map/attend/pallas_call | solution.py:326
  195.7 10.2 %all-gather.8.cloned.1.call-done.refs_6_.refs_4_ = bf16[2048,1024]{1,0:T(8,128)(2,1)} async-done(((bf16[512,1024]{1,0:T(8,128)(2,1)}), bf16[2048,1024]{1,0:T(8,128)(2,1)}) %all-gather.8.cloned.1.call-update) | async-done | bytes 4194320 | tf_op jit(solution)/shard_map/all_gather | solution.py:671
  213.4 22.5 %collective-permute-done.16 = bf16[256,2048]{1,0:T(8,128)(2,1)S(1)} collective-permute-done((bf16[256,2048]{1,0:T(8,128)(2,1)S(1)}, bf16[256,2048]{1,0:T(8,128)(2,1)S(1)}, u32[]{:S(2)}, u32[]{:S(2)}) %collective-permute-start.16) | collective-permute-done | bytes 1048608 | tf_op jit(solution)/shard_map/ppermute | solution.py:54
  238.4 24.2 %collective-permute-done.17 = bf16[256,2048]{1,0:T(8,128)(2,1)S(1)} collective-permute-done((bf16[256,2048]{1,0:T(8,128)(2,1)S(1)}, bf16[256,2048]{1,0:T(8,128)(2,1)S(1)}, u32[]{:S(2)}, u32[]{:S(2)}) %collective-permute-start.17) | collective-permute-done | bytes 1048608 | tf_op jit(solution)/shard_map/ppermute | solution.py:54
  269.5 28.6 %collective-permute-done.18 = bf16[256,2048]{1,0:T(8,128)(2,1)} collective-permute-done((bf16[256,2048]{1,0:T(8,128)(2,1)}, bf16[256,2048]{1,0:T(8,128)(2,1)}, u32[]{:S(2)}, u32[]{:S(2)}) %collective-permute-start.18) | collective-permute-done | bytes 1048608 | tf_op jit(solution)/shard_map/ppermute | solution.py:54
  306.4 6.4 collective-permute-done.19
  328.7 14.1 %collective-permute-done.20 = bf16[256,2048]{1,0:T(8,128)(2,1)} collective-permute-done((bf16[256,2048]{1,0:T(8,128)(2,1)}, bf16[256,2048]{1,0:T(8,128)(2,1)}, u32[]{:S(2)}, u32[]{:S(2)}) %collective-permute-start.20) | collective-permute-done | bytes 1048608 | tf_op jit(solution)/shard_map/ppermute | solution.py:118
  346.8 11.5 %feed_up.2 = (bf16[2048,2048]{1,0:T(8,128)(2,1)}, bf16[2048,1024]{1,0:T(8,128)(2,1)}, f32[1024,4]{1,0:T(8,128)S(1)}, f32[1024,1024]{1,0:T(8,128)}) custom-call(bf16[512,2048]{1,0:T(8,128)(2,1)} %pad_maximum_fusion.3.refs_0_, bf16[512,2048]{1,0:T(8,128)(2,1)} %collective-permute-done.23.refs_1_, f32[1]{0:T(128)} %copy.255.refs_2_, f32[2048,1]{1,0:T(8,128)S(1)} %copy-done.1, ...), custom_call_target="tpu_custom_call" | custom-call | flops 4294967296 | bytes 16777216 | tf_op jit(solution)/shard_map/feed_up/pallas_call | solution.py:520
  364.6 11.0 %feed_up.3 = (bf16[2048,2048]{1,0:T(8,128)(2,1)}, bf16[2048,1024]{1,0:T(8,128)(2,1)}, f32[1024,4]{1,0:T(8,128)S(1)}, f32[1024,1024]{1,0:T(8,128)}) custom-call(bf16[512,2048]{1,0:T(8,128)(2,1)S(1)} %pad_maximum_fusion.2.refs_0_, bf16[512,2048]{1,0:T(8,128)(2,1)} %copy-done.82, f32[1]{0:T(128)} %copy.255.refs_2_, ...), custom_call_target="tpu_custom_call", output_to_operand_aliasing={{0}: (7, {}), {1}: (8, {})} | custom-call | flops 4294967296 | bytes 16777216 | tf_op jit(solution)/shard_map/feed_up/pallas_call | solution.py:520
  376.4 14.1 %convolution_convert_fusion.1 = bf16[1024,2048]{1,0:T(8,128)(2,1)} fusion(bf16[2048,1024]{1,0:T(8,128)(2,1)} %get-tuple-element.120.refs_3_, bf16[2048,2048]{1,0:T(8,128)(2,1)} %copy-done.98), kind=kOutput, calls=%fused_computation.22 | convolution fusion | flops 8592031744 | bytes 16777216 | tf_op jit(solution)/shard_map/dot_general | solution.py:41
  391.5 21.8 %feed_down.2 = (bf16[2048,1024]{1,0:T(8,128)(2,1)}, f32[512,4]{1,0:T(8,128)S(1)}, f32[512,4]{1,0:T(8,128)}, bf16[512,2048]{1,0:T(8,128)(2,1)S(1)}, bf16[512,2048...) custom-call(bf16[2048,2048]{1,0:T(8,128)(2,1)} %copy-done.98, f32[1024,4]{1,0:T(8,128)S(1)} %copy-done.34, ...), custom_call_target="tpu_custom_call" | custom-call | flops 12884901888 | bytes 25165824 | tf_op jit(solution)/shard_map/feed_down/pallas_call | solution.py:559
  429.7 21.6 %feed_down.3 = (bf16[2048,1024]{1,0:T(8,128)(2,1)}, f32[512,4]{1,0:T(8,128)S(1)}, f32[512,4]{1,0:T(8,128)S(1)}, bf16[512,2048]{1,0:T(8,128)(2,1)S(1)}, bf16[512,...) custom-call(bf16[2048,2048]{1,0:T(8,128)(2,1)} %copy-done.98, ...), custom_call_target="tpu_custom_call", output_to_operand_aliasing={{0}: (6, {})} | custom-call | flops 12884901888 | bytes 25165824 | tf_op jit(solution)/shard_map/feed_down/pallas_call | solution.py:559
  473.2 6.2 collective-permute-done.33
  500.4 12.8 %convolution_convert_fusion.2 = bf16[2048,1024]{1,0:T(8,128)(2,1)} fusion(bf16[2048,2048]{1,0:T(8,128)(2,1)} %get-tuple-element.148, bf16[2048,1024]{1,0:T(8,128)(2,1)S(1)} %copy-done.113), kind=kOutput, calls=%fused_computation.23 | convolution fusion | flops 8592031744 | bytes 16777216 | tf_op jit(solution)/shard_map/dot_general | solution.py:41
  532.3 17.9 %collective-permute-done.42 = bf16[256,2048]{1,0:T(8,128)(2,1)S(1)} collective-permute-done((bf16[256,2048]{1,0:T(8,128)(2,1)}, bf16[256,2048]{1,0:T(8,128)(2,1)S(1)}, u32[]{:S(2)}, u32[]{:S(2)}) %collective-permute-start.42) | collective-permute-done | bytes 1048608 | tf_op jit(solution)/shard_map/ppermute | solution.py:54
  551.3 25.0 %collective-permute-done.43 = bf16[256,2048]{1,0:T(8,128)(2,1)} collective-permute-done((bf16[256,2048]{1,0:T(8,128)(2,1)S(1)}, bf16[256,2048]{1,0:T(8,128)(2,1)}, u32[]{:S(2)}, u32[]{:S(2)}) %collective-permute-start.43) | collective-permute-done | bytes 1048608 | tf_op jit(solution)/shard_map/ppermute | solution.py:54
  596.6 12.7 %attend_back_far.1 = (f32[4,2,128,512]{3,2,1,0:T(8,128)}, bf16[4,2,128,512]{3,2,1,0:T(8,128)(2,1)}, bf16[4,2,128,512]{3,2,1,0:T(8,128)(2,1)}) custom-call(bf16[2,128,512]{2,1,0:T(8,128)(2,1)S(1)} %copy-done.4, bf16[2,128,512]{2,1,0:T(8,128)(2,1)S(1)} %copy-done.8, bf16[2,128,512]{2,1,0:T(8,128)(2,1)S(1)} %copy-done.12, bf16[2,128,512]{2,1,0:T(8,128)(2,1)S(1)} %copy-done.16, ...), custom_call_target="tpu_custom_call" | custom-call | tf_op jit(solution)/shard_map/attend_back_far/pallas_call | solution.py:399
  625.6 12.6 %attend_back.1 = (f32[4,2,128,512]{3,2,1,0:T(8,128)}, bf16[4,2,128,512]{3,2,1,0:T(8,128)(2,1)S(1)}, bf16[4,2,128,512]{3,2,1,0:T(8,128)(2,1)}) custom-call(bf16[2,128,512]{2,1,0:T(8,128)(2,1)S(1)} %copy-done.5, bf16[2,128,512]{2,1,0:T(8,128)(2,1)S(1)} %copy-done.9, bf16[2,128,512]{2,1,0:T(8,128)(2,1)S(1)} %copy-done.13, bf16[2,128,512]{2,1,0:T(8,128)(2,1)S(1)} %copy-done.17, ...), custom_call_target="tpu_custom_call" | custom-call | tf_op jit(solution)/shard_map/attend_back/pallas_call | solution.py:399
  641.9 23.8 %collective-permute-done.45 = bf16[128,2048]{1,0:T(8,128)(2,1)} collective-permute-done((bf16[128,2048]{1,0:T(8,128)(2,1)}, bf16[128,2048]{1,0:T(8,128)(2,1)}, u32[]{:S(2)}, u32[]{:S(2)}) %collective-permute-start.45) | collective-permute-done | bytes 524320 | tf_op jit(solution)/shard_map/ppermute | solution.py:118
  689.1 7.8 fusion.75
  696.9 6.7 both_back.1
  709.0 8.5 convolution_convert_fusion
  752.9 6.1 collective-permute-done.61
  762.0 9.9 %collective-permute-done.57 = bf16[4,2,64,768]{3,2,0,1:T(8,128)(2,1)} collective-permute-done((bf16[4,2,64,768]{3,2,0,1:T(8,128)(2,1)}, bf16[4,2,64,768]{3,2,0,1:T(8,128)(2,1)}, u32[]{:S(2)}, u32[]{:S(2)}) %collective-permute-start.57) | collective-permute-done | bytes 786464 | tf_op jit(solution)/shard_map/ppermute | solution.py:118
  775.4 11.4 %collective-permute-done.59 = bf16[4,2,64,768]{3,2,0,1:T(8,128)(2,1)S(1)} collective-permute-done((bf16[4,2,64,768]{3,2,0,1:T(8,128)(2,1)S(1)}, bf16[4,2,64,768]{3,2,0,1:T(8,128)(2,1)S(1)}, u32[]{:S(2)}, u32[]{:S(2)}) %collective-permute-start.59) | collective-permute-done | bytes 786464 | tf_op jit(solution)/shard_map/ppermute | solution.py:118
  817.3 34.2 %collective-permute-done.65 = bf16[1,64,1536]{2,1,0:T(8,128)(2,1)S(1)} collective-permute-done((bf16[1,64,1536]{2,1,0:T(8,128)(2,1)S(1)}, bf16[1,64,1536]{2,1,0:T(8,128)(2,1)S(1)}, u32[]{:S(2)}, u32[]{:S(2)}) %collective-permute-start.65) | collective-permute-done | bytes 196640 | tf_op jit(solution)/shard_map/ppermute | solution.py:102
  (596 shorter events, 369.9 us)
Async XLA Ops:
  7.2 113.3 %all-gather.6.cloned.1.call-start = ((), (), s32[]{:S(2)}) async-start(), calls=%async_computation.5 | async-start | bytes 2359296 | tf_op jit(solution)/shard_map/all_gather | solution.py:668
  28.9 91.7 %all-gather.12.cloned.1.call-start = ((), (), s32[]{:S(2)}) async-start(), calls=%async_computation.11 | async-start | bytes 8847360 | tf_op jit(solution)/shard_map/all_gather | solution.py:659
  49.9 156.0 %all-gather.8.cloned.1.call-start = ((), (), s32[]{:S(2)}) async-start(), calls=%async_computation.6 | async-start | bytes 5242880 | tf_op jit(solution)/shard_map/all_gather | solution.py:671
  56.4 92.9 %collective-permute-start.11 = (bf16[128,2048]{1,0:T(8,128)(2,1)}, bf16[128,2048]{1,0:T(8,128)(2,1)}, u32[]{:S(2)}, u32[]{:S(2)}) collective-permute-start(bf16[128,2048]{1,0:T(8,128)(2,1)} %get-tuple-element.310), channel_id=1, source_target_pairs={{0,4},{4,0},{1,5},{5,1},{2,6},{6,2},{3,7},{7,3},{8,12},{12,8},{9,1... | collective-permute-start | bytes 1572872 | tf_op jit(solution)/shard_map/ppermute | solution.py:118
  57.0 95.4 %collective-permute-start.10 = (bf16[128,2048]{1,0:T(8,128)(2,1)}, bf16[128,2048]{1,0:T(8,128)(2,1)}, u32[]{:S(2)}, u32[]{:S(2)}) collective-permute-start(bf16[128,2048]{1,0:T(8,128)(2,1)} %get-tuple-element.311), channel_id=1, source_target_pairs={{0,2},{2,0},{1,3},{3,1},{4,6},{6,4},{5,7},{7,5},{8,10},{10,8},{9,1... | collective-permute-start | bytes 1572872 | tf_op jit(solution)/shard_map/ppermute | solution.py:118
  120.5 255.9 %all-gather.10.cloned.1.call-start = ((), (), s32[]{:S(2)}) async-start(), calls=%async_computation.7 | async-start | bytes 5242880 | tf_op jit(solution)/shard_map/all_gather | solution.py:740
  129.9 32.5 %collective-permute-start.6 = (bf16[2,128,1024]{2,1,0:T(8,128)(2,1)S(1)}, bf16[2,128,1024]{2,1,0:T(8,128)(2,1)S(1)}, u32[]{:S(2)}, u32[]{:S(2)}) collective-permute-start(bf16[2,128,1024]{2,1,0:T(8,128)(2,1)S(1)} %get-tuple-element.100.refs_5_.refs_13_.refs_4_.refs_8_), channel_id=1, source_target_pairs={{0,4},{4,0},{1,5},{5,1},{2,6},{6,2},{3,7},{7,3},{8,12},{12,8},{9,1... | collective-permute-start | bytes 1572872 | tf_op jit(solution)/shard_map/ppermute | solution.py:54
  149.3 30.6 %collective-permute-start.9 = (bf16[2,128,1024]{2,1,0:T(8,128)(2,1)S(1)}, bf16[2,128,1024]{2,1,0:T(8,128)(2,1)}, u32[]{:S(2)}, u32[]{:S(2)}) collective-permute-start(bf16[2,128,1024]{2,1,0:T(8,128)(2,1)S(1)} %get-tuple-element.111.refs_8_.refs_16_.refs_7_.refs_11_), channel_id=1, source_target_pairs={{0,4},{4,0},{1,5},{5,1},{2,6},{6,2},{3,7},{7,3},{8,12},{12,8},{9,1... | collective-permute-start | bytes 1572872 | tf_op jit(solution)/shard_map/ppermute | solution.py:54
  152.5 58.6 %collective-permute-start.14 = (bf16[256,2048]{1,0:T(8,128)(2,1)}, bf16[256,2048]{1,0:T(8,128)(2,1)}, u32[]{:S(2)}, u32[]{:S(2)}) collective-permute-start(bf16[256,2048]{1,0:T(8,128)(2,1)} %pad_maximum_fusion.5), channel_id=1, source_target_pairs={{0,2},{2,0},{1,3},{3,1},{4,6},{6,4},{5,7},{7,5},{8,10},{10,8},{9,1... | collective-permute-start | bytes 3145736 | tf_op jit(solution)/shard_map/ppermute | solution.py:118
  162.4 48.7 %collective-permute-start.13 = (bf16[256,2048]{1,0:T(8,128)(2,1)}, bf16[256,2048]{1,0:T(8,128)(2,1)}, u32[]{:S(2)}, u32[]{:S(2)}) collective-permute-start(bf16[256,2048]{1,0:T(8,128)(2,1)} %pad_maximum_fusion.4), channel_id=1, source_target_pairs={{0,4},{4,0},{1,5},{5,1},{2,6},{6,2},{3,7},{7,3},{8,12},{12,8},{9,1... | collective-permute-start | bytes 3145736 | tf_op jit(solution)/shard_map/ppermute | solution.py:118
  211.0 54.3 %collective-permute-start.12 = (bf16[512,2048]{1,0:T(8,128)(2,1)S(1)}, bf16[512,2048]{1,0:T(8,128)(2,1)S(1)}, u32[]{:S(2)}, u32[]{:S(2)}) collective-permute-start(bf16[512,2048]{1,0:T(8,128)(2,1)S(1)} %pad_maximum_fusion), channel_id=1, source_target_pairs={{0,1},{1,0},{2,3},{3,2},{4,5},{5,4},{6,7},{7,6},{8,9},{9,8},{10,11... | collective-permute-start | bytes 6291464 | tf_op jit(solution)/shard_map/ppermute | solution.py:118
  212.9 53.0 %collective-permute-start.15 = (bf16[512,2048]{1,0:T(8,128)(2,1)S(1)}, bf16[512,2048]{1,0:T(8,128)(2,1)S(1)}, u32[]{:S(2)}, u32[]{:S(2)}) collective-permute-start(bf16[512,2048]{1,0:T(8,128)(2,1)S(1)} %pad_maximum_fusion.1), channel_id=1, source_target_pairs={{0,1},{1,0},{2,3},{3,2},{4,5},{5,4},{6,7},{7,6},{8,9},{9,8},{10,11... | collective-permute-start | bytes 6291464 | tf_op jit(solution)/shard_map/ppermute | solution.py:118
  264.3 33.8 %collective-permute-start.18 = (bf16[256,2048]{1,0:T(8,128)(2,1)}, bf16[256,2048]{1,0:T(8,128)(2,1)}, u32[]{:S(2)}, u32[]{:S(2)}) collective-permute-start(bf16[256,2048]{1,0:T(8,128)(2,1)} %add_convert_fusion.11), channel_id=1, source_target_pairs={{0,8},{8,16},{16,24},{24,0},{1,9},{9,17},{17,25},{25,1},{2,10},{10... | collective-permute-start | bytes 3145736 | tf_op jit(solution)/shard_map/ppermute | solution.py:54
  269.4 219.8 %reduce-scatter.4.cloned.1.call-start = ((), (), s32[]{:S(2)}) async-start(), calls=%async_computation.8 | async-start | bytes 5242880 | tf_op jit(solution)/shard_map/reduce_scatter | solution.py:787
  315.9 30.9 %collective-permute-start.23 = (bf16[512,2048]{1,0:T(8,128)(2,1)}, bf16[512,2048]{1,0:T(8,128)(2,1)}, u32[]{:S(2)}, u32[]{:S(2)}) collective-permute-start(bf16[512,2048]{1,0:T(8,128)(2,1)} %pad_maximum_fusion.3.refs_0_), channel_id=1, source_target_pairs={{0,1},{1,0},{2,3},{3,2},{4,5},{5,4},{6,7},{7,6},{8,9},{9,8},{10,11... | collective-permute-start | bytes 6291464 | tf_op jit(solution)/shard_map/ppermute | solution.py:118
  415.9 293.1 %reduce-scatter.6.cloned.1.call-start = ((), (), s32[]{:S(2)}) async-start(), calls=%async_computation.9 | async-start | bytes 5242880 | tf_op jit(solution)/shard_map/reduce_scatter | solution.py:869
  489.3 28.1 %collective-permute-start.41 = (bf16[256,2048]{1,0:T(8,128)(2,1)}, bf16[256,2048]{1,0:T(8,128)(2,1)}, u32[]{:S(2)}, u32[]{:S(2)}) collective-permute-start(bf16[256,2048]{1,0:T(8,128)(2,1)} %get-tuple-element.143), channel_id=1, source_target_pairs={{0,8},{8,16},{16,24},{24,0},{1,9},{9,17},{17,25},{25,1},{2,10},{10... | collective-permute-start | bytes 3145736 | tf_op jit(solution)/shard_map/ppermute | solution.py:54
  491.2 34.5 %collective-permute-start.37 = (bf16[512,2048]{1,0:T(8,128)(2,1)}, bf16[512,2048]{1,0:T(8,128)(2,1)}, u32[]{:S(2)}, u32[]{:S(2)}) collective-permute-start(bf16[512,2048]{1,0:T(8,128)(2,1)} %get-tuple-element.145), channel_id=1, source_target_pairs={{0,1},{1,0},{2,3},{3,2},{4,5},{5,4},{6,7},{7,6},{8,9},{9,8},{10,11... | collective-permute-start | bytes 6291464 | tf_op jit(solution)/shard_map/ppermute | solution.py:118
  576.3 220.4 %reduce-scatter.8.cloned.1.call-start = ((), (), s32[]{:S(2)}) async-start(), calls=%async_computation.10 | async-start | bytes 2359296 | tf_op jit(solution)/shard_map/reduce_scatter | solution.py:970
  609.3 79.8 %collective-permute-start.46 = (bf16[4,2,128,512]{3,2,1,0:T(8,128)(2,1)}, bf16[4,2,128,512]{3,2,1,0:T(8,128)(2,1)}, u32[]{:S(2)}, u32[]{:S(2)}) collective-permute-start(bf16[4,2,128,512]{3,2,1,0:T(8,128)(2,1)} %get-tuple-element.159), channel_id=1, source_target_pairs={{0,4},{4,0},{1,5},{5,1},{2,6},{6,2},{3,7},{7,3},{8,12},{12,8},{9,1... | collective-permute-start | bytes 3145736 | tf_op jit(solution)/shard_map/ppermute | solution.py:54
  610.9 78.2 %collective-permute-start.47 = (bf16[4,2,128,512]{3,2,1,0:T(8,128)(2,1)}, bf16[4,2,128,512]{3,2,1,0:T(8,128)(2,1)}, u32[]{:S(2)}, u32[]{:S(2)}) collective-permute-start(bf16[4,2,128,512]{3,2,1,0:T(8,128)(2,1)} %get-tuple-element.160), channel_id=1, source_target_pairs={{0,4},{4,0},{1,5},{5,1},{2,6},{6,2},{3,7},{7,3},{8,12},{12,8},{9,1... | collective-permute-start | bytes 3145736 | tf_op jit(solution)/shard_map/ppermute | solution.py:54
  613.2 52.4 %collective-permute-start.45 = (bf16[128,2048]{1,0:T(8,128)(2,1)}, bf16[128,2048]{1,0:T(8,128)(2,1)}, u32[]{:S(2)}, u32[]{:S(2)}) collective-permute-start(bf16[128,2048]{1,0:T(8,128)(2,1)} %slice.268), channel_id=1, source_target_pairs={{0,4},{4,0},{1,5},{5,1},{2,6},{6,2},{3,7},{7,3},{8,12},{12,8},{9,1... | collective-permute-start | bytes 1572872 | tf_op jit(solution)/shard_map/ppermute | solution.py:118
  614.7 54.6 %collective-permute-start.44 = (bf16[128,2048]{1,0:T(8,128)(2,1)}, bf16[128,2048]{1,0:T(8,128)(2,1)}, u32[]{:S(2)}, u32[]{:S(2)}) collective-permute-start(bf16[128,2048]{1,0:T(8,128)(2,1)} %slice.266), channel_id=1, source_target_pairs={{0,2},{2,0},{1,3},{3,1},{4,6},{6,4},{5,7},{7,5},{8,10},{10,8},{9,1... | collective-permute-start | bytes 1572872 | tf_op jit(solution)/shard_map/ppermute | solution.py:118
  616.3 50.5 %collective-permute-start.48 = (bf16[4,2,2,64,384]{4,3,2,1,0:T(8,128)(2,1)}, bf16[4,2,2,64,384]{4,3,2,1,0:T(8,128)(2,1)}, u32[]{:S(2)}, u32[]{:S(2)}) collective-permute-start(bf16[4,2,2,64,384]{4,3,2,1,0:T(8,128)(2,1)} %dynamic-slice_bitcast_fusion.2), channel_id=1, source_target_pairs={{0,1},{1,0},{2,3},{3,2},{4,5},{5,4},{6,7},{7,6},{8,9},{9,8},{10,11... | collective-permute-start | bytes 2359304 | tf_op jit(solution)/shard_map/ppermute | solution.py:118
  740.0 31.9 %collective-permute-start.57 = (bf16[4,2,64,768]{3,2,0,1:T(8,128)(2,1)}, bf16[4,2,64,768]{3,2,0,1:T(8,128)(2,1)}, u32[]{:S(2)}, u32[]{:S(2)}) collective-permute-start(bf16[4,2,64,768]{3,2,0,1:T(8,128)(2,1)} %dynamic-slice_bitcast_fusion.1), channel_id=1, source_target_pairs={{0,4},{4,0},{1,5},{5,1},{2,6},{6,2},{3,7},{7,3},{8,12},{12,8},{9,1... | collective-permute-start | bytes 2359304 | tf_op jit(solution)/shard_map/ppermute | solution.py:118
  745.3 53.2 %all-to-all-start.1 = ((bf16[8,64,1024]{2,1,0:T(8,128)(2,1)}), bf16[8,64,1024]{2,1,0:T(8,128)(2,1)}, u32[]{:S(2)}, u32[]{:S(2)}) async-start(bf16[8,64,1024]{2,1,0:T(8,128)(2,1)} %bitcast.270), calls=%async_computation.3 | async-start | bytes 2097152 | tf_op jit(solution)/shard_map/all_to_all | solution.py:871
  750.9 35.9 %collective-permute-start.59 = (bf16[4,2,64,768]{3,2,0,1:T(8,128)(2,1)S(1)}, bf16[4,2,64,768]{3,2,0,1:T(8,128)(2,1)S(1)}, u32[]{:S(2)}, u32[]{:S(2)}) collective-permute-start(bf16[4,2,64,768]{3,2,0,1:T(8,128)(2,1)S(1)} %dynamic-slice_bitcast_fusion), channel_id=1, source_target_pairs={{0,2},{2,0},{1,3},{3,1},{4,6},{6,4},{5,7},{7,5},{8,10},{10,8},{9,1... | collective-permute-start | bytes 2359304 | tf_op jit(solution)/shard_map/ppermute | solution.py:118
  761.6 48.4 %collective-permute-start.62 = (bf16[256,2048]{1,0:T(8,128)(2,1)}, bf16[256,2048]{1,0:T(8,128)(2,1)}, u32[]{:S(2)}, u32[]{:S(2)}) collective-permute-start(bf16[256,2048]{1,0:T(8,128)(2,1)} %add_convert_fusion.5), channel_id=1, source_target_pairs={{0,8},{8,16},{16,24},{24,0},{1,9},{9,17},{17,25},{25,1},{2,10},{10... | collective-permute-start | bytes 3145736 | tf_op jit(solution)/shard_map/ppermute | solution.py:54
  774.2 30.1 %collective-permute-start.58 = (bf16[4,64,768]{2,1,0:T(8,128)(2,1)}, bf16[4,64,768]{2,1,0:T(8,128)(2,1)}, u32[]{:S(2)}, u32[]{:S(2)}) collective-permute-start(bf16[4,64,768]{2,1,0:T(8,128)(2,1)} %dynamic-slice_bitcast_fusion.4), channel_id=1, source_target_pairs={{0,2},{2,0},{1,3},{3,1},{4,6},{6,4},{5,7},{7,5},{8,10},{10,8},{9,1... | collective-permute-start | bytes 1179656 | tf_op jit(solution)/shard_map/ppermute | solution.py:118
  812.6 48.7 %collective-permute-start.63 = (bf16[256,2048]{1,0:T(8,128)(2,1)}, bf16[256,2048]{1,0:T(8,128)(2,1)}, u32[]{:S(2)}, u32[]{:S(2)}) collective-permute-start(bf16[256,2048]{1,0:T(8,128)(2,1)} %add_convert_fusion.4), channel_id=1, source_target_pairs={{0,8},{8,16},{16,24},{24,0},{1,9},{9,17},{17,25},{25,1},{2,10},{10... | collective-permute-start | bytes 3145736 | tf_op jit(solution)/shard_map/ppermute | solution.py:54
  812.6 38.9 %collective-permute-start.66 = (bf16[1,64,1536]{2,1,0:T(8,128)(2,1)S(1)}, bf16[1,64,1536]{2,1,0:T(8,128)(2,1)S(1)}, u32[]{:S(2)}, u32[]{:S(2)}) collective-permute-start(bf16[1,64,1536]{2,1,0:T(8,128)(2,1)S(1)} %get-tuple-element.315), channel_id=1, source_target_pairs={{0,8},{8,16},{16,24},{24,0},{1,9},{9,17},{17,25},{25,1},{2,10},{10... | collective-permute-start | bytes 589832 | tf_op jit(solution)/shard_map/ppermute | solution.py:102
  813.1 38.4 %collective-permute-start.65 = (bf16[1,64,1536]{2,1,0:T(8,128)(2,1)S(1)}, bf16[1,64,1536]{2,1,0:T(8,128)(2,1)S(1)}, u32[]{:S(2)}, u32[]{:S(2)}) collective-permute-start(bf16[1,64,1536]{2,1,0:T(8,128)(2,1)S(1)} %get-tuple-element.317), channel_id=1, source_target_pairs={{0,16},{8,24},{16,0},{24,8},{1,17},{9,25},{17,1},{25,9},{2,18},{10... | collective-permute-start | bytes 589832 | tf_op jit(solution)/shard_map/ppermute | solution.py:102
  (162 other events, 2029.2 us)
Sparse Core Ops, SparseCore 0:
  9.9 37.8 all-gather.5
  50.2 59.5 all-gather.11
  120.6 85.2 all-gather.7
  269.6 87.9 all-gather.9
  416.0 73.2 reduce-scatter.3
  576.4 74.0 reduce-scatter.5
  726.1 56.1 reduce-scatter.7

commit v3 on v2

--- a/solution.py
+++ b/solution.py
@@ -81,17 +81,14 @@
 
 
 def in_order(slots, axis):
-    size = lax.axis_size(axis)
-    run = slots[::-1] + slots[:0:-1]
+    size, me = lax.axis_size(axis), lax.axis_index(axis)
     rows = slots[0].shape[0]
-    start = (size - 1 - lax.axis_index(axis)) * rows
-    return lax.dynamic_slice_in_dim(
-        jnp.concatenate(run, axis=0), start, size * rows, axis=0
-    )
-
-
-def gather_in_order(block, axis):
-    return in_order(ring_gather(block, axis), axis)
+    placed = jnp.zeros((size * rows,) + slots[0].shape[1:], slots[0].dtype)
+    for far, slot in enumerate(slots):
+        placed = lax.dynamic_update_slice_in_dim(
+            placed, slot, (me - far) % size * rows, axis=0
+        )
+    return placed
 
 
 def rotate(pieces, axis):
@@ -124,11 +121,9 @@
     early = jnp.concatenate(
         [first, swap(first, "bx"), second, swap(second, "yb")], axis=0
     )
-    late = jnp.concatenate(
-        [swap(early[: 2 * half], "yb"), swap(early[2 * half :], "bx")], axis=0
-    )
+    late = swap(early[: 2 * half], "yb"), swap(early[2 * half :], "bx")
     groups = [(early, swap(early, "bc"))]
-    late = after(late, between(groups[0]))
+    late = jnp.concatenate(after(late, between(groups[0])), axis=0)
     return groups + [(late, swap(late, "bc"))]
 
 
@@ -138,34 +133,36 @@
     return late, swap(late[:half], "yb"), swap(late[half:], "bx")
 
 
-def plane_scatter(terms, came):
+def plane_scatter(terms, came, sums=None):
     rows = terms[0].shape[0] // 4
     early = add_low(terms[0], swap(terms[1], "bc"))
     first = add_low(early[: 2 * rows], came[1])
     second = add_low(early[2 * rows :], came[2])
+    if sums is not None:
+        sums.extend([first, second])
     first_sum = first[:rows].astype(f32) + swap(first[rows:], "bx").astype(f32)
     second_sum = second[:rows].astype(f32) + swap(second[rows:], "yb").astype(f32)
     return jnp.concatenate([first_sum, second_sum], axis=0)
 
 
-def keep_and_swap(blocks, axis, dim):
+def keep_and_swap(blocks, axis, dim, ready=()):
     me = lax.axis_index(axis)
-    kept = lax.dynamic_index_in_dim(blocks, me, dim, keepdims=False)
+    kept = lax.dynamic_index_in_dim(after(blocks, ready), me, dim, keepdims=False)
     sent = lax.dynamic_index_in_dim(blocks, 1 - me, dim, keepdims=False)
     return add_low(kept, swap(sent, axis))
 
 
-def plane_reduce(blocks, steps=None):
-    both = keep_and_swap(blocks, "bc", 3)
+def plane_reduce(blocks, stages=None, ready=((), ())):
+    both = keep_and_swap(blocks, "bc", 3, ready[0])
     middle = blocks.shape[-1] // 2
-    first = keep_and_swap(both[..., :middle], "yb", 1)
-    second = keep_and_swap(both[..., middle:], "bx", 2)
-    if steps is not None:
-        steps.extend([both, (first, second)])
+    first = keep_and_swap(both[..., :middle], "yb", 1, ready[1])
+    second = keep_and_swap(both[..., middle:], "bx", 2, ready[1])
+    if stages is not None:
+        stages.extend([both, (first, second)])
     first = keep_and_swap(first, "bx", 1)
     second = keep_and_swap(second, "yb", 1)
-    if steps is not None:
-        steps.append((first, second))
+    if stages is not None:
+        stages.append((first, second))
     return jnp.concatenate([first, second], axis=-1)
 
 
@@ -588,6 +585,38 @@
     return found[:1], *[found[1 + k * count : 1 + (k + 1) * count] for k in range(3)]
 
 
+def columns_kernel(parts, *refs):
+    place_ref, piece_refs, out_ref = refs[0], refs[1:-1], refs[-1]
+    places = out_ref.shape[1] // piece_refs[0].shape[2]
+    cols = piece_refs[0].shape[2] // parts
+    place = 0
+    for ref in piece_refs:
+        for i in range(ref.shape[0]):
+            for part in range(parts):
+                at = pl.multiple_of((part * places + place_ref[place]) * cols, cols)
+                block = ref[i, :, part * cols : (part + 1) * cols]
+                out_ref[:, pl.ds(at, cols)] = block.astype(f32)
+            place += 1
+
+
+def columns(pieces, places, parts):
+    count = sum(piece.shape[0] for piece in pieces)
+    _, rows, cols = pieces[0].shape
+    if cols // parts % LANES:
+        every = jnp.concatenate(pieces, axis=0)[jnp.argsort(places)]
+        every = every.reshape(count, rows, parts, cols // parts)
+        return jnp.transpose(every, (1, 2, 0, 3)).reshape(rows, -1).astype(f32)
+    return pl.pallas_call(
+        functools.partial(columns_kernel, parts),
+        in_specs=[pl.BlockSpec(memory_space=pltpu.SMEM)]
+        + [pl.BlockSpec(memory_space=pltpu.VMEM)] * len(pieces),
+        out_specs=pl.BlockSpec(memory_space=pltpu.VMEM),
+        out_shape=jax.ShapeDtypeStruct((rows, count * cols), f32),
+        compiler_params=pltpu.CompilerParams(vmem_limit_bytes=VMEM_LIMIT),
+        name="columns",
+    )(places, *pieces)
+
+
 def per_device(
     layer_entries,
     incoming_adjoint,
@@ -671,7 +700,6 @@
     up_own = lax.all_gather(
         after(up_cut, out_own, entry_slots[-1]), "za", axis=0, tiled=True
     )
-
     slot_ids = jnp.arange(ring, dtype=jnp.int32)
     table_ids = jnp.arange(spot_group_table.shape[0], dtype=jnp.int32)
 
@@ -714,7 +742,7 @@
 
     normed_slots, queries, boths = [], [], []
     for slot in range(ring):
-        held = after(entry_slots[slot], entry_slots[min(slot + 2, ring - 1)])
+        held = after(entry_slots[slot], entry_slots[2 if slot < 2 else ring - 1])
         if slot > 0:
             held = after(held, boths[-1][0])
         held = held.astype(f32)
@@ -728,16 +756,18 @@
         boths.append(ring_gather(both, "yb"))
     boths = [[slot[piece] for slot in boths] for piece in range(plane)]
     heads_out, attended, logs = attend(active, queries, boths, query_places, key_places)
-    attended = after(attended, up_own).reshape(ring * tokens, GROUP_WIDTH)
+    attended = attended.reshape(ring * tokens, GROUP_WIDTH)
     inputs = entries.astype(f32)
     hops = []
     parts = [
         lambda s=s: dot(attended[s * tokens : (s + 1) * tokens], out_own).astype(bf16)
         for s in range(ring)
     ]
-    parts[0] = lambda: dot(after(attended[:tokens], wide_adjoint), out_own).astype(bf16)
+    for slot, needed in ((0, wide_adjoint), (2, up_own)):
+        block = after(attended[slot * tokens : (slot + 1) * tokens], needed)
+        parts[slot] = lambda block=block: dot(block, out_own).astype(bf16)
     hidden = inputs + ring_scatter(parts, "za", hops)
-    down_own = lax.all_gather(after(shrink_matrix, hops), "za", axis=0, tiled=True)
+    down_own = lax.all_gather(after(shrink_matrix, hidden), "za", axis=0, tiled=True)
 
     centre = jnp.mean(hidden, axis=1, keepdims=True)
     centered = hidden - centre
@@ -752,9 +782,10 @@
     )
     route_out_lanes = jnp.pad(route_out, ((0, 0), (0, LANES - 4)))
 
-    def gather_back(groups, came=None):
+    def gather_back(groups, came=None, sums=None):
         if paired:
-            return plane_scatter(groups[0], came or plane_scatter_late(groups[1]))
+            came = came or plane_scatter_late(groups[1])
+            return plane_scatter(groups[0], came, sums)
         return lax.psum_scatter(
             groups[0][0], PLANE, scatter_dimension=0, tiled=True
         ).astype(f32)
@@ -803,12 +834,14 @@
         if paired and turn == 1:
             band_came = plane_scatter_late(grad_bands[1])
             came = plane_scatter_late(grad_ins[1])
-            passed = after(passed, came[0], band_came)
+            passed = after(passed, came[0])
     (grad_up,) = passed
     if paired:
         grad_ins[0] = after(grad_ins[0], came)
+    sums = []
+    grad_ffn_in = gather_back(grad_ins, came, sums)
+    grad_bands[0] = after(grad_bands[0], sums)
     grad_band_home = gather_back(grad_bands, band_came)
-    grad_ffn_in = gather_back(grad_ins, came)
 
     temperature = heat_divisor[0]
     squashed = jnp.tanh(dot(ffn_in, route_in))
@@ -822,11 +855,9 @@
         * (grad_mix - jnp.sum(routed * grad_mix, axis=1, keepdims=True))
         / temperature,
     ).astype(bf16)
-    grad_route_out = dot_rows(squashed.astype(bf16), grad_logits)
     grad_pre = (dot_cols(grad_logits, route_out) * (1.0 - squashed * squashed)).astype(
         bf16
     )
-    grad_route_in = dot_rows(ffn_in, grad_pre)
     grad_ffn_in = grad_ffn_in + dot_cols(grad_pre, route_in)
     grad_gain_two = jnp.sum(grad_ffn_in * normal, axis=0)
     grad_bias_two = jnp.sum(grad_ffn_in, axis=0)
@@ -836,18 +867,6 @@
         - jnp.mean(grad_normal, axis=1, keepdims=True)
         - normal * jnp.mean(grad_normal * normal, axis=1, keepdims=True)
     )
-    small_terms = jnp.concatenate(
-        [
-            grad_route_in.reshape(devices, rows, RH),
-            grad_gain_two.reshape(devices, rows, 1),
-            grad_bias_two.reshape(devices, rows, 1),
-            jnp.pad(
-                grad_route_out.reshape(devices, route_out_rows, 4),
-                ((0, 0), (0, rows - route_out_rows), (0, LANES - 6)),
-            ),
-        ],
-        axis=2,
-    ).astype(bf16)
     grad_low = after(grad_hidden.astype(bf16), grad_down)
     outs = after(outs, grad_low)
     came, steps = None, []
@@ -863,20 +882,57 @@
         out_sum = gather_back(outs)
     grad_attn = [grad_low, onward(grad_low, "za")]
     up_terms = dot_rows(wide_in, after(grad_up, grad_low)).astype(bf16)
-    grad_attn.append(onward(after(grad_attn[1], came, up_terms), "za"))
+    grad_attn.append(onward(after(grad_attn[1], came[0] if came else (), up_terms), "za"))
     grad_attn.append(onward(after(grad_attn[2], steps), "za"))
+    router_parts = after(
+        (ffn_in, grad_pre, squashed, grad_logits), grad_attn[2]
+    )
+    grad_route_in = dot_rows(router_parts[0], router_parts[1]).astype(bf16)
+    grad_route_out = dot_rows(router_parts[2].astype(bf16), router_parts[3])
+    others = jnp.concatenate(
+        [
+            grad_gain_two.reshape(devices, rows),
+            grad_bias_two.reshape(devices, rows),
+            grad_route_out.reshape(devices, 4 * route_out_rows),
+            jnp.zeros((devices, RH - 2 * rows - 4 * route_out_rows), f32),
+        ],
+        axis=1,
+    ).astype(bf16)
+    small_rows = rows + 16
+    small_terms = jnp.concatenate(
+        [
+            grad_route_in.reshape(devices, rows, RH),
+            others[:, None],
+            jnp.zeros((devices, 15, RH), bf16),
+        ],
+        axis=1,
+    )
+    if paired:
+        half_rows = steps[0].shape[0] // 2
+        out_sum = jnp.concatenate(
+            [
+                part[:half_rows].astype(f32) + swap(part[half_rows:], axis).astype(f32)
+                for part, axis in zip(steps, ("bx", "yb"))
+            ],
+            axis=0,
+        )
+        small_terms = keep_and_swap(
+            small_terms.reshape(ring, plane, 2, cores, small_rows, RH), "bc", 3
+        )
+    else:
+        small_terms = lax.psum_scatter(
+            small_terms.reshape(ring, group, small_rows, RH),
+            PLANE,
+            scatter_dimension=1,
+            tiled=False,
+        )
+    result = back((hidden + out_sum).astype(bf16))
+    grad_attn[3] = after(grad_attn[3], result, small_terms)
     up_terms = after(up_terms, grad_attn[3])
     up_terms = lax.psum_scatter(up_terms, "za", scatter_dimension=0, tiled=True)
-    up_sums = up_terms
     up_terms = lax.all_to_all(
         up_terms.reshape(group, rows, units), PLANE, 0, 0, tiled=True
     )
-    grad_wup = (
-        jnp.transpose(up_terms.reshape(group, rows, ring, hidden_rows), (1, 2, 0, 3))
-        .reshape(rows, FF)
-        .astype(f32)
-    )
-
     grad_heads = [
         (dot_cols(block, out_own) * active_rows)
         .astype(bf16)
@@ -902,7 +958,6 @@
         )
         if name == "attend_back_far":
             found, grad_heads = lax.optimization_barrier((found, grad_heads))
-            steps, small_terms = after((steps, small_terms), found)
 
             def from_others(grads):
                 running = grads[0]
@@ -917,40 +972,16 @@
             grad_values.append(found[2][0])
         grad_queries.append(found[0])
     if paired:
-        half_rows = steps[0].shape[0] // 2
-        out_sum = jnp.concatenate(
-            [
-                part[:half_rows].astype(f32) + swap(part[half_rows:], axis).astype(f32)
-                for part, axis in zip(steps, ("bx", "yb"))
-            ],
-            axis=0,
-        )
-        small_terms = plane_reduce(
-            small_terms.reshape(ring, plane, 2, cores, rows, RH + LANES)
-        )
-    else:
-        small_terms = lax.psum_scatter(
-            small_terms.reshape(ring, group, rows, RH + LANES),
-            PLANE,
-            scatter_dimension=1,
-            tiled=False,
-        )
-    small_sum = sum(
-        part.astype(f32)
-        for part in rotate(
-            lambda i: lax.dynamic_index_in_dim(small_terms, i, 0, keepdims=False), "za"
-        )
-    )
-    result = back((hidden + out_sum).astype(bf16))
+        small_terms = keep_and_swap(after(small_terms, grad_queries[0]), "bx", 2)
     joint = query_back(grad_queries, cosine, sine)
     attn_wide = jnp.concatenate(grad_attn, axis=0)
     normed_wide = jnp.concatenate(normed_slots, axis=0)
 
-    def to_rows(terms, steps=None):
+    def to_rows(terms, stages, ready):
         cols = terms.shape[-1]
         if paired:
             terms = plane_reduce(
-                terms.reshape(ring, plane, 2, cores, rows, cols), steps
+                terms.reshape(ring, plane, 2, cores, rows, cols), stages, ready
             )
         else:
             terms = lax.psum_scatter(
@@ -959,38 +990,49 @@
                 scatter_dimension=1,
                 tiled=False,
             )
-        return exchange(terms, "za").astype(f32)
+        return rotate(lambda i: lax.dynamic_index_in_dim(terms, i, 0), "za")
 
     flat_joint = lambda array: array.reshape(ring * tokens, 3 * GROUP_WIDTH)
     query_terms = dot_cols(
-        flat_joint(after(joint, grad_keys, grad_values, result, small_sum))[:, :GROUP_WIDTH],
+        flat_joint(after(joint, grad_keys, grad_values, small_terms))[:, :GROUP_WIDTH],
         qkv_own[:, :GROUP_WIDTH],
     )
-    grad_out_terms = dot_rows(attended, attn_wide).astype(bf16)
+    grad_out_terms = dot_rows(after(attended, grad_keys, grad_values), attn_wide).astype(bf16)
     grad_wout = lax.psum_scatter(
         grad_out_terms, PLANE, scatter_dimension=0, tiled=True
     ).astype(f32)
     grad_keys = after(grad_keys, query_terms, grad_out_terms)
     joint = flat_joint(both_back(grad_keys, grad_values, cosine, sine, joint))
     both_own = qkv_own[:, GROUP_WIDTH : 3 * GROUP_WIDTH]
-    low_terms = []
-    for s in range(ring):
-        at = slice(s * tokens, (s + 1) * tokens)
-        terms = query_terms[at] + dot_cols(joint[at, GROUP_WIDTH:], both_own)
-        low_terms.append(terms.astype(bf16))
-    low_terms[1] = after(low_terms[1], up_sums)
-    weight_terms = dot_rows(normed_wide, after(joint, low_terms[1])).astype(bf16)
-    steps = []
-    qkv_rows = to_rows(weight_terms, steps)
-    low_terms[2] = after(low_terms[2], weight_terms)
-    if steps:
-        low_terms[2] = after(low_terms[2], steps[0])
-        low_terms[3] = after(low_terms[3], steps[1], up_terms)
-        low_terms[0] = after(low_terms[0], steps[2])
-    grad_normed = ring_scatter([lambda s=s: low_terms[s] for s in range(ring)], "za")
-    grad_wqkv = jnp.transpose(
-        qkv_rows.reshape(ring, rows, 3, GROUP_WIDTH), (1, 2, 0, 3)
-    ).reshape(rows, 3 * width)
+    def low_term(s, ready):
+        rows_of = after(joint, ready)[s * tokens : (s + 1) * tokens, GROUP_WIDTH:]
+        terms = query_terms[s * tokens : (s + 1) * tokens] + dot_cols(rows_of, both_own)
+        return terms.astype(bf16)
+
+    running = after(low_term(1, ()), up_terms)
+    moved_once = onward(running, "za")
+    weight_terms = dot_rows(normed_wide, after(joint, running)).astype(bf16)
+    running = add_low(after(low_term(2, ()), weight_terms), moved_once)
+    moved_twice = onward(running, "za")
+    stages = []
+    qkv_rows = to_rows(weight_terms, stages, (moved_once, ()))
+    if paired:
+        small_terms = keep_and_swap(after(small_terms, stages[1]), "yb", 1)
+    grad_wup = columns([after(up_terms, running)], jnp.arange(group, dtype=jnp.int32), ring)
+    running = add_low(after(low_term(3, (running, stages[:1])), stages[:2]), moved_twice)
+    moved = onward(running, "za")
+    small_sum = sum(
+        part.astype(f32)
+        for part in rotate(
+            lambda i: lax.dynamic_index_in_dim(
+                after(small_terms, running, stages[2:]), i, 0, keepdims=False
+            ),
+            "za",
+        )
+    )
+    last = after(low_term(0, running), stages[2:], grad_wup, result, small_sum)
+    grad_normed = last.astype(f32) + moved.astype(f32)
+    grad_wqkv = columns(qkv_rows, ((za - slot_ids) % ring).astype(jnp.int32), 3)
     weight_rows = triple_projector_matrix.astype(f32)
     grad_gain_one = jnp.sum(grad_wqkv * weight_rows, axis=1) / (
         mixing_rescale_scalers.astype(f32)
@@ -1008,12 +1050,12 @@
         grad_gain_one,
         grad_wqkv,
         grad_wout,
-        small_sum[:, RH],
-        small_sum[:, RH + 1],
+        small_sum[rows, :rows],
+        small_sum[rows, rows : 2 * rows],
         grad_wup,
         grad_down.astype(f32),
-        small_sum[:, :RH],
-        small_sum[:route_out_rows, RH + 2 : RH + 6],
+        small_sum[:rows],
+        small_sum[rows, 2 * rows : 2 * rows + 4 * route_out_rows].reshape(-1, 4),
     )
 
 

time: 885 us -> 815 us (0.921)
  waiting for transfers between devices: 372 us -> 337 us
  starting transfers between devices: 86.5 us -> 66.7 us
  local copies, waits for them, and re-layouts: 97.4 us -> 84 us
    ppermute x40 -> x38, waiting for transfers between devices: 107 us -> 59.2 us  [swap(): return lax.ppermute(block, axis, SWAP)]
    ppermute x18, waiting for transfers between devices: 203 us -> 225 us  [onward(): return lax.ppermute(block, axis, [(i, (i + 1) % size) for i in range(size)])]
    ppermute x9, waiting for transfers between devices: 48.6 us -> 32.1 us  [rotate(): came.append(lax.ppermute(pieces((me + far) % size), axis, route))]
    all_gather x1, waiting for transfers between devices: 0.01 us -> 14.6 us  [per_device(): lax.all_gather(after(shrink_matrix, hidden), 'za', axis=0, tiled=True)]
    reshape x5 -> x0, local copies, waits for them, and re-layouts: 11.1 us -> none  [the longest x3 7.53 us: per_device(): grad_wqkv = jnp.transpose(qkv_rows.reshape(ring, rows, 3, GROUP_WIDTH), (...]
    all_gather x1, waiting for transfers between devices: 10.2 us -> 0.01 us  [per_device(): lax.all_gather(after(up_cut, out_own, entry_slots[-1]), 'za', axis=0, til...]
    ppermute x18, starting transfers between devices: 18.9 us -> 9.65 us  [onward(): return lax.ppermute(block, axis, [(i, (i + 1) % size) for i in range(size)])]
    ppermute x40 -> x38, starting transfers between devices: 41.2 us -> 34.4 us  [swap(): return lax.ppermute(block, axis, SWAP)]
  transfers between devices with their start and end apart: 76 -> 74, of which waited for: 41 -> 39; matrix products, arithmetic and copies ran while one was open for 26% -> 26% of each run, Pallas kernels for 11% -> 13%
where the time goes in v3:
time: 815 us; the launch traced here: 805 us
  waiting for transfers between devices  337 us (41%)
  Pallas kernels  123 us (15%)
  matrix products  104 us (13%)
  local copies, waits for them, and re-layouts  84 us (10%)
  other arithmetic  73.6 us (9%)
  starting transfers between devices  66.7 us (8%)
  between operations  17.4 us (2%)
    ppermute x18, waiting for transfers between devices, onward(): return lax.ppermute(block, axis, [(i, (i + 1) % size) for i in range(size)])  225 us
    ppermute x38, waiting for transfers between devices, swap(): return lax.ppermute(block, axis, SWAP)  59.2 us
    dot_general x6, matrix products, dot_rows(): lax.dot_general(left_mat, right_mat, (((0,), (0,)), ((), ())), preferred_...  43.7 us
    pallas_call x2, Pallas kernels, feed_down(): pl.pallas_call(functools.partial(feed_down_kernel, count, steps, len(pass...  43.5 us
    dot_general x12, matrix products, dot_cols(): lax.dot_general(left_mat, right_mat, (((1,), (1,)), ((), ())), preferred_...  37 us
    ppermute x38, starting transfers between devices, swap(): return lax.ppermute(block, axis, SWAP)  34.4 us
    ppermute x9, waiting for transfers between devices, rotate(): came.append(lax.ppermute(pieces((me + far) % size), axis, route))  32.1 us
    unnamed x251, local copies, waits for them, and re-layouts  31.3 us
  transfers between devices with their start and end apart: 74, of which 39 were waited for; matrix products, arithmetic and copies ran while one was open for 26% of the time, Pallas kernels for 13%

profile of v3, /device:TPU:0, one launch (start us, length us, event | category | flops | bytes accessed | tf_op | source)
XLA Modules:
  0.0 805.1 jit_solution(10126626591536174366)
XLA Ops:
  30.2 11.3 %collective-permute-done.3 = bf16[1,64,1920]{2,1,0:T(8,128)(2,1)} collective-permute-done((bf16[1,64,1920]{2,1,0:T(8,128)(2,1)}, bf16[1,64,1920]{2,1,0:T(8,128)(2,1)}, u32[]{:S(2)}, u32[]{:S(2)}) %collective-permute-start.3) | collective-permute-done | bytes 245792 | tf_op jit(solution)/shard_map/ppermute | solution.py:99
  55.0 20.1 %collective-permute-done = bf16[256,2048]{1,0:T(8,128)(2,1)S(1)} collective-permute-done((bf16[256,2048]{1,0:T(8,128)(2,1)S(1)}, bf16[256,2048]{1,0:T(8,128)(2,1)S(1)}, u32[]{:S(2)}, u32[]{:S(2)}) %collective-permute-start) | collective-permute-done | bytes 1048608 | tf_op jit(solution)/shard_map/ppermute | solution.py:54
  76.8 24.2 %collective-permute-done.1 = bf16[256,2048]{1,0:T(8,128)(2,1)S(1)} collective-permute-done((bf16[256,2048]{1,0:T(8,128)(2,1)S(1)}, bf16[256,2048]{1,0:T(8,128)(2,1)S(1)}, u32[]{:S(2)}, u32[]{:S(2)}) %collective-permute-start.1) | collective-permute-done | bytes 1048608 | tf_op jit(solution)/shard_map/ppermute | solution.py:54
  102.3 23.8 %collective-permute-done.5 = bf16[256,2048]{1,0:T(8,128)(2,1)} collective-permute-done((bf16[256,2048]{1,0:T(8,128)(2,1)S(1)}, bf16[256,2048]{1,0:T(8,128)(2,1)}, u32[]{:S(2)}, u32[]{:S(2)}) %collective-permute-start.5) | collective-permute-done | bytes 1048608 | tf_op jit(solution)/shard_map/ppermute | solution.py:54
  161.6 11.3 %collective-permute-done.8.refs_11_.refs_19_.refs_6_.refs_10_ = bf16[2,128,1024]{2,1,0:T(8,128)(2,1)} collective-permute-done((bf16[2,128,1024]{2,1,0:T(8,128)(2,1)S(1)}, bf16[2,128,1024]{2,1,0:T(8,128)(2,1)}, u32[]{:S(2)}, u32[]{:S(2)}) %collective-permute-start.8) | collective-permute-done | bytes 524320 | tf_op jit(solution)/shard_map/ppermute | solution.py:54
  173.0 11.2 %collective-permute-done.9.refs_12_.refs_20_.refs_7_.refs_11_ = bf16[2,128,1024]{2,1,0:T(8,128)(2,1)} collective-permute-done((bf16[2,128,1024]{2,1,0:T(8,128)(2,1)S(1)}, bf16[2,128,1024]{2,1,0:T(8,128)(2,1)}, u32[]{:S(2)}, u32[]{:S(2)}) %collective-permute-start.9) | collective-permute-done | bytes 524320 | tf_op jit(solution)/shard_map/ppermute | solution.py:54
  184.2 15.8 %attend.1 = (f32[4,2,128,512]{3,2,1,0:T(8,128)}, bf16[4,2,128,512]{3,2,1,0:T(8,128)(2,1)}, f32[2,4,512,1]{3,2,1,0:T(8,128)}) custom-call(f32[2]{0:T(128)S(1)} %compare_convert_fusion.refs_0_, bf16[2,128,512]{2,1,0:T(8,128)(2,1)S(1)} %copy-done.4, bf16[2,128,512]{2,1,0:T(8,128)(2,1)S(1)} %copy-done.8, bf16[2,128,512]{2,1,0:T(8,128)(2,1)S(1)} %copy-done.12, ...), custom_call_target="tpu_custom_call" | custom-call | tf_op jit(solution)/shard_map/attend/pallas_call | solution.py:323
  210.0 17.0 %collective-permute-done.16 = bf16[256,2048]{1,0:T(8,128)(2,1)} collective-permute-done((bf16[256,2048]{1,0:T(8,128)(2,1)}, bf16[256,2048]{1,0:T(8,128)(2,1)}, u32[]{:S(2)}, u32[]{:S(2)}) %collective-permute-start.16) | collective-permute-done | bytes 1048608 | tf_op jit(solution)/shard_map/ppermute | solution.py:54
  232.1 19.5 %collective-permute-done.17 = bf16[256,2048]{1,0:T(8,128)(2,1)S(1)} collective-permute-done((bf16[256,2048]{1,0:T(8,128)(2,1)S(1)}, bf16[256,2048]{1,0:T(8,128)(2,1)S(1)}, u32[]{:S(2)}, u32[]{:S(2)}) %collective-permute-start.17) | collective-permute-done | bytes 1048608 | tf_op jit(solution)/shard_map/ppermute | solution.py:54
  257.5 16.0 %collective-permute-done.18 = bf16[256,2048]{1,0:T(8,128)(2,1)S(1)} collective-permute-done((bf16[256,2048]{1,0:T(8,128)(2,1)S(1)}, bf16[256,2048]{1,0:T(8,128)(2,1)S(1)}, u32[]{:S(2)}, u32[]{:S(2)}) %collective-permute-start.18) | collective-permute-done | bytes 1048608 | tf_op jit(solution)/shard_map/ppermute | solution.py:54
  310.5 11.7 %feed_up.2 = (bf16[2048,2048]{1,0:T(8,128)(2,1)}, bf16[2048,1024]{1,0:T(8,128)(2,1)}, f32[1024,4]{1,0:T(8,128)S(1)}, f32[1024,1024]{1,0:T(8,128)}) custom-call(bf16[512,2048]{1,0:T(8,128)(2,1)} %pad_maximum_fusion.2.refs_0_, bf16[512,2048]{1,0:T(8,128)(2,1)} %collective-permute-done.23.refs_1_, f32[1]{0:T(128)} %copy.205.refs_2_, f32[2048,1]{1,0:T(8,128)S(1)} %copy-done.1, ...), custom_call_target="tpu_custom_call" | custom-call | flops 4294967296 | bytes 16777216 | tf_op jit(solution)/shard_map/feed_up/pallas_call | solution.py:517
  332.6 11.1 %feed_up.3 = (bf16[2048,2048]{1,0:T(8,128)(2,1)}, bf16[2048,1024]{1,0:T(8,128)(2,1)}, f32[1024,4]{1,0:T(8,128)S(1)}, f32[1024,1024]{1,0:T(8,128)}) custom-call(bf16[512,2048]{1,0:T(8,128)(2,1)S(1)} %constant_dynamic-update-slice_fusion.8.refs_0_, bf16[512,2048]{1,0:T(8,128)(2,1)} %copy-done.83, ...), custom_call_target="tpu_custom_call", output_to_operand_aliasing={{0}: (7, {}), {1}: (8, {})} | custom-call | flops 4294967296 | bytes 16777216 | tf_op jit(solution)/shard_map/feed_up/pallas_call | solution.py:517
  344.5 14.6 %all-gather.10.cloned.1.call-done.refs_5_ = bf16[1024,2048]{1,0:T(8,128)(2,1)} async-done(((bf16[256,2048]{1,0:T(8,128)(2,1)}), bf16[1024,2048]{1,0:T(8,128)(2,1)}) %all-gather.10.cloned.1.call-update) | async-done | bytes 4194320 | tf_op jit(solution)/shard_map/all_gather | solution.py:770
  359.1 14.1 %convolution_convert_fusion.1 = bf16[1024,2048]{1,0:T(8,128)(2,1)} fusion(bf16[2048,1024]{1,0:T(8,128)(2,1)} %get-tuple-element.137.refs_3_, bf16[2048,2048]{1,0:T(8,128)(2,1)} %copy-done.103), kind=kOutput, calls=%fused_computation.22 | convolution fusion | flops 8592031744 | bytes 16777216 | tf_op jit(solution)/shard_map/dot_general | solution.py:41
  374.3 21.8 %feed_down.2 = (bf16[2048,1024]{1,0:T(8,128)(2,1)}, f32[512,4]{1,0:T(8,128)S(1)}, f32[512,4]{1,0:T(8,128)S(1)}, bf16[512,2048]{1,0:T(8,128)(2,1)S(1)}, bf16[512,...) custom-call(bf16[2048,2048]{1,0:T(8,128)(2,1)} %copy-done.103, f32[1024,4]{1,0:T(8,128)S(1)} %copy-done.40, ...), custom_call_target="tpu_custom_call" | custom-call | flops 12884901888 | bytes 25165824 | tf_op jit(solution)/shard_map/feed_down/pallas_call | solution.py:556
  410.4 21.7 %feed_down.3 = (bf16[2048,1024]{1,0:T(8,128)(2,1)}, f32[512,4]{1,0:T(8,128)S(1)}, f32[512,4]{1,0:T(8,128)S(1)}, bf16[512,2048]{1,0:T(8,128)(2,1)S(1)}, bf16[512,...) custom-call(bf16[2048,2048]{1,0:T(8,128)(2,1)} %copy-done.103, ...), custom_call_target="tpu_custom_call", output_to_operand_aliasing={{0}: (6, {})} | custom-call | flops 12884901888 | bytes 25165824 | tf_op jit(solution)/shard_map/feed_down/pallas_call | solution.py:556
  453.5 10.2 %collective-permute-done.34 = f32[128,4]{1,0:T(8,128)} collective-permute-done((f32[128,4]{1,0:T(8,128)}, f32[128,4]{1,0:T(8,128)}, u32[]{:S(2)}, u32[]{:S(2)}) %collective-permute-start.34) | collective-permute-done | bytes 2080 | tf_op jit(solution)/shard_map/ppermute | solution.py:115
  479.1 14.0 %convolution_convert_fusion.2 = bf16[2048,1024]{1,0:T(8,128)(2,1)} fusion(bf16[2048,2048]{1,0:T(8,128)(2,1)} %get-tuple-element.167, bf16[2048,1024]{1,0:T(8,128)(2,1)} %get-tuple-element.169), kind=kOutput, calls=%fused_computation.23 | convolution fusion | flops 8592031744 | bytes 16777216 | tf_op jit(solution)/shard_map/dot_general | solution.py:41
  496.1 10.1 %collective-permute-done.43 = bf16[256,2048]{1,0:T(8,128)(2,1)} collective-permute-done((bf16[256,2048]{1,0:T(8,128)(2,1)}, bf16[256,2048]{1,0:T(8,128)(2,1)}, u32[]{:S(2)}, u32[]{:S(2)}) %collective-permute-start.43) | collective-permute-done | bytes 1048608 | tf_op jit(solution)/shard_map/ppermute | solution.py:54
  520.2 12.9 %collective-permute-done.44 = bf16[256,2048]{1,0:T(8,128)(2,1)} collective-permute-done((bf16[256,2048]{1,0:T(8,128)(2,1)}, bf16[256,2048]{1,0:T(8,128)(2,1)}, u32[]{:S(2)}, u32[]{:S(2)}) %collective-permute-start.44) | collective-permute-done | bytes 1048608 | tf_op jit(solution)/shard_map/ppermute | solution.py:54
  542.9 9.3 %collective-permute-done.42 = bf16[128,2048]{1,0:T(8,128)(2,1)S(1)} collective-permute-done((bf16[128,2048]{1,0:T(8,128)(2,1)S(1)}, bf16[128,2048]{1,0:T(8,128)(2,1)S(1)}, u32[]{:S(2)}, u32[]{:S(2)}) %collective-permute-start.42) | collective-permute-done | bytes 524320 | tf_op jit(solution)/shard_map/ppermute | solution.py:115
  557.0 13.6 %collective-permute-done.45 = bf16[256,2048]{1,0:T(8,128)(2,1)} collective-permute-done((bf16[256,2048]{1,0:T(8,128)(2,1)}, bf16[256,2048]{1,0:T(8,128)(2,1)}, u32[]{:S(2)}, u32[]{:S(2)}) %collective-permute-start.45) | collective-permute-done | bytes 1048608 | tf_op jit(solution)/shard_map/ppermute | solution.py:54
  580.3 12.3 %attend_back_far.1 = (f32[4,2,128,512]{3,2,1,0:T(8,128)}, bf16[4,2,128,512]{3,2,1,0:T(8,128)(2,1)}, bf16[4,2,128,512]{3,2,1,0:T(8,128)(2,1)}) custom-call(bf16[2,128,512]{2,1,0:T(8,128)(2,1)S(1)} %copy-done.5, bf16[2,128,512]{2,1,0:T(8,128)(2,1)S(1)} %copy-done.9, bf16[2,128,512]{2,1,0:T(8,128)(2,1)S(1)} %copy-done.13, bf16[2,128,512]{2,1,0:T(8,128)(2,1)S(1)} %copy-done.17, ...), custom_call_target="tpu_custom_call" | custom-call | tf_op jit(solution)/shard_map/attend_back_far/pallas_call | solution.py:396
  604.1 12.7 %attend_back.1 = (f32[4,2,128,512]{3,2,1,0:T(8,128)}, bf16[4,2,128,512]{3,2,1,0:T(8,128)(2,1)S(1)}, bf16[4,2,128,512]{3,2,1,0:T(8,128)(2,1)}) custom-call(bf16[2,128,512]{2,1,0:T(8,128)(2,1)S(1)} %copy-done.6, bf16[2,128,512]{2,1,0:T(8,128)(2,1)S(1)} %copy-done.10, bf16[2,128,512]{2,1,0:T(8,128)(2,1)S(1)} %copy-done.14, bf16[2,128,512]{2,1,0:T(8,128)(2,1)S(1)} %copy-done.18, ...), custom_call_target="tpu_custom_call" | custom-call | tf_op jit(solution)/shard_map/attend_back/pallas_call | solution.py:396
  622.6 17.6 %collective-permute-done.48.refs_2_ = bf16[4,2,128,512]{3,2,1,0:T(8,128)(2,1)} collective-permute-done((bf16[4,2,128,512]{3,2,1,0:T(8,128)(2,1)}, bf16[4,2,128,512]{3,2,1,0:T(8,128)(2,1)}, u32[]{:S(2)}, u32[]{:S(2)}) %collective-permute-start.48) | collective-permute-done | bytes 1048608 | tf_op jit(solution)/shard_map/ppermute | solution.py:54
  654.2 7.5 both_back.1
  666.4 9.4 %convolution_convert_fusion = bf16[2048,1536]{1,0:T(8,128)(2,1)S(1)} fusion(bf16[1024,1536]{1,0:T(8,128)(2,1)} %bitcast.227, bf16[256,2048]{1,0:T(8,128)(2,1)} %copy-done.92, bf16[256,2048]{1,0:T(8,128)(2,1)} %copy-done.91, bf16[256,2048]{1,0:T(8,128)(2,1)} %copy-done.90, bf16[256,2048]{1,0:T(8,128)(2,1)S(1)} %copy-done.89), kind=kOutput, calls=%fused_computation | convolution fusion | flops 6462373888 | bytes 13631488 | tf_op jit(solution)/shard_map/dot_general | solution.py:41
  692.0 15.1 %collective-permute-done.50 = bf16[256,2048]{1,0:T(8,128)(2,1)} collective-permute-done((bf16[256,2048]{1,0:T(8,128)(2,1)}, bf16[256,2048]{1,0:T(8,128)(2,1)}, u32[]{:S(2)}, u32[]{:S(2)}) %collective-permute-start.50) | collective-permute-done | bytes 1048608 | tf_op jit(solution)/shard_map/ppermute | solution.py:54
  723.3 9.0 %collective-permute-done.53 = bf16[4,2,64,768]{3,2,0,1:T(8,128)(2,1)S(1)} collective-permute-done((bf16[4,2,64,768]{3,2,0,1:T(8,128)(2,1)S(1)}, bf16[4,2,64,768]{3,2,0,1:T(8,128)(2,1)S(1)}, u32[]{:S(2)}, u32[]{:S(2)}) %collective-permute-start.53) | collective-permute-done | bytes 786464 | tf_op jit(solution)/shard_map/ppermute | solution.py:115
  732.7 10.0 %collective-permute-done.54 = bf16[256,2048]{1,0:T(8,128)(2,1)S(1)} collective-permute-done((bf16[256,2048]{1,0:T(8,128)(2,1)S(1)}, bf16[256,2048]{1,0:T(8,128)(2,1)S(1)}, u32[]{:S(2)}, u32[]{:S(2)}) %collective-permute-start.54) | collective-permute-done | bytes 1048608 | tf_op jit(solution)/shard_map/ppermute | solution.py:54
  765.3 7.9 collective-permute-done.58
  782.5 7.1 collective-permute-done.63.refs_3_
  (584 shorter events, 343.5 us)
Async XLA Ops:
  7.2 118.9 %all-gather.6.cloned.1.call-start = ((), (), s32[]{:S(2)}) async-start(), calls=%async_computation.5 | async-start | bytes 2359296 | tf_op jit(solution)/shard_map/all_gather | solution.py:697
  26.1 100.1 %all-gather.12.cloned.1.call-start = ((), (), s32[]{:S(2)}) async-start(), calls=%async_computation.11 | async-start | bytes 8847360 | tf_op jit(solution)/shard_map/all_gather | solution.py:688
  47.1 162.9 %all-gather.8.cloned.1.call-start = ((), (), s32[]{:S(2)}) async-start(), calls=%async_computation.6 | async-start | bytes 5242880 | tf_op jit(solution)/shard_map/all_gather | solution.py:700
  48.4 26.8 %collective-permute-start = (bf16[256,2048]{1,0:T(8,128)(2,1)S(1)}, bf16[256,2048]{1,0:T(8,128)(2,1)S(1)}, u32[]{:S(2)}, u32[]{:S(2)}) collective-permute-start(bf16[256,2048]{1,0:T(8,128)(2,1)S(1)} %bitcast.218), channel_id=1, source_target_pairs={{0,8},{8,16},{16,24},{24,0},{1,9},{9,17},{17,25},{25,1},{2,10},{10... | collective-permute-start | bytes 3145736 | tf_op jit(solution)/shard_map/ppermute | solution.py:54
  52.4 100.8 %collective-permute-start.11 = (bf16[128,2048]{1,0:T(8,128)(2,1)}, bf16[128,2048]{1,0:T(8,128)(2,1)}, u32[]{:S(2)}, u32[]{:S(2)}) collective-permute-start(bf16[128,2048]{1,0:T(8,128)(2,1)} %get-tuple-element.323), channel_id=1, source_target_pairs={{0,4},{4,0},{1,5},{5,1},{2,6},{6,2},{3,7},{7,3},{8,12},{12,8},{9,1... | collective-permute-start | bytes 1572872 | tf_op jit(solution)/shard_map/ppermute | solution.py:115
  53.5 102.7 %collective-permute-start.10 = (bf16[128,2048]{1,0:T(8,128)(2,1)}, bf16[128,2048]{1,0:T(8,128)(2,1)}, u32[]{:S(2)}, u32[]{:S(2)}) collective-permute-start(bf16[128,2048]{1,0:T(8,128)(2,1)} %get-tuple-element.324), channel_id=1, source_target_pairs={{0,2},{2,0},{1,3},{3,1},{4,6},{6,4},{5,7},{7,5},{8,10},{10,8},{9,1... | collective-permute-start | bytes 1572872 | tf_op jit(solution)/shard_map/ppermute | solution.py:115
  75.2 25.9 %collective-permute-start.1 = (bf16[256,2048]{1,0:T(8,128)(2,1)S(1)}, bf16[256,2048]{1,0:T(8,128)(2,1)S(1)}, u32[]{:S(2)}, u32[]{:S(2)}) collective-permute-start(bf16[256,2048]{1,0:T(8,128)(2,1)S(1)} %collective-permute-done), channel_id=1, source_target_pairs={{0,8},{8,16},{16,24},{24,0},{1,9},{9,17},{17,25},{25,1},{2,10},{10... | collective-permute-start | bytes 3145736 | tf_op jit(solution)/shard_map/ppermute | solution.py:54
  126.1 233.0 %all-gather.10.cloned.1.call-start = ((), (), s32[]{:S(2)}) async-start(), calls=%async_computation.7 | async-start | bytes 5242880 | tf_op jit(solution)/shard_map/all_gather | solution.py:770
  145.8 27.2 %collective-permute-start.8 = (bf16[2,128,1024]{2,1,0:T(8,128)(2,1)S(1)}, bf16[2,128,1024]{2,1,0:T(8,128)(2,1)}, u32[]{:S(2)}, u32[]{:S(2)}) collective-permute-start(bf16[2,128,1024]{2,1,0:T(8,128)(2,1)S(1)} %get-tuple-element.122.refs_7_.refs_15_.refs_6_.refs_10_), channel_id=1, source_target_pairs={{0,4},{4,0},{1,5},{5,1},{2,6},{6,2},{3,7},{7,3},{8,12},{12,8},{9,1... | collective-permute-start | bytes 1572872 | tf_op jit(solution)/shard_map/ppermute | solution.py:54
  153.2 31.1 %collective-permute-start.9 = (bf16[2,128,1024]{2,1,0:T(8,128)(2,1)S(1)}, bf16[2,128,1024]{2,1,0:T(8,128)(2,1)}, u32[]{:S(2)}, u32[]{:S(2)}) collective-permute-start(bf16[2,128,1024]{2,1,0:T(8,128)(2,1)S(1)} %get-tuple-element.125.refs_8_.refs_16_.refs_7_.refs_11_), channel_id=1, source_target_pairs={{0,4},{4,0},{1,5},{5,1},{2,6},{6,2},{3,7},{7,3},{8,12},{12,8},{9,1... | collective-permute-start | bytes 1572872 | tf_op jit(solution)/shard_map/ppermute | solution.py:54
  156.2 51.3 %collective-permute-start.14 = (bf16[256,2048]{1,0:T(8,128)(2,1)S(1)}, bf16[256,2048]{1,0:T(8,128)(2,1)S(1)}, u32[]{:S(2)}, u32[]{:S(2)}) collective-permute-start(bf16[256,2048]{1,0:T(8,128)(2,1)S(1)} %pad_maximum_fusion.4), channel_id=1, source_target_pairs={{0,2},{2,0},{1,3},{3,1},{4,6},{6,4},{5,7},{7,5},{8,10},{10,8},{9,1... | collective-permute-start | bytes 3145736 | tf_op jit(solution)/shard_map/ppermute | solution.py:115
  157.9 49.6 %collective-permute-start.13 = (bf16[256,2048]{1,0:T(8,128)(2,1)S(1)}, bf16[256,2048]{1,0:T(8,128)(2,1)S(1)}, u32[]{:S(2)}, u32[]{:S(2)}) collective-permute-start(bf16[256,2048]{1,0:T(8,128)(2,1)S(1)} %pad_maximum_fusion.3), channel_id=1, source_target_pairs={{0,4},{4,0},{1,5},{5,1},{2,6},{6,2},{3,7},{7,3},{8,12},{12,8},{9,1... | collective-permute-start | bytes 3145736 | tf_op jit(solution)/shard_map/ppermute | solution.py:115
  207.5 45.0 %collective-permute-start.12 = (bf16[512,2048]{1,0:T(8,128)(2,1)}, bf16[512,2048]{1,0:T(8,128)(2,1)}, u32[]{:S(2)}, u32[]{:S(2)}) collective-permute-start(bf16[512,2048]{1,0:T(8,128)(2,1)} %pad_maximum_fusion), channel_id=1, source_target_pairs={{0,1},{1,0},{2,3},{3,2},{4,5},{5,4},{6,7},{7,6},{8,9},{9,8},{10,11... | collective-permute-start | bytes 6291464 | tf_op jit(solution)/shard_map/ppermute | solution.py:115
  209.5 46.2 %collective-permute-start.15 = (bf16[512,2048]{1,0:T(8,128)(2,1)}, bf16[512,2048]{1,0:T(8,128)(2,1)}, u32[]{:S(2)}, u32[]{:S(2)}) collective-permute-start(bf16[512,2048]{1,0:T(8,128)(2,1)} %pad_maximum_fusion.1), channel_id=1, source_target_pairs={{0,1},{1,0},{2,3},{3,2},{4,5},{5,4},{6,7},{7,6},{8,9},{9,8},{10,11... | collective-permute-start | bytes 6291464 | tf_op jit(solution)/shard_map/ppermute | solution.py:115
  281.4 196.7 %reduce-scatter.4.cloned.1.call-start = ((), (), s32[]{:S(2)}) async-start(), calls=%async_computation.8 | async-start | bytes 5242880 | tf_op jit(solution)/shard_map/reduce_scatter | solution.py:818
  294.8 27.3 %collective-permute-start.22 = (bf16[256,2048]{1,0:T(8,128)(2,1)}, bf16[256,2048]{1,0:T(8,128)(2,1)}, u32[]{:S(2)}, u32[]{:S(2)}) collective-permute-start(bf16[256,2048]{1,0:T(8,128)(2,1)} %pad_maximum_fusion.6), channel_id=1, source_target_pairs={{0,2},{2,0},{1,3},{3,1},{4,6},{6,4},{5,7},{7,5},{8,10},{10,8},{9,1... | collective-permute-start | bytes 3145736 | tf_op jit(solution)/shard_map/ppermute | solution.py:115
  298.6 25.6 %collective-permute-start.20 = (bf16[256,2048]{1,0:T(8,128)(2,1)}, bf16[256,2048]{1,0:T(8,128)(2,1)}, u32[]{:S(2)}, u32[]{:S(2)}) collective-permute-start(bf16[256,2048]{1,0:T(8,128)(2,1)} %pad_maximum_fusion.5), channel_id=1, source_target_pairs={{0,4},{4,0},{1,5},{5,1},{2,6},{6,2},{3,7},{7,3},{8,12},{12,8},{9,1... | collective-permute-start | bytes 3145736 | tf_op jit(solution)/shard_map/ppermute | solution.py:115
  398.8 247.0 %reduce-scatter.6.cloned.1.call-start = ((), (), s32[]{:S(2)}) async-start(), calls=%async_computation.9 | async-start | bytes 5242880 | tf_op jit(solution)/shard_map/reduce_scatter | solution.py:932
  407.2 25.4 %collective-permute-start.26 = (bf16[256,2048]{1,0:T(8,128)(2,1)S(1)}, bf16[256,2048]{1,0:T(8,128)(2,1)S(1)}, u32[]{:S(2)}, u32[]{:S(2)}) collective-permute-start(bf16[256,2048]{1,0:T(8,128)(2,1)S(1)} %get-tuple-element.313), channel_id=1, source_target_pairs={{0,4},{4,0},{1,5},{5,1},{2,6},{6,2},{3,7},{7,3},{8,12},{12,8},{9,1... | collective-permute-start | bytes 3145736 | tf_op jit(solution)/shard_map/ppermute | solution.py:115
  478.1 28.1 %collective-permute-start.43 = (bf16[256,2048]{1,0:T(8,128)(2,1)}, bf16[256,2048]{1,0:T(8,128)(2,1)}, u32[]{:S(2)}, u32[]{:S(2)}) collective-permute-start(bf16[256,2048]{1,0:T(8,128)(2,1)} %get-tuple-element.162), channel_id=1, source_target_pairs={{0,8},{8,16},{16,24},{24,0},{1,9},{9,17},{17,25},{25,1},{2,10},{10... | collective-permute-start | bytes 3145736 | tf_op jit(solution)/shard_map/ppermute | solution.py:54
  478.5 37.3 %collective-permute-start.37 = (bf16[512,2048]{1,0:T(8,128)(2,1)}, bf16[512,2048]{1,0:T(8,128)(2,1)}, u32[]{:S(2)}, u32[]{:S(2)}) collective-permute-start(bf16[512,2048]{1,0:T(8,128)(2,1)} %get-tuple-element.164), channel_id=1, source_target_pairs={{0,1},{1,0},{2,3},{3,2},{4,5},{5,4},{6,7},{7,6},{8,9},{9,8},{10,11... | collective-permute-start | bytes 6291464 | tf_op jit(solution)/shard_map/ppermute | solution.py:115
  506.2 26.9 %collective-permute-start.44 = (bf16[256,2048]{1,0:T(8,128)(2,1)}, bf16[256,2048]{1,0:T(8,128)(2,1)}, u32[]{:S(2)}, u32[]{:S(2)}) collective-permute-start(bf16[256,2048]{1,0:T(8,128)(2,1)} %collective-permute-done.43), channel_id=1, source_target_pairs={{0,8},{8,16},{16,24},{24,0},{1,9},{9,17},{17,25},{25,1},{2,10},{10... | collective-permute-start | bytes 3145736 | tf_op jit(solution)/shard_map/ppermute | solution.py:54
  507.6 28.6 %collective-permute-start.39 = (bf16[256,2048]{1,0:T(8,128)(2,1)}, bf16[256,2048]{1,0:T(8,128)(2,1)}, u32[]{:S(2)}, u32[]{:S(2)}) collective-permute-start(bf16[256,2048]{1,0:T(8,128)(2,1)} %get-tuple-element.309), channel_id=1, source_target_pairs={{0,4},{4,0},{1,5},{5,1},{2,6},{6,2},{3,7},{7,3},{8,12},{12,8},{9,1... | collective-permute-start | bytes 3145736 | tf_op jit(solution)/shard_map/ppermute | solution.py:115
  509.1 27.2 %collective-permute-start.41 = (bf16[256,2048]{1,0:T(8,128)(2,1)}, bf16[256,2048]{1,0:T(8,128)(2,1)}, u32[]{:S(2)}, u32[]{:S(2)}) collective-permute-start(bf16[256,2048]{1,0:T(8,128)(2,1)} %get-tuple-element.310), channel_id=1, source_target_pairs={{0,2},{2,0},{1,3},{3,1},{4,6},{6,4},{5,7},{7,5},{8,10},{10,8},{9,1... | collective-permute-start | bytes 3145736 | tf_op jit(solution)/shard_map/ppermute | solution.py:115
  542.9 27.7 %collective-permute-start.45 = (bf16[256,2048]{1,0:T(8,128)(2,1)}, bf16[256,2048]{1,0:T(8,128)(2,1)}, u32[]{:S(2)}, u32[]{:S(2)}) collective-permute-start(bf16[256,2048]{1,0:T(8,128)(2,1)} %collective-permute-done.44), channel_id=1, source_target_pairs={{0,8},{8,16},{16,24},{24,0},{1,9},{9,17},{17,25},{25,1},{2,10},{10... | collective-permute-start | bytes 3145736 | tf_op jit(solution)/shard_map/ppermute | solution.py:54
  570.6 119.6 %reduce-scatter.8.cloned.1.call-start = ((), (), s32[]{:S(2)}) async-start(), calls=%async_computation.10 | async-start | bytes 2359296 | tf_op jit(solution)/shard_map/reduce_scatter | solution.py:1001
  592.6 30.0 %collective-permute-start.47 = (bf16[4,2,128,512]{3,2,1,0:T(8,128)(2,1)}, bf16[4,2,128,512]{3,2,1,0:T(8,128)(2,1)}, u32[]{:S(2)}, u32[]{:S(2)}) collective-permute-start(bf16[4,2,128,512]{3,2,1,0:T(8,128)(2,1)} %get-tuple-element.188), channel_id=1, source_target_pairs={{0,4},{4,0},{1,5},{5,1},{2,6},{6,2},{3,7},{7,3},{8,12},{12,8},{9,1... | collective-permute-start | bytes 3145736 | tf_op jit(solution)/shard_map/ppermute | solution.py:54
  593.1 47.1 %collective-permute-start.48 = (bf16[4,2,128,512]{3,2,1,0:T(8,128)(2,1)}, bf16[4,2,128,512]{3,2,1,0:T(8,128)(2,1)}, u32[]{:S(2)}, u32[]{:S(2)}) collective-permute-start(bf16[4,2,128,512]{3,2,1,0:T(8,128)(2,1)} %get-tuple-element.190), channel_id=1, source_target_pairs={{0,4},{4,0},{1,5},{5,1},{2,6},{6,2},{3,7},{7,3},{8,12},{12,8},{9,1... | collective-permute-start | bytes 3145736 | tf_op jit(solution)/shard_map/ppermute | solution.py:54
  679.4 27.7 %collective-permute-start.51 = (bf16[4,2,2,64,1536]{4,3,0,1,2:T(8,128)(2,1)}, bf16[4,2,2,64,1536]{4,3,0,1,2:T(8,128)(2,1)}, u32[]{:S(2)}, u32[]{:S(2)}) collective-permute-start(bf16[4,2,2,64,1536]{4,3,0,1,2:T(8,128)(2,1)} %copy_bitcast_fusion), channel_id=1, source_target_pairs={{0,1},{1,0},{2,3},{3,2},{4,5},{5,4},{6,7},{7,6},{8,9},{9,8},{10,11... | collective-permute-start | bytes 9437192 | tf_op jit(solution)/shard_map/ppermute | solution.py:115
  679.9 27.3 %collective-permute-start.50 = (bf16[256,2048]{1,0:T(8,128)(2,1)}, bf16[256,2048]{1,0:T(8,128)(2,1)}, u32[]{:S(2)}, u32[]{:S(2)}) collective-permute-start(bf16[256,2048]{1,0:T(8,128)(2,1)} %fusion.45), channel_id=1, source_target_pairs={{0,8},{8,16},{16,24},{24,0},{1,9},{9,17},{17,25},{25,1},{2,10},{10... | collective-permute-start | bytes 3145736 | tf_op jit(solution)/shard_map/ppermute | solution.py:54
  716.7 26.1 %collective-permute-start.54 = (bf16[256,2048]{1,0:T(8,128)(2,1)S(1)}, bf16[256,2048]{1,0:T(8,128)(2,1)S(1)}, u32[]{:S(2)}, u32[]{:S(2)}) collective-permute-start(bf16[256,2048]{1,0:T(8,128)(2,1)S(1)} %add_convert_fusion.5), channel_id=1, source_target_pairs={{0,8},{8,16},{16,24},{24,0},{1,9},{9,17},{17,25},{25,1},{2,10},{10... | collective-permute-start | bytes 3145736 | tf_op jit(solution)/shard_map/ppermute | solution.py:54
  744.1 49.5 %collective-permute-start.61 = (bf16[256,2048]{1,0:T(8,128)(2,1)}, bf16[256,2048]{1,0:T(8,128)(2,1)S(1)}, u32[]{:S(2)}, u32[]{:S(2)}) collective-permute-start(bf16[256,2048]{1,0:T(8,128)(2,1)} %add_convert_fusion.4), channel_id=1, source_target_pairs={{0,8},{8,16},{16,24},{24,0},{1,9},{9,17},{17,25},{25,1},{2,10},{10... | collective-permute-start | bytes 3145736 | tf_op jit(solution)/shard_map/ppermute | solution.py:54
  (161 other events, 1855.4 us)
Sparse Core Ops, SparseCore 0:
  9.9 36.2 all-gather.5
  48.7 59.3 all-gather.11
  126.3 80.0 all-gather.7
  281.5 77.5 all-gather.9
  399.0 75.4 reduce-scatter.3
  570.7 73.8 reduce-scatter.5
  648.4 41.7 reduce-scatter.7

commit v4 on v3

--- a/solution.py
+++ b/solution.py
@@ -882,17 +882,27 @@
         out_sum = gather_back(outs)
     grad_attn = [grad_low, onward(grad_low, "za")]
     up_terms = dot_rows(wide_in, after(grad_up, grad_low)).astype(bf16)
-    grad_attn.append(onward(after(grad_attn[1], came[0] if came else (), up_terms), "za"))
-    grad_attn.append(onward(after(grad_attn[2], steps), "za"))
+
+    def head_grads(block):
+        heads = (dot_cols(block, out_own) * active_rows).astype(bf16)
+        return heads.reshape(seqs, block_len, GROUP_WIDTH)
+
+    grad_heads = [head_grads(grad_attn[0])]
+    beside = (came[0] if came else (), up_terms, grad_heads[0])
+    grad_attn.append(onward(after(grad_attn[1], beside), "za"))
+    grad_heads.append(head_grads(grad_attn[1]))
+    grad_attn.append(onward(after(grad_attn[2], grad_heads[1], steps), "za"))
+    grad_heads.append(head_grads(grad_attn[2]))
     router_parts = after(
-        (ffn_in, grad_pre, squashed, grad_logits), grad_attn[2]
+        (ffn_in, grad_pre, squashed, grad_logits, grad_gain_two, grad_bias_two),
+        grad_attn[2],
     )
     grad_route_in = dot_rows(router_parts[0], router_parts[1]).astype(bf16)
     grad_route_out = dot_rows(router_parts[2].astype(bf16), router_parts[3])
     others = jnp.concatenate(
         [
-            grad_gain_two.reshape(devices, rows),
-            grad_bias_two.reshape(devices, rows),
+            router_parts[4].reshape(devices, rows),
+            router_parts[5].reshape(devices, rows),
             grad_route_out.reshape(devices, 4 * route_out_rows),
             jnp.zeros((devices, RH - 2 * rows - 4 * route_out_rows), f32),
         ],
@@ -927,18 +937,13 @@
             tiled=False,
         )
     result = back((hidden + out_sum).astype(bf16))
-    grad_attn[3] = after(grad_attn[3], result, small_terms)
+    grad_attn[3] = after(grad_attn[3], result, small_terms, grad_heads[2])
+    grad_heads.append(head_grads(grad_attn[3]))
     up_terms = after(up_terms, grad_attn[3])
     up_terms = lax.psum_scatter(up_terms, "za", scatter_dimension=0, tiled=True)
     up_terms = lax.all_to_all(
         up_terms.reshape(group, rows, units), PLANE, 0, 0, tiled=True
     )
-    grad_heads = [
-        (dot_cols(block, out_own) * active_rows)
-        .astype(bf16)
-        .reshape(seqs, block_len, GROUP_WIDTH)
-        for block in grad_attn
-    ]
     grad_queries, grad_keys, grad_values = [], [], []
     for name, chosen in (
         ("attend_back_far", range(1, plane)),
@@ -1025,18 +1030,13 @@
         part.astype(f32)
         for part in rotate(
             lambda i: lax.dynamic_index_in_dim(
-                after(small_terms, running, stages[2:]), i, 0, keepdims=False
+                after(small_terms, qkv_rows[1:]), i, 0, keepdims=False
             ),
             "za",
         )
     )
-    last = after(low_term(0, running), stages[2:], grad_wup, result, small_sum)
+    last = after(low_term(0, running), stages[2:], grad_wup, result)
     grad_normed = last.astype(f32) + moved.astype(f32)
-    grad_wqkv = columns(qkv_rows, ((za - slot_ids) % ring).astype(jnp.int32), 3)
-    weight_rows = triple_projector_matrix.astype(f32)
-    grad_gain_one = jnp.sum(grad_wqkv * weight_rows, axis=1) / (
-        mixing_rescale_scalers.astype(f32)
-    )
     inv_home = lax.rsqrt(jnp.mean(inputs * inputs, axis=1, keepdims=True) + epsilon)
     scaled = inputs * inv_home
     grad_scaled = grad_normed * gain_one
@@ -1044,6 +1044,11 @@
         grad_scaled - scaled * jnp.mean(grad_scaled * scaled, axis=1, keepdims=True)
     )
     grad_tokens = back(grad_inputs.astype(bf16))
+    grad_wqkv = columns(after(qkv_rows, grad_tokens), ((za - slot_ids) % ring).astype(jnp.int32), 3)
+    weight_rows = triple_projector_matrix.astype(f32)
+    grad_gain_one = jnp.sum(grad_wqkv * weight_rows, axis=1) / (
+        mixing_rescale_scalers.astype(f32)
+    )
     return (
         result,
         grad_tokens,

time: 815 us -> 829 us (1.017)
    ppermute x18, waiting for transfers between devices: 225 us -> 212 us  [onward(): return lax.ppermute(block, axis, [(i, (i + 1) % size) for i in range(size)])]
    ppermute x9, waiting for transfers between devices: 32.1 us -> 44.6 us  [rotate(): came.append(lax.ppermute(pieces((me + far) % size), axis, route))]
    unnamed x251 -> x285, local copies, waits for them, and re-layouts: 31.3 us -> 33.2 us
  transfers between devices with their start and end apart: 74 -> 74, of which waited for: 39 -> 36; matrix products, arithmetic and copies ran while one was open for 26% -> 26% of each run, Pallas kernels for 13% -> 12%
where the time goes in v4:
time: 829 us; the launch traced here: 819 us
  waiting for transfers between devices  339 us (41%)
  Pallas kernels  124 us (15%)
  matrix products  106 us (13%)
  local copies, waits for them, and re-layouts  83.3 us (10%)
  other arithmetic  78.6 us (9%)
  starting transfers between devices  70.1 us (8%)
  between operations  17.6 us (2%)
    ppermute x18, waiting for transfers between devices, onward(): return lax.ppermute(block, axis, [(i, (i + 1) % size) for i in range(size)])  212 us
    ppermute x38, waiting for transfers between devices, swap(): return lax.ppermute(block, axis, SWAP)  56.1 us
    ppermute x9, waiting for transfers between devices, rotate(): came.append(lax.ppermute(pieces((me + far) % size), axis, route))  44.6 us
    dot_general x6, matrix products, dot_rows(): lax.dot_general(left_mat, right_mat, (((0,), (0,)), ((), ())), preferred_...  44 us
    pallas_call x2, Pallas kernels, feed_down(): pl.pallas_call(functools.partial(feed_down_kernel, count, steps, len(pass...  44 us
    dot_general x12, matrix products, dot_cols(): lax.dot_general(left_mat, right_mat, (((1,), (1,)), ((), ())), preferred_...  39 us
    ppermute x38, starting transfers between devices, swap(): return lax.ppermute(block, axis, SWAP)  35 us
    unnamed x285, local copies, waits for them, and re-layouts  33.2 us
  transfers between devices with their start and end apart: 74, of which 36 were waited for; matrix products, arithmetic and copies ran while one was open for 26% of the time, Pallas kernels for 12%

profile of v4, /device:TPU:0, one launch (start us, length us, event | category | flops | bytes accessed | tf_op | source)
XLA Modules:
  0.0 818.6 jit_solution(2916713682613852142)
XLA Ops:
  30.2 11.3 %collective-permute-done.3 = bf16[1,64,1920]{2,1,0:T(8,128)(2,1)} collective-permute-done((bf16[1,64,1920]{2,1,0:T(8,128)(2,1)}, bf16[1,64,1920]{2,1,0:T(8,128)(2,1)}, u32[]{:S(2)}, u32[]{:S(2)}) %collective-permute-start.3) | collective-permute-done | bytes 245792 | tf_op jit(solution)/shard_map/ppermute | solution.py:99
  55.3 20.4 %collective-permute-done = bf16[256,2048]{1,0:T(8,128)(2,1)} collective-permute-done((bf16[256,2048]{1,0:T(8,128)(2,1)S(1)}, bf16[256,2048]{1,0:T(8,128)(2,1)}, u32[]{:S(2)}, u32[]{:S(2)}) %collective-permute-start) | collective-permute-done | bytes 1048608 | tf_op jit(solution)/shard_map/ppermute | solution.py:54
  77.3 24.5 %collective-permute-done.1 = bf16[256,2048]{1,0:T(8,128)(2,1)S(1)} collective-permute-done((bf16[256,2048]{1,0:T(8,128)(2,1)}, bf16[256,2048]{1,0:T(8,128)(2,1)S(1)}, u32[]{:S(2)}, u32[]{:S(2)}) %collective-permute-start.1) | collective-permute-done | bytes 1048608 | tf_op jit(solution)/shard_map/ppermute | solution.py:54
  102.3 24.6 %collective-permute-done.5 = bf16[256,2048]{1,0:T(8,128)(2,1)} collective-permute-done((bf16[256,2048]{1,0:T(8,128)(2,1)S(1)}, bf16[256,2048]{1,0:T(8,128)(2,1)}, u32[]{:S(2)}, u32[]{:S(2)}) %collective-permute-start.5) | collective-permute-done | bytes 1048608 | tf_op jit(solution)/shard_map/ppermute | solution.py:54
  128.8 6.5 fusion.148.joint_ref
  162.4 11.3 %collective-permute-done.8.refs_11_.refs_19_.refs_6_.refs_10_ = bf16[2,128,1024]{2,1,0:T(8,128)(2,1)} collective-permute-done((bf16[2,128,1024]{2,1,0:T(8,128)(2,1)S(1)}, bf16[2,128,1024]{2,1,0:T(8,128)(2,1)}, u32[]{:S(2)}, u32[]{:S(2)}) %collective-permute-start.8) | collective-permute-done | bytes 524320 | tf_op jit(solution)/shard_map/ppermute | solution.py:54
  173.6 11.2 %collective-permute-done.9.refs_12_.refs_20_.refs_7_.refs_11_ = bf16[2,128,1024]{2,1,0:T(8,128)(2,1)} collective-permute-done((bf16[2,128,1024]{2,1,0:T(8,128)(2,1)S(1)}, bf16[2,128,1024]{2,1,0:T(8,128)(2,1)}, u32[]{:S(2)}, u32[]{:S(2)}) %collective-permute-start.9) | collective-permute-done | bytes 524320 | tf_op jit(solution)/shard_map/ppermute | solution.py:54
  184.9 15.9 %attend.1 = (f32[4,2,128,512]{3,2,1,0:T(8,128)}, bf16[4,2,128,512]{3,2,1,0:T(8,128)(2,1)}, f32[2,4,512,1]{3,2,1,0:T(8,128)}) custom-call(f32[2]{0:T(128)S(1)} %compare_convert_fusion.refs_0_, bf16[2,128,512]{2,1,0:T(8,128)(2,1)S(1)} %copy-done.4, bf16[2,128,512]{2,1,0:T(8,128)(2,1)S(1)} %copy-done.8, bf16[2,128,512]{2,1,0:T(8,128)(2,1)S(1)} %copy-done.12, ...), custom_call_target="tpu_custom_call" | custom-call | tf_op jit(solution)/shard_map/attend/pallas_call | solution.py:323
  210.6 17.7 %collective-permute-done.16 = bf16[256,2048]{1,0:T(8,128)(2,1)} collective-permute-done((bf16[256,2048]{1,0:T(8,128)(2,1)}, bf16[256,2048]{1,0:T(8,128)(2,1)}, u32[]{:S(2)}, u32[]{:S(2)}) %collective-permute-start.16) | collective-permute-done | bytes 1048608 | tf_op jit(solution)/shard_map/ppermute | solution.py:54
  233.5 19.9 %collective-permute-done.17 = bf16[256,2048]{1,0:T(8,128)(2,1)S(1)} collective-permute-done((bf16[256,2048]{1,0:T(8,128)(2,1)S(1)}, bf16[256,2048]{1,0:T(8,128)(2,1)S(1)}, u32[]{:S(2)}, u32[]{:S(2)}) %collective-permute-start.17) | collective-permute-done | bytes 1048608 | tf_op jit(solution)/shard_map/ppermute | solution.py:54
  259.3 16.3 %collective-permute-done.18 = bf16[256,2048]{1,0:T(8,128)(2,1)S(1)} collective-permute-done((bf16[256,2048]{1,0:T(8,128)(2,1)S(1)}, bf16[256,2048]{1,0:T(8,128)(2,1)S(1)}, u32[]{:S(2)}, u32[]{:S(2)}) %collective-permute-start.18) | collective-permute-done | bytes 1048608 | tf_op jit(solution)/shard_map/ppermute | solution.py:54
  312.3 11.7 %feed_up.2 = (bf16[2048,2048]{1,0:T(8,128)(2,1)}, bf16[2048,1024]{1,0:T(8,128)(2,1)}, f32[1024,4]{1,0:T(8,128)S(1)}, f32[1024,1024]{1,0:T(8,128)}) custom-call(bf16[512,2048]{1,0:T(8,128)(2,1)} %pad_maximum_fusion.2.refs_0_, bf16[512,2048]{1,0:T(8,128)(2,1)} %collective-permute-done.23.refs_1_, f32[1]{0:T(128)} %copy.205.refs_2_, f32[2048,1]{1,0:T(8,128)S(1)} %copy-done.1, ...), custom_call_target="tpu_custom_call" | custom-call | flops 4294967296 | bytes 16777216 | tf_op jit(solution)/shard_map/feed_up/pallas_call | solution.py:517
  333.8 11.3 %feed_up.3 = (bf16[2048,2048]{1,0:T(8,128)(2,1)}, bf16[2048,1024]{1,0:T(8,128)(2,1)}, f32[1024,4]{1,0:T(8,128)S(1)}, f32[1024,1024]{1,0:T(8,128)}) custom-call(bf16[512,2048]{1,0:T(8,128)(2,1)S(1)} %constant_dynamic-update-slice_fusion.8.refs_0_, bf16[512,2048]{1,0:T(8,128)(2,1)} %copy-done.92, ...), custom_call_target="tpu_custom_call", output_to_operand_aliasing={{0}: (7, {}), {1}: (8, {})} | custom-call | flops 4294967296 | bytes 16777216 | tf_op jit(solution)/shard_map/feed_up/pallas_call | solution.py:517
  345.9 15.0 %all-gather.10.cloned.1.call-done.refs_5_ = bf16[1024,2048]{1,0:T(8,128)(2,1)} async-done(((bf16[256,2048]{1,0:T(8,128)(2,1)}), bf16[1024,2048]{1,0:T(8,128)(2,1)}) %all-gather.10.cloned.1.call-update) | async-done | bytes 4194320 | tf_op jit(solution)/shard_map/all_gather | solution.py:770
  360.8 14.0 %convolution_convert_fusion.1 = bf16[1024,2048]{1,0:T(8,128)(2,1)} fusion(bf16[2048,1024]{1,0:T(8,128)(2,1)} %get-tuple-element.143.refs_3_, bf16[2048,2048]{1,0:T(8,128)(2,1)} %copy-done.112), kind=kOutput, calls=%fused_computation.22 | convolution fusion | flops 8592031744 | bytes 16777216 | tf_op jit(solution)/shard_map/dot_general | solution.py:41
  375.9 21.8 %feed_down.2 = (bf16[2048,1024]{1,0:T(8,128)(2,1)}, f32[512,4]{1,0:T(8,128)S(1)}, f32[512,4]{1,0:T(8,128)S(1)}, bf16[512,2048]{1,0:T(8,128)(2,1)S(1)}, bf16[512,...) custom-call(bf16[2048,2048]{1,0:T(8,128)(2,1)} %copy-done.112, f32[1024,4]{1,0:T(8,128)S(1)} %copy-done.44, ...), custom_call_target="tpu_custom_call" | custom-call | flops 12884901888 | bytes 25165824 | tf_op jit(solution)/shard_map/feed_down/pallas_call | solution.py:556
  412.1 22.2 %feed_down.3 = (bf16[2048,1024]{1,0:T(8,128)(2,1)}, f32[512,4]{1,0:T(8,128)S(1)}, f32[512,4]{1,0:T(8,128)S(1)}, bf16[512,2048]{1,0:T(8,128)(2,1)S(1)}, bf16[512,...) custom-call(bf16[2048,2048]{1,0:T(8,128)(2,1)} %copy-done.112, ...), custom_call_target="tpu_custom_call", output_to_operand_aliasing={{0}: (6, {})} | custom-call | flops 12884901888 | bytes 25165824 | tf_op jit(solution)/shard_map/feed_down/pallas_call | solution.py:556
  458.9 10.7 %collective-permute-done.34 = f32[128,4]{1,0:T(8,128)} collective-permute-done((f32[128,4]{1,0:T(8,128)}, f32[128,4]{1,0:T(8,128)}, u32[]{:S(2)}, u32[]{:S(2)}) %collective-permute-start.34) | collective-permute-done | bytes 2080 | tf_op jit(solution)/shard_map/ppermute | solution.py:115
  485.1 14.0 %convolution_convert_fusion.2 = bf16[2048,1024]{1,0:T(8,128)(2,1)} fusion(bf16[2048,2048]{1,0:T(8,128)(2,1)} %get-tuple-element.173, bf16[2048,1024]{1,0:T(8,128)(2,1)} %get-tuple-element.175), kind=kOutput, calls=%fused_computation.23 | convolution fusion | flops 8592031744 | bytes 16777216 | tf_op jit(solution)/shard_map/dot_general | solution.py:41
  521.0 15.0 %collective-permute-done.44 = bf16[256,2048]{1,0:T(8,128)(2,1)S(1)} collective-permute-done((bf16[256,2048]{1,0:T(8,128)(2,1)}, bf16[256,2048]{1,0:T(8,128)(2,1)S(1)}, u32[]{:S(2)}, u32[]{:S(2)}) %collective-permute-start.44) | collective-permute-done | bytes 1048608 | tf_op jit(solution)/shard_map/ppermute | solution.py:54
  550.8 6.3 collective-permute-done.42
  565.6 10.8 %collective-permute-done.45 = bf16[256,2048]{1,0:T(8,128)(2,1)S(1)} collective-permute-done((bf16[256,2048]{1,0:T(8,128)(2,1)S(1)}, bf16[256,2048]{1,0:T(8,128)(2,1)S(1)}, u32[]{:S(2)}, u32[]{:S(2)}) %collective-permute-start.45) | collective-permute-done | bytes 1048608 | tf_op jit(solution)/shard_map/ppermute | solution.py:54
  580.3 12.5 %attend_back_far.1 = (f32[4,2,128,512]{3,2,1,0:T(8,128)}, bf16[4,2,128,512]{3,2,1,0:T(8,128)(2,1)}, bf16[4,2,128,512]{3,2,1,0:T(8,128)(2,1)}) custom-call(bf16[2,128,512]{2,1,0:T(8,128)(2,1)S(1)} %copy-done.5, bf16[2,128,512]{2,1,0:T(8,128)(2,1)S(1)} %copy-done.9, bf16[2,128,512]{2,1,0:T(8,128)(2,1)S(1)} %copy-done.13, bf16[2,128,512]{2,1,0:T(8,128)(2,1)S(1)} %copy-done.17, ...), custom_call_target="tpu_custom_call" | custom-call | tf_op jit(solution)/shard_map/attend_back_far/pallas_call | solution.py:396
  603.4 12.8 %attend_back.1 = (f32[4,2,128,512]{3,2,1,0:T(8,128)}, bf16[4,2,128,512]{3,2,1,0:T(8,128)(2,1)S(1)}, bf16[4,2,128,512]{3,2,1,0:T(8,128)(2,1)}) custom-call(bf16[2,128,512]{2,1,0:T(8,128)(2,1)S(1)} %copy-done.6, bf16[2,128,512]{2,1,0:T(8,128)(2,1)S(1)} %copy-done.10, bf16[2,128,512]{2,1,0:T(8,128)(2,1)S(1)} %copy-done.14, bf16[2,128,512]{2,1,0:T(8,128)(2,1)S(1)} %copy-done.18, ...), custom_call_target="tpu_custom_call" | custom-call | tf_op jit(solution)/shard_map/attend_back/pallas_call | solution.py:396
  622.1 18.0 %collective-permute-done.48.refs_2_ = bf16[4,2,128,512]{3,2,1,0:T(8,128)(2,1)} collective-permute-done((bf16[4,2,128,512]{3,2,1,0:T(8,128)(2,1)}, bf16[4,2,128,512]{3,2,1,0:T(8,128)(2,1)}, u32[]{:S(2)}, u32[]{:S(2)}) %collective-permute-start.48) | collective-permute-done | bytes 1048608 | tf_op jit(solution)/shard_map/ppermute | solution.py:54
  645.1 6.6 reduce-scatter.6.cloned.1.call-done
  660.1 7.5 both_back.1
  672.4 9.4 %convolution_convert_fusion = bf16[2048,1536]{1,0:T(8,128)(2,1)S(1)} fusion(bf16[1024,1536]{1,0:T(8,128)(2,1)} %bitcast.227, bf16[256,2048]{1,0:T(8,128)(2,1)} %copy-done.102, bf16[256,2048]{1,0:T(8,128)(2,1)} %copy-done.101, bf16[256,2048]{1,0:T(8,128)(2,1)} %copy-done.100, bf16[256,2048]{1,0:T(8,128)(2,1)S(1)} %copy-done.99), kind=kOutput, calls=%fused_computation | convolution fusion | flops 6462373888 | bytes 13631488 | tf_op jit(solution)/shard_map/dot_general | solution.py:41
  699.0 14.1 %collective-permute-done.50 = bf16[256,2048]{1,0:T(8,128)(2,1)} collective-permute-done((bf16[256,2048]{1,0:T(8,128)(2,1)}, bf16[256,2048]{1,0:T(8,128)(2,1)}, u32[]{:S(2)}, u32[]{:S(2)}) %collective-permute-start.50) | collective-permute-done | bytes 1048608 | tf_op jit(solution)/shard_map/ppermute | solution.py:54
  729.3 7.4 collective-permute-done.52
  758.6 22.0 %collective-permute-done.60.refs_4_ = bf16[1,64,1536]{2,1,0:T(8,128)(2,1)S(1)} collective-permute-done((bf16[1,64,1536]{2,1,0:T(8,128)(2,1)S(1)}, bf16[1,64,1536]{2,1,0:T(8,128)(2,1)S(1)}, u32[]{:S(2)}, u32[]{:S(2)}) %collective-permute-start.60) | collective-permute-done | bytes 196640 | tf_op jit(solution)/shard_map/ppermute | solution.py:99
  784.9 6.3 collective-permute-done.59.refs_3_
  (619 shorter events, 352.0 us)
Async XLA Ops:
  7.2 119.8 %all-gather.6.cloned.1.call-start = ((), (), s32[]{:S(2)}) async-start(), calls=%async_computation.5 | async-start | bytes 2359296 | tf_op jit(solution)/shard_map/all_gather | solution.py:697
  26.1 101.0 %all-gather.12.cloned.1.call-start = ((), (), s32[]{:S(2)}) async-start(), calls=%async_computation.11 | async-start | bytes 8847360 | tf_op jit(solution)/shard_map/all_gather | solution.py:688
  47.1 163.5 %all-gather.8.cloned.1.call-start = ((), (), s32[]{:S(2)}) async-start(), calls=%async_computation.6 | async-start | bytes 5242880 | tf_op jit(solution)/shard_map/all_gather | solution.py:700
  47.6 28.2 %collective-permute-start = (bf16[256,2048]{1,0:T(8,128)(2,1)S(1)}, bf16[256,2048]{1,0:T(8,128)(2,1)}, u32[]{:S(2)}, u32[]{:S(2)}) collective-permute-start(bf16[256,2048]{1,0:T(8,128)(2,1)S(1)} %bitcast.218), channel_id=1, source_target_pairs={{0,8},{8,16},{16,24},{24,0},{1,9},{9,17},{17,25},{25,1},{2,10},{10... | collective-permute-start | bytes 3145736 | tf_op jit(solution)/shard_map/ppermute | solution.py:54
  52.2 103.6 %collective-permute-start.11 = (bf16[128,2048]{1,0:T(8,128)(2,1)}, bf16[128,2048]{1,0:T(8,128)(2,1)}, u32[]{:S(2)}, u32[]{:S(2)}) collective-permute-start(bf16[128,2048]{1,0:T(8,128)(2,1)} %get-tuple-element.335), channel_id=1, source_target_pairs={{0,4},{4,0},{1,5},{5,1},{2,6},{6,2},{3,7},{7,3},{8,12},{12,8},{9,1... | collective-permute-start | bytes 1572872 | tf_op jit(solution)/shard_map/ppermute | solution.py:115
  53.8 104.6 %collective-permute-start.10 = (bf16[128,2048]{1,0:T(8,128)(2,1)}, bf16[128,2048]{1,0:T(8,128)(2,1)}, u32[]{:S(2)}, u32[]{:S(2)}) collective-permute-start(bf16[128,2048]{1,0:T(8,128)(2,1)} %get-tuple-element.336), channel_id=1, source_target_pairs={{0,2},{2,0},{1,3},{3,1},{4,6},{6,4},{5,7},{7,5},{8,10},{10,8},{9,1... | collective-permute-start | bytes 1572872 | tf_op jit(solution)/shard_map/ppermute | solution.py:115
  127.0 233.8 %all-gather.10.cloned.1.call-start = ((), (), s32[]{:S(2)}) async-start(), calls=%async_computation.7 | async-start | bytes 5242880 | tf_op jit(solution)/shard_map/all_gather | solution.py:770
  155.8 29.1 %collective-permute-start.9 = (bf16[2,128,1024]{2,1,0:T(8,128)(2,1)S(1)}, bf16[2,128,1024]{2,1,0:T(8,128)(2,1)}, u32[]{:S(2)}, u32[]{:S(2)}) collective-permute-start(bf16[2,128,1024]{2,1,0:T(8,128)(2,1)S(1)} %get-tuple-element.131.refs_8_.refs_16_.refs_7_.refs_11_), channel_id=1, source_target_pairs={{0,4},{4,0},{1,5},{5,1},{2,6},{6,2},{3,7},{7,3},{8,12},{12,8},{9,1... | collective-permute-start | bytes 1572872 | tf_op jit(solution)/shard_map/ppermute | solution.py:54
  158.4 49.8 %collective-permute-start.14 = (bf16[256,2048]{1,0:T(8,128)(2,1)S(1)}, bf16[256,2048]{1,0:T(8,128)(2,1)S(1)}, u32[]{:S(2)}, u32[]{:S(2)}) collective-permute-start(bf16[256,2048]{1,0:T(8,128)(2,1)S(1)} %pad_maximum_fusion.4), channel_id=1, source_target_pairs={{0,2},{2,0},{1,3},{3,1},{4,6},{6,4},{5,7},{7,5},{8,10},{10,8},{9,1... | collective-permute-start | bytes 3145736 | tf_op jit(solution)/shard_map/ppermute | solution.py:115
  160.9 47.3 %collective-permute-start.13 = (bf16[256,2048]{1,0:T(8,128)(2,1)S(1)}, bf16[256,2048]{1,0:T(8,128)(2,1)S(1)}, u32[]{:S(2)}, u32[]{:S(2)}) collective-permute-start(bf16[256,2048]{1,0:T(8,128)(2,1)S(1)} %pad_maximum_fusion.3), channel_id=1, source_target_pairs={{0,4},{4,0},{1,5},{5,1},{2,6},{6,2},{3,7},{7,3},{8,12},{12,8},{9,1... | collective-permute-start | bytes 3145736 | tf_op jit(solution)/shard_map/ppermute | solution.py:115
  208.2 46.1 %collective-permute-start.12 = (bf16[512,2048]{1,0:T(8,128)(2,1)}, bf16[512,2048]{1,0:T(8,128)(2,1)}, u32[]{:S(2)}, u32[]{:S(2)}) collective-permute-start(bf16[512,2048]{1,0:T(8,128)(2,1)} %pad_maximum_fusion), channel_id=1, source_target_pairs={{0,1},{1,0},{2,3},{3,2},{4,5},{5,4},{6,7},{7,6},{8,9},{9,8},{10,11... | collective-permute-start | bytes 6291464 | tf_op jit(solution)/shard_map/ppermute | solution.py:115
  210.1 47.3 %collective-permute-start.15 = (bf16[512,2048]{1,0:T(8,128)(2,1)}, bf16[512,2048]{1,0:T(8,128)(2,1)}, u32[]{:S(2)}, u32[]{:S(2)}) collective-permute-start(bf16[512,2048]{1,0:T(8,128)(2,1)} %pad_maximum_fusion.1), channel_id=1, source_target_pairs={{0,1},{1,0},{2,3},{3,2},{4,5},{5,4},{6,7},{7,6},{8,9},{9,8},{10,11... | collective-permute-start | bytes 6291464 | tf_op jit(solution)/shard_map/ppermute | solution.py:115
  282.7 201.4 %reduce-scatter.4.cloned.1.call-start = ((), (), s32[]{:S(2)}) async-start(), calls=%async_computation.8 | async-start | bytes 5242880 | tf_op jit(solution)/shard_map/reduce_scatter | solution.py:818
  296.1 27.9 %collective-permute-start.22 = (bf16[256,2048]{1,0:T(8,128)(2,1)}, bf16[256,2048]{1,0:T(8,128)(2,1)}, u32[]{:S(2)}, u32[]{:S(2)}) collective-permute-start(bf16[256,2048]{1,0:T(8,128)(2,1)} %pad_maximum_fusion.6), channel_id=1, source_target_pairs={{0,2},{2,0},{1,3},{3,1},{4,6},{6,4},{5,7},{7,5},{8,10},{10,8},{9,1... | collective-permute-start | bytes 3145736 | tf_op jit(solution)/shard_map/ppermute | solution.py:115
  400.6 251.0 %reduce-scatter.6.cloned.1.call-start = ((), (), s32[]{:S(2)}) async-start(), calls=%async_computation.9 | async-start | bytes 5242880 | tf_op jit(solution)/shard_map/reduce_scatter | solution.py:943
  408.9 28.2 %collective-permute-start.26 = (bf16[256,2048]{1,0:T(8,128)(2,1)S(1)}, bf16[256,2048]{1,0:T(8,128)(2,1)}, u32[]{:S(2)}, u32[]{:S(2)}) collective-permute-start(bf16[256,2048]{1,0:T(8,128)(2,1)S(1)} %get-tuple-element.325), channel_id=1, source_target_pairs={{0,4},{4,0},{1,5},{5,1},{2,6},{6,2},{3,7},{7,3},{8,12},{12,8},{9,1... | collective-permute-start | bytes 3145736 | tf_op jit(solution)/shard_map/ppermute | solution.py:115
  410.7 26.5 %collective-permute-start.27 = (bf16[256,2048]{1,0:T(8,128)(2,1)S(1)}, bf16[256,2048]{1,0:T(8,128)(2,1)}, u32[]{:S(2)}, u32[]{:S(2)}) collective-permute-start(bf16[256,2048]{1,0:T(8,128)(2,1)S(1)} %get-tuple-element.326), channel_id=1, source_target_pairs={{0,2},{2,0},{1,3},{3,1},{4,6},{6,4},{5,7},{7,5},{8,10},{10,8},{9,1... | collective-permute-start | bytes 3145736 | tf_op jit(solution)/shard_map/ppermute | solution.py:115
  484.1 26.7 %collective-permute-start.43 = (bf16[256,2048]{1,0:T(8,128)(2,1)}, bf16[256,2048]{1,0:T(8,128)(2,1)}, u32[]{:S(2)}, u32[]{:S(2)}) collective-permute-start(bf16[256,2048]{1,0:T(8,128)(2,1)} %get-tuple-element.168), channel_id=1, source_target_pairs={{0,8},{8,16},{16,24},{24,0},{1,9},{9,17},{17,25},{25,1},{2,10},{10... | collective-permute-start | bytes 3145736 | tf_op jit(solution)/shard_map/ppermute | solution.py:54
  484.5 32.8 %collective-permute-start.37 = (bf16[512,2048]{1,0:T(8,128)(2,1)}, bf16[512,2048]{1,0:T(8,128)(2,1)}, u32[]{:S(2)}, u32[]{:S(2)}) collective-permute-start(bf16[512,2048]{1,0:T(8,128)(2,1)} %get-tuple-element.170), channel_id=1, source_target_pairs={{0,1},{1,0},{2,3},{3,2},{4,5},{5,4},{6,7},{7,6},{8,9},{9,8},{10,11... | collective-permute-start | bytes 6291464 | tf_op jit(solution)/shard_map/ppermute | solution.py:115
  512.2 30.4 %collective-permute-start.39 = (bf16[256,2048]{1,0:T(8,128)(2,1)}, bf16[256,2048]{1,0:T(8,128)(2,1)}, u32[]{:S(2)}, u32[]{:S(2)}) collective-permute-start(bf16[256,2048]{1,0:T(8,128)(2,1)} %get-tuple-element.321), channel_id=1, source_target_pairs={{0,4},{4,0},{1,5},{5,1},{2,6},{6,2},{3,7},{7,3},{8,12},{12,8},{9,1... | collective-permute-start | bytes 3145736 | tf_op jit(solution)/shard_map/ppermute | solution.py:115
  513.2 29.5 %collective-permute-start.41 = (bf16[256,2048]{1,0:T(8,128)(2,1)}, bf16[256,2048]{1,0:T(8,128)(2,1)}, u32[]{:S(2)}, u32[]{:S(2)}) collective-permute-start(bf16[256,2048]{1,0:T(8,128)(2,1)} %get-tuple-element.322), channel_id=1, source_target_pairs={{0,2},{2,0},{1,3},{3,1},{4,6},{6,4},{5,7},{7,5},{8,10},{10,8},{9,1... | collective-permute-start | bytes 3145736 | tf_op jit(solution)/shard_map/ppermute | solution.py:115
  549.1 27.2 %collective-permute-start.45 = (bf16[256,2048]{1,0:T(8,128)(2,1)S(1)}, bf16[256,2048]{1,0:T(8,128)(2,1)S(1)}, u32[]{:S(2)}, u32[]{:S(2)}) collective-permute-start(bf16[256,2048]{1,0:T(8,128)(2,1)S(1)} %copy-done.123), channel_id=1, source_target_pairs={{0,8},{8,16},{16,24},{24,0},{1,9},{9,17},{17,25},{25,1},{2,10},{10... | collective-permute-start | bytes 3145736 | tf_op jit(solution)/shard_map/ppermute | solution.py:54
  577.4 119.9 %reduce-scatter.8.cloned.1.call-start = ((), (), s32[]{:S(2)}) async-start(), calls=%async_computation.10 | async-start | bytes 2359296 | tf_op jit(solution)/shard_map/reduce_scatter | solution.py:1006
  592.9 29.1 %collective-permute-start.47 = (bf16[4,2,128,512]{3,2,1,0:T(8,128)(2,1)}, bf16[4,2,128,512]{3,2,1,0:T(8,128)(2,1)}, u32[]{:S(2)}, u32[]{:S(2)}) collective-permute-start(bf16[4,2,128,512]{3,2,1,0:T(8,128)(2,1)} %get-tuple-element.196), channel_id=1, source_target_pairs={{0,4},{4,0},{1,5},{5,1},{2,6},{6,2},{3,7},{7,3},{8,12},{12,8},{9,1... | collective-permute-start | bytes 3145736 | tf_op jit(solution)/shard_map/ppermute | solution.py:54
  593.6 46.4 %collective-permute-start.48 = (bf16[4,2,128,512]{3,2,1,0:T(8,128)(2,1)}, bf16[4,2,128,512]{3,2,1,0:T(8,128)(2,1)}, u32[]{:S(2)}, u32[]{:S(2)}) collective-permute-start(bf16[4,2,128,512]{3,2,1,0:T(8,128)(2,1)} %get-tuple-element.198), channel_id=1, source_target_pairs={{0,4},{4,0},{1,5},{5,1},{2,6},{6,2},{3,7},{7,3},{8,12},{12,8},{9,1... | collective-permute-start | bytes 3145736 | tf_op jit(solution)/shard_map/ppermute | solution.py:54
  685.4 27.7 %collective-permute-start.51 = (bf16[4,2,2,64,1536]{4,3,0,1,2:T(8,128)(2,1)}, bf16[4,2,2,64,1536]{4,3,0,1,2:T(8,128)(2,1)}, u32[]{:S(2)}, u32[]{:S(2)}) collective-permute-start(bf16[4,2,2,64,1536]{4,3,0,1,2:T(8,128)(2,1)} %copy_bitcast_fusion), channel_id=1, source_target_pairs={{0,1},{1,0},{2,3},{3,2},{4,5},{5,4},{6,7},{7,6},{8,9},{9,8},{10,11... | collective-permute-start | bytes 9437192 | tf_op jit(solution)/shard_map/ppermute | solution.py:115
  685.8 27.2 %collective-permute-start.50 = (bf16[256,2048]{1,0:T(8,128)(2,1)}, bf16[256,2048]{1,0:T(8,128)(2,1)}, u32[]{:S(2)}, u32[]{:S(2)}) collective-permute-start(bf16[256,2048]{1,0:T(8,128)(2,1)} %fusion.45), channel_id=1, source_target_pairs={{0,8},{8,16},{16,24},{24,0},{1,9},{9,17},{17,25},{25,1},{2,10},{10... | collective-permute-start | bytes 3145736 | tf_op jit(solution)/shard_map/ppermute | solution.py:54
  721.1 26.4 %collective-permute-start.54 = (bf16[256,2048]{1,0:T(8,128)(2,1)S(1)}, bf16[256,2048]{1,0:T(8,128)(2,1)S(1)}, u32[]{:S(2)}, u32[]{:S(2)}) collective-permute-start(bf16[256,2048]{1,0:T(8,128)(2,1)S(1)} %add_convert_fusion.5), channel_id=1, source_target_pairs={{0,8},{8,16},{16,24},{24,0},{1,9},{9,17},{17,25},{25,1},{2,10},{10... | collective-permute-start | bytes 3145736 | tf_op jit(solution)/shard_map/ppermute | solution.py:54
  748.9 53.1 %collective-permute-start.57 = (bf16[256,2048]{1,0:T(8,128)(2,1)}, bf16[256,2048]{1,0:T(8,128)(2,1)S(1)}, u32[]{:S(2)}, u32[]{:S(2)}) collective-permute-start(bf16[256,2048]{1,0:T(8,128)(2,1)} %add_convert_fusion.4), channel_id=1, source_target_pairs={{0,8},{8,16},{16,24},{24,0},{1,9},{9,17},{17,25},{25,1},{2,10},{10... | collective-permute-start | bytes 3145736 | tf_op jit(solution)/shard_map/ppermute | solution.py:54
  754.1 26.6 %collective-permute-start.60 = (bf16[1,64,1536]{2,1,0:T(8,128)(2,1)S(1)}, bf16[1,64,1536]{2,1,0:T(8,128)(2,1)S(1)}, u32[]{:S(2)}, u32[]{:S(2)}) collective-permute-start(bf16[1,64,1536]{2,1,0:T(8,128)(2,1)S(1)} %get-tuple-element.341), channel_id=1, source_target_pairs={{0,24},{8,0},{16,8},{24,16},{1,25},{9,1},{17,9},{25,17},{2,26},{10... | collective-permute-start | bytes 589832 | tf_op jit(solution)/shard_map/ppermute | solution.py:99
  757.9 27.0 %collective-permute-start.58 = (bf16[1,64,1536]{2,1,0:T(8,128)(2,1)S(1)}, bf16[1,64,1536]{2,1,0:T(8,128)(2,1)S(1)}, u32[]{:S(2)}, u32[]{:S(2)}) collective-permute-start(bf16[1,64,1536]{2,1,0:T(8,128)(2,1)S(1)} %get-tuple-element.343), channel_id=1, source_target_pairs={{0,8},{8,16},{16,24},{24,0},{1,9},{9,17},{17,25},{25,1},{2,10},{10... | collective-permute-start | bytes 589832 | tf_op jit(solution)/shard_map/ppermute | solution.py:99
  757.9 33.2 %collective-permute-start.59 = (bf16[1,64,1536]{2,1,0:T(8,128)(2,1)S(1)}, bf16[1,64,1536]{2,1,0:T(8,128)(2,1)S(1)}, u32[]{:S(2)}, u32[]{:S(2)}) collective-permute-start(bf16[1,64,1536]{2,1,0:T(8,128)(2,1)S(1)} %get-tuple-element.344), channel_id=1, source_target_pairs={{0,16},{8,24},{16,0},{24,8},{1,17},{9,25},{17,1},{25,9},{2,18},{10... | collective-permute-start | bytes 589832 | tf_op jit(solution)/shard_map/ppermute | solution.py:99
  (178 other events, 1880.5 us)
Sparse Core Ops, SparseCore 0:
  9.9 36.2 all-gather.5
  48.7 59.9 all-gather.11
  127.1 80.6 all-gather.7
  282.8 77.9 all-gather.9
  400.7 75.4 reduce-scatter.3
  577.5 74.1 reduce-scatter.5
  655.5 41.6 reduce-scatter.7

commit v5 on v3

--- a/solution.py
+++ b/solution.py
@@ -971,8 +971,15 @@
             grad_keys.append(found[1][0])
             grad_values.append(found[2][0])
         grad_queries.append(found[0])
-    if paired:
-        small_terms = keep_and_swap(after(small_terms, grad_queries[0]), "bx", 2)
+    small_terms = sum(
+        part.astype(f32)
+        for part in rotate(
+            lambda i: lax.dynamic_index_in_dim(
+                after(small_terms, grad_queries[0]), i, 0, keepdims=False
+            ),
+            "za",
+        )
+    ).astype(bf16)
     joint = query_back(grad_queries, cosine, sine)
     attn_wide = jnp.concatenate(grad_attn, axis=0)
     normed_wide = jnp.concatenate(normed_slots, axis=0)
@@ -1012,25 +1019,18 @@
     running = after(low_term(1, ()), up_terms)
     moved_once = onward(running, "za")
     weight_terms = dot_rows(normed_wide, after(joint, running)).astype(bf16)
-    running = add_low(after(low_term(2, ()), weight_terms), moved_once)
+    small_sums = after(small_terms, running)
+    if paired:
+        small_sums = keep_and_swap(keep_and_swap(small_sums, "bx", 1), "yb", 0)
+    small_sum = small_sums.astype(f32)
+    running = add_low(after(low_term(2, ()), weight_terms, small_sums), moved_once)
     moved_twice = onward(running, "za")
     stages = []
     qkv_rows = to_rows(weight_terms, stages, (moved_once, ()))
-    if paired:
-        small_terms = keep_and_swap(after(small_terms, stages[1]), "yb", 1)
     grad_wup = columns([after(up_terms, running)], jnp.arange(group, dtype=jnp.int32), ring)
     running = add_low(after(low_term(3, (running, stages[:1])), stages[:2]), moved_twice)
     moved = onward(running, "za")
-    small_sum = sum(
-        part.astype(f32)
-        for part in rotate(
-            lambda i: lax.dynamic_index_in_dim(
-                after(small_terms, running, stages[2:]), i, 0, keepdims=False
-            ),
-            "za",
-        )
-    )
-    last = after(low_term(0, running), stages[2:], grad_wup, result, small_sum)
+    last = after(low_term(0, running), stages[2:], grad_wup, result)
     grad_normed = last.astype(f32) + moved.astype(f32)
     grad_wqkv = columns(qkv_rows, ((za - slot_ids) % ring).astype(jnp.int32), 3)
     weight_rows = triple_projector_matrix.astype(f32)

time: 815 us -> 819 us (level)
  waiting for transfers between devices: 337 us -> 350 us
    ppermute x9, waiting for transfers between devices: 32.1 us -> 51.3 us  [rotate(): came.append(lax.ppermute(pieces((me + far) % size), axis, route))]
    ppermute x18, waiting for transfers between devices: 225 us -> 206 us  [onward(): return lax.ppermute(block, axis, [(i, (i + 1) % size) for i in range(size)])]
    reduce_scatter x1, waiting for transfers between devices: 0.02 us -> 8.76 us  [per_device(): up_terms = lax.psum_scatter(up_terms, 'za', scatter_dimension=0, tiled=True)]
    convert_element_type x16 -> x15, other arithmetic: 25.5 us -> 22.2 us  [add_low(): return (left.astype(f32) + right.astype(f32)).astype(left.dtype)]
    unnamed x251 -> x241, local copies, waits for them, and re-layouts: 31.3 us -> 29.4 us
  transfers between devices with their start and end apart: 74 -> 74, of which waited for: 39 -> 41; matrix products, arithmetic and copies ran while one was open for 26% -> 25% of each run, Pallas kernels for 13% -> 12%
where the time goes in v5:
time: 819 us; the launch traced here: 809 us
  waiting for transfers between devices  350 us (43%)
  Pallas kernels  121 us (15%)
  matrix products  102 us (12%)
  local copies, waits for them, and re-layouts  80.5 us (10%)
  starting transfers between devices  72 us (9%)
  other arithmetic  66.3 us (8%)
  between operations  17.3 us (2%)
    ppermute x18, waiting for transfers between devices, onward(): return lax.ppermute(block, axis, [(i, (i + 1) % size) for i in range(size)])  206 us
    ppermute x38, waiting for transfers between devices, swap(): return lax.ppermute(block, axis, SWAP)  63.1 us
    ppermute x9, waiting for transfers between devices, rotate(): came.append(lax.ppermute(pieces((me + far) % size), axis, route))  51.3 us
    dot_general x6, matrix products, dot_rows(): lax.dot_general(left_mat, right_mat, (((0,), (0,)), ((), ())), preferred_...  43.6 us
    pallas_call x2, Pallas kernels, feed_down(): pl.pallas_call(functools.partial(feed_down_kernel, count, steps, len(pass...  43.6 us
    dot_general x12, matrix products, dot_cols(): lax.dot_general(left_mat, right_mat, (((1,), (1,)), ((), ())), preferred_...  36 us
    ppermute x38, starting transfers between devices, swap(): return lax.ppermute(block, axis, SWAP)  33.3 us
    unnamed x241, local copies, waits for them, and re-layouts  29.4 us
  transfers between devices with their start and end apart: 74, of which 41 were waited for; matrix products, arithmetic and copies ran while one was open for 25% of the time, Pallas kernels for 12%

profile of v5, /device:TPU:0, one launch (start us, length us, event | category | flops | bytes accessed | tf_op | source)
XLA Modules:
  0.0 809.4 jit_solution(13538607221319407296)
XLA Ops:
  30.2 11.3 %collective-permute-done.3 = bf16[1,64,1920]{2,1,0:T(8,128)(2,1)} collective-permute-done((bf16[1,64,1920]{2,1,0:T(8,128)(2,1)}, bf16[1,64,1920]{2,1,0:T(8,128)(2,1)}, u32[]{:S(2)}, u32[]{:S(2)}) %collective-permute-start.3) | collective-permute-done | bytes 245792 | tf_op jit(solution)/shard_map/ppermute | solution.py:99
  55.1 20.2 %collective-permute-done = bf16[256,2048]{1,0:T(8,128)(2,1)S(1)} collective-permute-done((bf16[256,2048]{1,0:T(8,128)(2,1)S(1)}, bf16[256,2048]{1,0:T(8,128)(2,1)S(1)}, u32[]{:S(2)}, u32[]{:S(2)}) %collective-permute-start) | collective-permute-done | bytes 1048608 | tf_op jit(solution)/shard_map/ppermute | solution.py:54
  76.8 24.2 %collective-permute-done.1 = bf16[256,2048]{1,0:T(8,128)(2,1)S(1)} collective-permute-done((bf16[256,2048]{1,0:T(8,128)(2,1)S(1)}, bf16[256,2048]{1,0:T(8,128)(2,1)S(1)}, u32[]{:S(2)}, u32[]{:S(2)}) %collective-permute-start.1) | collective-permute-done | bytes 1048608 | tf_op jit(solution)/shard_map/ppermute | solution.py:54
  102.4 23.8 %collective-permute-done.5 = bf16[256,2048]{1,0:T(8,128)(2,1)} collective-permute-done((bf16[256,2048]{1,0:T(8,128)(2,1)S(1)}, bf16[256,2048]{1,0:T(8,128)(2,1)}, u32[]{:S(2)}, u32[]{:S(2)}) %collective-permute-start.5) | collective-permute-done | bytes 1048608 | tf_op jit(solution)/shard_map/ppermute | solution.py:54
  161.7 11.3 %collective-permute-done.8.refs_11_.refs_19_.refs_6_.refs_10_ = bf16[2,128,1024]{2,1,0:T(8,128)(2,1)} collective-permute-done((bf16[2,128,1024]{2,1,0:T(8,128)(2,1)S(1)}, bf16[2,128,1024]{2,1,0:T(8,128)(2,1)}, u32[]{:S(2)}, u32[]{:S(2)}) %collective-permute-start.8) | collective-permute-done | bytes 524320 | tf_op jit(solution)/shard_map/ppermute | solution.py:54
  173.0 11.2 %collective-permute-done.9.refs_12_.refs_20_.refs_7_.refs_11_ = bf16[2,128,1024]{2,1,0:T(8,128)(2,1)} collective-permute-done((bf16[2,128,1024]{2,1,0:T(8,128)(2,1)S(1)}, bf16[2,128,1024]{2,1,0:T(8,128)(2,1)}, u32[]{:S(2)}, u32[]{:S(2)}) %collective-permute-start.9) | collective-permute-done | bytes 524320 | tf_op jit(solution)/shard_map/ppermute | solution.py:54
  184.2 15.8 %attend.1 = (f32[4,2,128,512]{3,2,1,0:T(8,128)}, bf16[4,2,128,512]{3,2,1,0:T(8,128)(2,1)}, f32[2,4,512,1]{3,2,1,0:T(8,128)}) custom-call(f32[2]{0:T(128)S(1)} %compare_convert_fusion.refs_0_, bf16[2,128,512]{2,1,0:T(8,128)(2,1)S(1)} %copy-done.4, bf16[2,128,512]{2,1,0:T(8,128)(2,1)S(1)} %copy-done.7, bf16[2,128,512]{2,1,0:T(8,128)(2,1)S(1)} %copy-done.10, ...), custom_call_target="tpu_custom_call" | custom-call | tf_op jit(solution)/shard_map/attend/pallas_call | solution.py:323
  210.0 17.0 %collective-permute-done.16 = bf16[256,2048]{1,0:T(8,128)(2,1)} collective-permute-done((bf16[256,2048]{1,0:T(8,128)(2,1)}, bf16[256,2048]{1,0:T(8,128)(2,1)}, u32[]{:S(2)}, u32[]{:S(2)}) %collective-permute-start.16) | collective-permute-done | bytes 1048608 | tf_op jit(solution)/shard_map/ppermute | solution.py:54
  232.2 19.5 %collective-permute-done.17 = bf16[256,2048]{1,0:T(8,128)(2,1)S(1)} collective-permute-done((bf16[256,2048]{1,0:T(8,128)(2,1)S(1)}, bf16[256,2048]{1,0:T(8,128)(2,1)S(1)}, u32[]{:S(2)}, u32[]{:S(2)}) %collective-permute-start.17) | collective-permute-done | bytes 1048608 | tf_op jit(solution)/shard_map/ppermute | solution.py:54
  257.5 16.1 %collective-permute-done.18 = bf16[256,2048]{1,0:T(8,128)(2,1)S(1)} collective-permute-done((bf16[256,2048]{1,0:T(8,128)(2,1)S(1)}, bf16[256,2048]{1,0:T(8,128)(2,1)S(1)}, u32[]{:S(2)}, u32[]{:S(2)}) %collective-permute-start.18) | collective-permute-done | bytes 1048608 | tf_op jit(solution)/shard_map/ppermute | solution.py:54
  310.5 11.7 %feed_up.2 = (bf16[2048,2048]{1,0:T(8,128)(2,1)}, bf16[2048,1024]{1,0:T(8,128)(2,1)}, f32[1024,4]{1,0:T(8,128)S(1)}, f32[1024,1024]{1,0:T(8,128)}) custom-call(bf16[512,2048]{1,0:T(8,128)(2,1)} %pad_maximum_fusion.2.refs_0_, bf16[512,2048]{1,0:T(8,128)(2,1)} %collective-permute-done.23.refs_1_, f32[1]{0:T(128)} %copy.205.refs_2_, f32[2048,1]{1,0:T(8,128)S(1)} %copy-done.1, ...), custom_call_target="tpu_custom_call" | custom-call | flops 4294967296 | bytes 16777216 | tf_op jit(solution)/shard_map/feed_up/pallas_call | solution.py:517
  332.6 11.1 %feed_up.3 = (bf16[2048,2048]{1,0:T(8,128)(2,1)}, bf16[2048,1024]{1,0:T(8,128)(2,1)}, f32[1024,4]{1,0:T(8,128)S(1)}, f32[1024,1024]{1,0:T(8,128)}) custom-call(bf16[512,2048]{1,0:T(8,128)(2,1)S(1)} %constant_dynamic-update-slice_fusion.8.refs_0_, bf16[512,2048]{1,0:T(8,128)(2,1)} %copy-done.74, ...), custom_call_target="tpu_custom_call", output_to_operand_aliasing={{0}: (7, {}), {1}: (8, {})} | custom-call | flops 4294967296 | bytes 16777216 | tf_op jit(solution)/shard_map/feed_up/pallas_call | solution.py:517
  344.5 14.6 %all-gather.10.cloned.1.call-done.refs_5_ = bf16[1024,2048]{1,0:T(8,128)(2,1)} async-done(((bf16[256,2048]{1,0:T(8,128)(2,1)}), bf16[1024,2048]{1,0:T(8,128)(2,1)}) %all-gather.10.cloned.1.call-update) | async-done | bytes 4194320 | tf_op jit(solution)/shard_map/all_gather | solution.py:770
  359.1 14.1 %convolution_convert_fusion.1 = bf16[1024,2048]{1,0:T(8,128)(2,1)} fusion(bf16[2048,1024]{1,0:T(8,128)(2,1)} %get-tuple-element.136.refs_3_, bf16[2048,2048]{1,0:T(8,128)(2,1)} %copy-done.96), kind=kOutput, calls=%fused_computation.22 | convolution fusion | flops 8592031744 | bytes 16777216 | tf_op jit(solution)/shard_map/dot_general | solution.py:41
  374.3 21.9 %feed_down.2 = (bf16[2048,1024]{1,0:T(8,128)(2,1)}, f32[512,4]{1,0:T(8,128)S(1)}, f32[512,4]{1,0:T(8,128)S(1)}, bf16[512,2048]{1,0:T(8,128)(2,1)S(1)}, bf16[512,...) custom-call(bf16[2048,2048]{1,0:T(8,128)(2,1)} %copy-done.96, f32[1024,4]{1,0:T(8,128)S(1)} %copy-done.28, ...), custom_call_target="tpu_custom_call" | custom-call | flops 12884901888 | bytes 25165824 | tf_op jit(solution)/shard_map/feed_down/pallas_call | solution.py:556
  410.5 21.6 %feed_down.3 = (bf16[2048,1024]{1,0:T(8,128)(2,1)}, f32[512,4]{1,0:T(8,128)S(1)}, f32[512,4]{1,0:T(8,128)S(1)}, bf16[512,2048]{1,0:T(8,128)(2,1)S(1)}, bf16[512,...) custom-call(bf16[2048,2048]{1,0:T(8,128)(2,1)} %copy-done.96, ...), custom_call_target="tpu_custom_call", output_to_operand_aliasing={{0}: (6, {})} | custom-call | flops 12884901888 | bytes 25165824 | tf_op jit(solution)/shard_map/feed_down/pallas_call | solution.py:556
  453.5 10.2 %collective-permute-done.34 = f32[128,4]{1,0:T(8,128)} collective-permute-done((f32[128,4]{1,0:T(8,128)}, f32[128,4]{1,0:T(8,128)}, u32[]{:S(2)}, u32[]{:S(2)}) %collective-permute-start.34) | collective-permute-done | bytes 2080 | tf_op jit(solution)/shard_map/ppermute | solution.py:115
  479.1 14.0 %convolution_convert_fusion.2 = bf16[2048,1024]{1,0:T(8,128)(2,1)} fusion(bf16[2048,2048]{1,0:T(8,128)(2,1)} %get-tuple-element.166, bf16[2048,1024]{1,0:T(8,128)(2,1)} %get-tuple-element.168), kind=kOutput, calls=%fused_computation.23 | convolution fusion | flops 8592031744 | bytes 16777216 | tf_op jit(solution)/shard_map/dot_general | solution.py:41
  496.2 10.1 %collective-permute-done.43 = bf16[256,2048]{1,0:T(8,128)(2,1)} collective-permute-done((bf16[256,2048]{1,0:T(8,128)(2,1)}, bf16[256,2048]{1,0:T(8,128)(2,1)}, u32[]{:S(2)}, u32[]{:S(2)}) %collective-permute-start.43) | collective-permute-done | bytes 1048608 | tf_op jit(solution)/shard_map/ppermute | solution.py:54
  520.3 12.8 %collective-permute-done.44 = bf16[256,2048]{1,0:T(8,128)(2,1)} collective-permute-done((bf16[256,2048]{1,0:T(8,128)(2,1)}, bf16[256,2048]{1,0:T(8,128)(2,1)}, u32[]{:S(2)}, u32[]{:S(2)}) %collective-permute-start.44) | collective-permute-done | bytes 1048608 | tf_op jit(solution)/shard_map/ppermute | solution.py:54
  543.0 9.3 %collective-permute-done.42 = bf16[128,2048]{1,0:T(8,128)(2,1)S(1)} collective-permute-done((bf16[128,2048]{1,0:T(8,128)(2,1)S(1)}, bf16[128,2048]{1,0:T(8,128)(2,1)S(1)}, u32[]{:S(2)}, u32[]{:S(2)}) %collective-permute-start.42) | collective-permute-done | bytes 524320 | tf_op jit(solution)/shard_map/ppermute | solution.py:115
  557.0 13.6 %collective-permute-done.45 = bf16[256,2048]{1,0:T(8,128)(2,1)} collective-permute-done((bf16[256,2048]{1,0:T(8,128)(2,1)}, bf16[256,2048]{1,0:T(8,128)(2,1)}, u32[]{:S(2)}, u32[]{:S(2)}) %collective-permute-start.45) | collective-permute-done | bytes 1048608 | tf_op jit(solution)/shard_map/ppermute | solution.py:54
  580.1 12.4 %attend_back_far.1 = (f32[4,2,128,512]{3,2,1,0:T(8,128)}, bf16[4,2,128,512]{3,2,1,0:T(8,128)(2,1)S(1)}, bf16[4,2,128,512]{3,2,1,0:T(8,128)(2,1)}) custom-call(bf16[2,128,512]{2,1,0:T(8,128)(2,1)S(1)} %copy-done.5, bf16[2,128,512]{2,1,0:T(8,128)(2,1)S(1)} %copy-done.8, bf16[2,128,512]{2,1,0:T(8,128)(2,1)S(1)} %copy-done.11, ...), custom_call_target="tpu_custom_call" | custom-call | tf_op jit(solution)/shard_map/attend_back_far/pallas_call | solution.py:396
  598.8 12.7 %attend_back.1 = (f32[4,2,128,512]{3,2,1,0:T(8,128)}, bf16[4,2,128,512]{3,2,1,0:T(8,128)(2,1)S(1)}, bf16[4,2,128,512]{3,2,1,0:T(8,128)(2,1)}) custom-call(bf16[2,128,512]{2,1,0:T(8,128)(2,1)S(1)} %copy-done.5, bf16[2,128,512]{2,1,0:T(8,128)(2,1)S(1)} %copy-done.8, bf16[2,128,512]{2,1,0:T(8,128)(2,1)S(1)} %copy-done.11, bf16[2,128,512]{2,1,0:T(8,128)(2,1)S(1)} %copy-done.14, ...), custom_call_target="tpu_custom_call" | custom-call | tf_op jit(solution)/shard_map/attend_back/pallas_call | solution.py:396
  616.3 10.7 %collective-permute-done.50 = bf16[2,2,80,256]{3,2,0,1:T(8,128)(2,1)S(1)} collective-permute-done((bf16[2,2,80,256]{3,2,0,1:T(8,128)(2,1)S(1)}, bf16[2,2,80,256]{3,2,0,1:T(8,128)(2,1)S(1)}, u32[]{:S(2)}, u32[]{:S(2)}) %collective-permute-start.50) | collective-permute-done | bytes 163872 | tf_op jit(solution)/shard_map/ppermute | solution.py:99
  628.0 11.8 %collective-permute-done.48.refs_2_ = bf16[4,2,128,512]{3,2,1,0:T(8,128)(2,1)S(1)} collective-permute-done((bf16[4,2,128,512]{3,2,1,0:T(8,128)(2,1)}, bf16[4,2,128,512]{3,2,1,0:T(8,128)(2,1)S(1)}, u32[]{:S(2)}, u32[]{:S(2)}) %collective-permute-start.48) | collective-permute-done | bytes 1048608 | tf_op jit(solution)/shard_map/ppermute | solution.py:54
  646.4 8.8 %reduce-scatter.6.cloned.1.call-done = bf16[512,1024]{1,0:T(8,128)(2,1)} async-done(((bf16[2048,1024]{1,0:T(8,128)(2,1)}), bf16[512,1024]{1,0:T(8,128)(2,1)}) %reduce-scatter.6.cloned.1.call-update) | async-done | bytes 1048592 | tf_op jit(solution)/shard_map/reduce_scatter | solution.py:932
  674.5 9.3 %convolution_convert_fusion = bf16[2048,1536]{1,0:T(8,128)(2,1)S(1)} fusion(bf16[1024,1536]{1,0:T(8,128)(2,1)} %bitcast.228, bf16[256,2048]{1,0:T(8,128)(2,1)} %copy-done.85, bf16[256,2048]{1,0:T(8,128)(2,1)} %copy-done.84, bf16[256,2048]{1,0:T(8,128)(2,1)S(1)} %copy-done.83, bf16[256,2048]{1,0:T(8,128)(2,1)S(1)} %copy-done.81), kind=kOutput, calls=%fused_computation | convolution fusion | flops 6462373888 | bytes 13631488 | tf_op jit(solution)/shard_map/dot_general | solution.py:41
  707.4 11.9 %collective-permute-done.54 = bf16[256,2048]{1,0:T(8,128)(2,1)S(1)} collective-permute-done((bf16[256,2048]{1,0:T(8,128)(2,1)}, bf16[256,2048]{1,0:T(8,128)(2,1)S(1)}, u32[]{:S(2)}, u32[]{:S(2)}) %collective-permute-start.54) | collective-permute-done | bytes 1048608 | tf_op jit(solution)/shard_map/ppermute | solution.py:54
  735.5 7.0 collective-permute-done.56
  744.0 7.0 collective-permute-done.57
  764.7 18.7 %collective-permute-done.64.refs_4_ = bf16[1,64,1536]{2,1,0:T(8,128)(2,1)S(1)} collective-permute-done((bf16[1,64,1536]{2,1,0:T(8,128)(2,1)S(1)}, bf16[1,64,1536]{2,1,0:T(8,128)(2,1)S(1)}, u32[]{:S(2)}, u32[]{:S(2)}) %collective-permute-start.64) | collective-permute-done | bytes 196640 | tf_op jit(solution)/shard_map/ppermute | solution.py:99
  (575 shorter events, 346.2 us)
Async XLA Ops:
  7.2 119.0 %all-gather.6.cloned.1.call-start = ((), (), s32[]{:S(2)}) async-start(), calls=%async_computation.5 | async-start | bytes 2359296 | tf_op jit(solution)/shard_map/all_gather | solution.py:697
  26.1 100.1 %all-gather.12.cloned.1.call-start = ((), (), s32[]{:S(2)}) async-start(), calls=%async_computation.11 | async-start | bytes 8847360 | tf_op jit(solution)/shard_map/all_gather | solution.py:688
  47.1 162.9 %all-gather.8.cloned.1.call-start = ((), (), s32[]{:S(2)}) async-start(), calls=%async_computation.6 | async-start | bytes 5242880 | tf_op jit(solution)/shard_map/all_gather | solution.py:700
  48.4 26.8 %collective-permute-start = (bf16[256,2048]{1,0:T(8,128)(2,1)S(1)}, bf16[256,2048]{1,0:T(8,128)(2,1)S(1)}, u32[]{:S(2)}, u32[]{:S(2)}) collective-permute-start(bf16[256,2048]{1,0:T(8,128)(2,1)S(1)} %bitcast.219), channel_id=1, source_target_pairs={{0,8},{8,16},{16,24},{24,0},{1,9},{9,17},{17,25},{25,1},{2,10},{10... | collective-permute-start | bytes 3145736 | tf_op jit(solution)/shard_map/ppermute | solution.py:54
  52.4 100.8 %collective-permute-start.11 = (bf16[128,2048]{1,0:T(8,128)(2,1)}, bf16[128,2048]{1,0:T(8,128)(2,1)}, u32[]{:S(2)}, u32[]{:S(2)}) collective-permute-start(bf16[128,2048]{1,0:T(8,128)(2,1)} %get-tuple-element.323), channel_id=1, source_target_pairs={{0,4},{4,0},{1,5},{5,1},{2,6},{6,2},{3,7},{7,3},{8,12},{12,8},{9,1... | collective-permute-start | bytes 1572872 | tf_op jit(solution)/shard_map/ppermute | solution.py:115
  53.5 102.7 %collective-permute-start.10 = (bf16[128,2048]{1,0:T(8,128)(2,1)}, bf16[128,2048]{1,0:T(8,128)(2,1)}, u32[]{:S(2)}, u32[]{:S(2)}) collective-permute-start(bf16[128,2048]{1,0:T(8,128)(2,1)} %get-tuple-element.324), channel_id=1, source_target_pairs={{0,2},{2,0},{1,3},{3,1},{4,6},{6,4},{5,7},{7,5},{8,10},{10,8},{9,1... | collective-permute-start | bytes 1572872 | tf_op jit(solution)/shard_map/ppermute | solution.py:115
  126.2 233.0 %all-gather.10.cloned.1.call-start = ((), (), s32[]{:S(2)}) async-start(), calls=%async_computation.7 | async-start | bytes 5242880 | tf_op jit(solution)/shard_map/all_gather | solution.py:770
  145.8 27.2 %collective-permute-start.8 = (bf16[2,128,1024]{2,1,0:T(8,128)(2,1)S(1)}, bf16[2,128,1024]{2,1,0:T(8,128)(2,1)}, u32[]{:S(2)}, u32[]{:S(2)}) collective-permute-start(bf16[2,128,1024]{2,1,0:T(8,128)(2,1)S(1)} %get-tuple-element.121.refs_7_.refs_15_.refs_6_.refs_10_), channel_id=1, source_target_pairs={{0,4},{4,0},{1,5},{5,1},{2,6},{6,2},{3,7},{7,3},{8,12},{12,8},{9,1... | collective-permute-start | bytes 1572872 | tf_op jit(solution)/shard_map/ppermute | solution.py:54
  153.2 31.0 %collective-permute-start.9 = (bf16[2,128,1024]{2,1,0:T(8,128)(2,1)S(1)}, bf16[2,128,1024]{2,1,0:T(8,128)(2,1)}, u32[]{:S(2)}, u32[]{:S(2)}) collective-permute-start(bf16[2,128,1024]{2,1,0:T(8,128)(2,1)S(1)} %get-tuple-element.124.refs_8_.refs_16_.refs_7_.refs_11_), channel_id=1, source_target_pairs={{0,4},{4,0},{1,5},{5,1},{2,6},{6,2},{3,7},{7,3},{8,12},{12,8},{9,1... | collective-permute-start | bytes 1572872 | tf_op jit(solution)/shard_map/ppermute | solution.py:54
  156.3 51.3 %collective-permute-start.14 = (bf16[256,2048]{1,0:T(8,128)(2,1)S(1)}, bf16[256,2048]{1,0:T(8,128)(2,1)S(1)}, u32[]{:S(2)}, u32[]{:S(2)}) collective-permute-start(bf16[256,2048]{1,0:T(8,128)(2,1)S(1)} %pad_maximum_fusion.4), channel_id=1, source_target_pairs={{0,2},{2,0},{1,3},{3,1},{4,6},{6,4},{5,7},{7,5},{8,10},{10,8},{9,1... | collective-permute-start | bytes 3145736 | tf_op jit(solution)/shard_map/ppermute | solution.py:115
  157.9 49.6 %collective-permute-start.13 = (bf16[256,2048]{1,0:T(8,128)(2,1)S(1)}, bf16[256,2048]{1,0:T(8,128)(2,1)S(1)}, u32[]{:S(2)}, u32[]{:S(2)}) collective-permute-start(bf16[256,2048]{1,0:T(8,128)(2,1)S(1)} %pad_maximum_fusion.3), channel_id=1, source_target_pairs={{0,4},{4,0},{1,5},{5,1},{2,6},{6,2},{3,7},{7,3},{8,12},{12,8},{9,1... | collective-permute-start | bytes 3145736 | tf_op jit(solution)/shard_map/ppermute | solution.py:115
  207.5 45.0 %collective-permute-start.12 = (bf16[512,2048]{1,0:T(8,128)(2,1)}, bf16[512,2048]{1,0:T(8,128)(2,1)}, u32[]{:S(2)}, u32[]{:S(2)}) collective-permute-start(bf16[512,2048]{1,0:T(8,128)(2,1)} %pad_maximum_fusion), channel_id=1, source_target_pairs={{0,1},{1,0},{2,3},{3,2},{4,5},{5,4},{6,7},{7,6},{8,9},{9,8},{10,11... | collective-permute-start | bytes 6291464 | tf_op jit(solution)/shard_map/ppermute | solution.py:115
  209.5 46.2 %collective-permute-start.15 = (bf16[512,2048]{1,0:T(8,128)(2,1)}, bf16[512,2048]{1,0:T(8,128)(2,1)}, u32[]{:S(2)}, u32[]{:S(2)}) collective-permute-start(bf16[512,2048]{1,0:T(8,128)(2,1)} %pad_maximum_fusion.1), channel_id=1, source_target_pairs={{0,1},{1,0},{2,3},{3,2},{4,5},{5,4},{6,7},{7,6},{8,9},{9,8},{10,11... | collective-permute-start | bytes 6291464 | tf_op jit(solution)/shard_map/ppermute | solution.py:115
  281.4 196.7 %reduce-scatter.4.cloned.1.call-start = ((), (), s32[]{:S(2)}) async-start(), calls=%async_computation.8 | async-start | bytes 5242880 | tf_op jit(solution)/shard_map/reduce_scatter | solution.py:818
  294.8 27.4 %collective-permute-start.22 = (bf16[256,2048]{1,0:T(8,128)(2,1)}, bf16[256,2048]{1,0:T(8,128)(2,1)}, u32[]{:S(2)}, u32[]{:S(2)}) collective-permute-start(bf16[256,2048]{1,0:T(8,128)(2,1)} %pad_maximum_fusion.6), channel_id=1, source_target_pairs={{0,2},{2,0},{1,3},{3,1},{4,6},{6,4},{5,7},{7,5},{8,10},{10,8},{9,1... | collective-permute-start | bytes 3145736 | tf_op jit(solution)/shard_map/ppermute | solution.py:115
  399.0 256.2 %reduce-scatter.6.cloned.1.call-start = ((), (), s32[]{:S(2)}) async-start(), calls=%async_computation.9 | async-start | bytes 5242880 | tf_op jit(solution)/shard_map/reduce_scatter | solution.py:932
  478.2 28.1 %collective-permute-start.43 = (bf16[256,2048]{1,0:T(8,128)(2,1)}, bf16[256,2048]{1,0:T(8,128)(2,1)}, u32[]{:S(2)}, u32[]{:S(2)}) collective-permute-start(bf16[256,2048]{1,0:T(8,128)(2,1)} %get-tuple-element.161), channel_id=1, source_target_pairs={{0,8},{8,16},{16,24},{24,0},{1,9},{9,17},{17,25},{25,1},{2,10},{10... | collective-permute-start | bytes 3145736 | tf_op jit(solution)/shard_map/ppermute | solution.py:54
  478.6 37.3 %collective-permute-start.37 = (bf16[512,2048]{1,0:T(8,128)(2,1)}, bf16[512,2048]{1,0:T(8,128)(2,1)}, u32[]{:S(2)}, u32[]{:S(2)}) collective-permute-start(bf16[512,2048]{1,0:T(8,128)(2,1)} %get-tuple-element.163), channel_id=1, source_target_pairs={{0,1},{1,0},{2,3},{3,2},{4,5},{5,4},{6,7},{7,6},{8,9},{9,8},{10,11... | collective-permute-start | bytes 6291464 | tf_op jit(solution)/shard_map/ppermute | solution.py:115
  506.2 26.9 %collective-permute-start.44 = (bf16[256,2048]{1,0:T(8,128)(2,1)}, bf16[256,2048]{1,0:T(8,128)(2,1)}, u32[]{:S(2)}, u32[]{:S(2)}) collective-permute-start(bf16[256,2048]{1,0:T(8,128)(2,1)} %collective-permute-done.43), channel_id=1, source_target_pairs={{0,8},{8,16},{16,24},{24,0},{1,9},{9,17},{17,25},{25,1},{2,10},{10... | collective-permute-start | bytes 3145736 | tf_op jit(solution)/shard_map/ppermute | solution.py:54
  507.7 28.6 %collective-permute-start.39 = (bf16[256,2048]{1,0:T(8,128)(2,1)}, bf16[256,2048]{1,0:T(8,128)(2,1)}, u32[]{:S(2)}, u32[]{:S(2)}) collective-permute-start(bf16[256,2048]{1,0:T(8,128)(2,1)} %get-tuple-element.309), channel_id=1, source_target_pairs={{0,4},{4,0},{1,5},{5,1},{2,6},{6,2},{3,7},{7,3},{8,12},{12,8},{9,1... | collective-permute-start | bytes 3145736 | tf_op jit(solution)/shard_map/ppermute | solution.py:115
  509.2 27.2 %collective-permute-start.41 = (bf16[256,2048]{1,0:T(8,128)(2,1)}, bf16[256,2048]{1,0:T(8,128)(2,1)}, u32[]{:S(2)}, u32[]{:S(2)}) collective-permute-start(bf16[256,2048]{1,0:T(8,128)(2,1)} %get-tuple-element.310), channel_id=1, source_target_pairs={{0,2},{2,0},{1,3},{3,1},{4,6},{6,4},{5,7},{7,5},{8,10},{10,8},{9,1... | collective-permute-start | bytes 3145736 | tf_op jit(solution)/shard_map/ppermute | solution.py:115
  542.9 27.7 %collective-permute-start.45 = (bf16[256,2048]{1,0:T(8,128)(2,1)}, bf16[256,2048]{1,0:T(8,128)(2,1)}, u32[]{:S(2)}, u32[]{:S(2)}) collective-permute-start(bf16[256,2048]{1,0:T(8,128)(2,1)} %collective-permute-done.44), channel_id=1, source_target_pairs={{0,8},{8,16},{16,24},{24,0},{1,9},{9,17},{17,25},{25,1},{2,10},{10... | collective-permute-start | bytes 3145736 | tf_op jit(solution)/shard_map/ppermute | solution.py:54
  570.6 133.0 %reduce-scatter.8.cloned.1.call-start = ((), (), s32[]{:S(2)}) async-start(), calls=%async_computation.10 | async-start | bytes 2359296 | tf_op jit(solution)/shard_map/reduce_scatter | solution.py:1008
  592.6 34.5 %collective-permute-start.47 = (bf16[4,2,128,512]{3,2,1,0:T(8,128)(2,1)S(1)}, bf16[4,2,128,512]{3,2,1,0:T(8,128)(2,1)S(1)}, u32[]{:S(2)}, u32[]{:S(2)}) collective-permute-start(bf16[4,2,128,512]{3,2,1,0:T(8,128)(2,1)S(1)} %get-tuple-element.187), channel_id=1, source_target_pairs={{0,4},{4,0},{1,5},{5,1},{2,6},{6,2},{3,7},{7,3},{8,12},{12,8},{9,1... | collective-permute-start | bytes 3145736 | tf_op jit(solution)/shard_map/ppermute | solution.py:54
  593.0 46.9 %collective-permute-start.48 = (bf16[4,2,128,512]{3,2,1,0:T(8,128)(2,1)}, bf16[4,2,128,512]{3,2,1,0:T(8,128)(2,1)S(1)}, u32[]{:S(2)}, u32[]{:S(2)}) collective-permute-start(bf16[4,2,128,512]{3,2,1,0:T(8,128)(2,1)} %get-tuple-element.189), channel_id=1, source_target_pairs={{0,4},{4,0},{1,5},{5,1},{2,6},{6,2},{3,7},{7,3},{8,12},{12,8},{9,1... | collective-permute-start | bytes 3145736 | tf_op jit(solution)/shard_map/ppermute | solution.py:54
  598.5 28.4 %collective-permute-start.50 = (bf16[2,2,80,256]{3,2,0,1:T(8,128)(2,1)S(1)}, bf16[2,2,80,256]{3,2,0,1:T(8,128)(2,1)S(1)}, u32[]{:S(2)}, u32[]{:S(2)}) collective-permute-start(bf16[2,2,80,256]{3,2,0,1:T(8,128)(2,1)S(1)} %get-tuple-element.335), channel_id=1, source_target_pairs={{0,16},{8,24},{16,0},{24,8},{1,17},{9,25},{17,1},{25,9},{2,18},{10... | collective-permute-start | bytes 491528 | tf_op jit(solution)/shard_map/ppermute | solution.py:99
  687.3 32.0 %collective-permute-start.55 = (bf16[4,2,2,64,1536]{4,3,0,1,2:T(8,128)(2,1)}, bf16[4,2,2,64,1536]{4,3,0,1,2:T(8,128)(2,1)}, u32[]{:S(2)}, u32[]{:S(2)}) collective-permute-start(bf16[4,2,2,64,1536]{4,3,0,1,2:T(8,128)(2,1)} %copy_bitcast_fusion), channel_id=1, source_target_pairs={{0,1},{1,0},{2,3},{3,2},{4,5},{5,4},{6,7},{7,6},{8,9},{9,8},{10,11... | collective-permute-start | bytes 9437192 | tf_op jit(solution)/shard_map/ppermute | solution.py:115
  691.5 27.8 %collective-permute-start.54 = (bf16[256,2048]{1,0:T(8,128)(2,1)}, bf16[256,2048]{1,0:T(8,128)(2,1)S(1)}, u32[]{:S(2)}, u32[]{:S(2)}) collective-permute-start(bf16[256,2048]{1,0:T(8,128)(2,1)} %fusion.45), channel_id=1, source_target_pairs={{0,8},{8,16},{16,24},{24,0},{1,9},{9,17},{17,25},{25,1},{2,10},{10... | collective-permute-start | bytes 3145736 | tf_op jit(solution)/shard_map/ppermute | solution.py:54
  725.6 26.1 %collective-permute-start.58 = (bf16[256,2048]{1,0:T(8,128)(2,1)S(1)}, bf16[256,2048]{1,0:T(8,128)(2,1)S(1)}, u32[]{:S(2)}, u32[]{:S(2)}) collective-permute-start(bf16[256,2048]{1,0:T(8,128)(2,1)S(1)} %add_convert_fusion.5), channel_id=1, source_target_pairs={{0,8},{8,16},{16,24},{24,0},{1,9},{9,17},{17,25},{25,1},{2,10},{10... | collective-permute-start | bytes 3145736 | tf_op jit(solution)/shard_map/ppermute | solution.py:54
  752.2 45.8 %collective-permute-start.61 = (bf16[256,2048]{1,0:T(8,128)(2,1)S(1)}, bf16[256,2048]{1,0:T(8,128)(2,1)S(1)}, u32[]{:S(2)}, u32[]{:S(2)}) collective-permute-start(bf16[256,2048]{1,0:T(8,128)(2,1)S(1)} %add_convert_fusion.4), channel_id=1, source_target_pairs={{0,8},{8,16},{16,24},{24,0},{1,9},{9,17},{17,25},{25,1},{2,10},{10... | collective-permute-start | bytes 3145736 | tf_op jit(solution)/shard_map/ppermute | solution.py:54
  760.7 27.0 %collective-permute-start.62 = (bf16[1,64,1536]{2,1,0:T(8,128)(2,1)S(1)}, bf16[1,64,1536]{2,1,0:T(8,128)(2,1)S(1)}, u32[]{:S(2)}, u32[]{:S(2)}) collective-permute-start(bf16[1,64,1536]{2,1,0:T(8,128)(2,1)S(1)} %get-tuple-element.331), channel_id=1, source_target_pairs={{0,8},{8,16},{16,24},{24,0},{1,9},{9,17},{17,25},{25,1},{2,10},{10... | collective-permute-start | bytes 589832 | tf_op jit(solution)/shard_map/ppermute | solution.py:99
  761.3 32.7 %collective-permute-start.63 = (bf16[1,64,1536]{2,1,0:T(8,128)(2,1)S(1)}, bf16[1,64,1536]{2,1,0:T(8,128)(2,1)S(1)}, u32[]{:S(2)}, u32[]{:S(2)}) collective-permute-start(bf16[1,64,1536]{2,1,0:T(8,128)(2,1)S(1)} %get-tuple-element.332), channel_id=1, source_target_pairs={{0,16},{8,24},{16,0},{24,8},{1,17},{9,25},{17,1},{25,9},{2,18},{10... | collective-permute-start | bytes 589832 | tf_op jit(solution)/shard_map/ppermute | solution.py:99
  (156 other events, 1961.5 us)
Sparse Core Ops, SparseCore 0:
  9.9 36.2 all-gather.5
  48.7 59.3 all-gather.11
  126.3 80.0 all-gather.7
  281.6 77.5 all-gather.9
  399.1 75.4 reduce-scatter.3
  570.8 84.3 reduce-scatter.5
  659.0 44.5 reduce-scatter.7

commit v6 on v3

--- a/solution.py
+++ b/solution.py
@@ -930,9 +930,7 @@
     grad_attn[3] = after(grad_attn[3], result, small_terms)
     up_terms = after(up_terms, grad_attn[3])
     up_terms = lax.psum_scatter(up_terms, "za", scatter_dimension=0, tiled=True)
-    up_terms = lax.all_to_all(
-        up_terms.reshape(group, rows, units), PLANE, 0, 0, tiled=True
-    )
+    up_sums = up_terms
     grad_heads = [
         (dot_cols(block, out_own) * active_rows)
         .astype(bf16)
@@ -1009,23 +1007,26 @@
         terms = query_terms[s * tokens : (s + 1) * tokens] + dot_cols(rows_of, both_own)
         return terms.astype(bf16)
 
-    running = after(low_term(1, ()), up_terms)
+    running = after(low_term(1, ()), up_sums)
     moved_once = onward(running, "za")
     weight_terms = dot_rows(normed_wide, after(joint, running)).astype(bf16)
     running = add_low(after(low_term(2, ()), weight_terms), moved_once)
     moved_twice = onward(running, "za")
     stages = []
-    qkv_rows = to_rows(weight_terms, stages, (moved_once, ()))
+    qkv_rows = to_rows(weight_terms, stages, (moved_once, moved_twice))
     if paired:
-        small_terms = keep_and_swap(after(small_terms, stages[1]), "yb", 1)
-    grad_wup = columns([after(up_terms, running)], jnp.arange(group, dtype=jnp.int32), ring)
-    running = add_low(after(low_term(3, (running, stages[:1])), stages[:2]), moved_twice)
+        small_terms = keep_and_swap(after(small_terms, stages[0]), "yb", 1)
+    up_terms = lax.all_to_all(
+        after(up_sums, moved_once, stages[:1]).reshape(group, rows, units), PLANE, 0, 0, tiled=True
+    )
+    grad_wup = columns([up_terms], jnp.arange(group, dtype=jnp.int32), ring)
+    running = add_low(after(low_term(3, (running, stages[:1])), stages[:1]), moved_twice)
     moved = onward(running, "za")
     small_sum = sum(
         part.astype(f32)
         for part in rotate(
             lambda i: lax.dynamic_index_in_dim(
-                after(small_terms, running, stages[2:]), i, 0, keepdims=False
+                after(small_terms, running), i, 0, keepdims=False
             ),
             "za",
         )

time: 815 us -> 816 us (level)
  waiting for transfers between devices: 337 us -> 321 us
  other arithmetic: 73.6 us -> 84.1 us
    ppermute x9, waiting for transfers between devices: 32.1 us -> 20.7 us  [rotate(): came.append(lax.ppermute(pieces((me + far) % size), axis, route))]
    unnamed x251 -> x261, local copies, waits for them, and re-layouts: 31.3 us -> 32 us
  transfers between devices with their start and end apart: 74 -> 74, of which waited for: 39 -> 38; matrix products, arithmetic and copies ran while one was open for 26% -> 29% of each run, Pallas kernels for 13% -> 12%
where the time goes in v6:
time: 816 us; the launch traced here: 806 us
  waiting for transfers between devices  321 us (39%)
  Pallas kernels  122 us (15%)
  matrix products  108 us (13%)
  local copies, waits for them, and re-layouts  88.2 us (11%)
  other arithmetic  84.1 us (10%)
  starting transfers between devices  65.2 us (8%)
  between operations  17.3 us (2%)
    ppermute x18, waiting for transfers between devices, onward(): return lax.ppermute(block, axis, [(i, (i + 1) % size) for i in range(size)])  227 us
    ppermute x38, waiting for transfers between devices, swap(): return lax.ppermute(block, axis, SWAP)  53.1 us
    pallas_call x2, Pallas kernels, feed_down(): pl.pallas_call(functools.partial(feed_down_kernel, count, steps, len(pass...  43.5 us
    dot_general x6, matrix products, dot_rows(): lax.dot_general(left_mat, right_mat, (((0,), (0,)), ((), ())), preferred_...  43.2 us
    dot_general x12, matrix products, dot_cols(): lax.dot_general(left_mat, right_mat, (((1,), (1,)), ((), ())), preferred_...  42.2 us
    ppermute x38, starting transfers between devices, swap(): return lax.ppermute(block, axis, SWAP)  33.6 us
    convert_element_type x16, other arithmetic, add_low(): return (left.astype(f32) + right.astype(f32)).astype(left.dtype)  33.2 us
    unnamed x261, local copies, waits for them, and re-layouts  32 us
  transfers between devices with their start and end apart: 74, of which 38 were waited for; matrix products, arithmetic and copies ran while one was open for 29% of the time, Pallas kernels for 12%

profile of v6, /device:TPU:0, one launch (start us, length us, event | category | flops | bytes accessed | tf_op | source)
XLA Modules:
  0.0 806.3 jit_solution(8349337519911703865)
XLA Ops:
  30.2 11.3 %collective-permute-done.3 = bf16[1,64,1920]{2,1,0:T(8,128)(2,1)} collective-permute-done((bf16[1,64,1920]{2,1,0:T(8,128)(2,1)}, bf16[1,64,1920]{2,1,0:T(8,128)(2,1)}, u32[]{:S(2)}, u32[]{:S(2)}) %collective-permute-start.3) | collective-permute-done | bytes 245792 | tf_op jit(solution)/shard_map/ppermute | solution.py:99
  55.0 20.2 %collective-permute-done = bf16[256,2048]{1,0:T(8,128)(2,1)S(1)} collective-permute-done((bf16[256,2048]{1,0:T(8,128)(2,1)S(1)}, bf16[256,2048]{1,0:T(8,128)(2,1)S(1)}, u32[]{:S(2)}, u32[]{:S(2)}) %collective-permute-start) | collective-permute-done | bytes 1048608 | tf_op jit(solution)/shard_map/ppermute | solution.py:54
  76.8 24.2 %collective-permute-done.1 = bf16[256,2048]{1,0:T(8,128)(2,1)S(1)} collective-permute-done((bf16[256,2048]{1,0:T(8,128)(2,1)S(1)}, bf16[256,2048]{1,0:T(8,128)(2,1)S(1)}, u32[]{:S(2)}, u32[]{:S(2)}) %collective-permute-start.1) | collective-permute-done | bytes 1048608 | tf_op jit(solution)/shard_map/ppermute | solution.py:54
  102.3 23.8 %collective-permute-done.5 = bf16[256,2048]{1,0:T(8,128)(2,1)} collective-permute-done((bf16[256,2048]{1,0:T(8,128)(2,1)S(1)}, bf16[256,2048]{1,0:T(8,128)(2,1)}, u32[]{:S(2)}, u32[]{:S(2)}) %collective-permute-start.5) | collective-permute-done | bytes 1048608 | tf_op jit(solution)/shard_map/ppermute | solution.py:54
  127.9 6.7 fusion.148.joint_ref
  161.6 11.3 %collective-permute-done.8.refs_11_.refs_19_.refs_6_.refs_10_ = bf16[2,128,1024]{2,1,0:T(8,128)(2,1)} collective-permute-done((bf16[2,128,1024]{2,1,0:T(8,128)(2,1)S(1)}, bf16[2,128,1024]{2,1,0:T(8,128)(2,1)}, u32[]{:S(2)}, u32[]{:S(2)}) %collective-permute-start.8) | collective-permute-done | bytes 524320 | tf_op jit(solution)/shard_map/ppermute | solution.py:54
  173.0 11.2 %collective-permute-done.9.refs_12_.refs_20_.refs_7_.refs_11_ = bf16[2,128,1024]{2,1,0:T(8,128)(2,1)} collective-permute-done((bf16[2,128,1024]{2,1,0:T(8,128)(2,1)S(1)}, bf16[2,128,1024]{2,1,0:T(8,128)(2,1)}, u32[]{:S(2)}, u32[]{:S(2)}) %collective-permute-start.9) | collective-permute-done | bytes 524320 | tf_op jit(solution)/shard_map/ppermute | solution.py:54
  184.2 15.8 %attend.1 = (f32[4,2,128,512]{3,2,1,0:T(8,128)}, bf16[4,2,128,512]{3,2,1,0:T(8,128)(2,1)}, f32[2,4,512,1]{3,2,1,0:T(8,128)}) custom-call(f32[2]{0:T(128)S(1)} %compare_convert_fusion.refs_0_, bf16[2,128,512]{2,1,0:T(8,128)(2,1)S(1)} %copy-done.4, bf16[2,128,512]{2,1,0:T(8,128)(2,1)S(1)} %copy-done.8, bf16[2,128,512]{2,1,0:T(8,128)(2,1)S(1)} %copy-done.12, ...), custom_call_target="tpu_custom_call" | custom-call | tf_op jit(solution)/shard_map/attend/pallas_call | solution.py:323
  210.0 17.0 %collective-permute-done.16 = bf16[256,2048]{1,0:T(8,128)(2,1)} collective-permute-done((bf16[256,2048]{1,0:T(8,128)(2,1)}, bf16[256,2048]{1,0:T(8,128)(2,1)}, u32[]{:S(2)}, u32[]{:S(2)}) %collective-permute-start.16) | collective-permute-done | bytes 1048608 | tf_op jit(solution)/shard_map/ppermute | solution.py:54
  232.1 19.5 %collective-permute-done.17 = bf16[256,2048]{1,0:T(8,128)(2,1)S(1)} collective-permute-done((bf16[256,2048]{1,0:T(8,128)(2,1)S(1)}, bf16[256,2048]{1,0:T(8,128)(2,1)S(1)}, u32[]{:S(2)}, u32[]{:S(2)}) %collective-permute-start.17) | collective-permute-done | bytes 1048608 | tf_op jit(solution)/shard_map/ppermute | solution.py:54
  257.5 16.1 %collective-permute-done.18 = bf16[256,2048]{1,0:T(8,128)(2,1)S(1)} collective-permute-done((bf16[256,2048]{1,0:T(8,128)(2,1)S(1)}, bf16[256,2048]{1,0:T(8,128)(2,1)S(1)}, u32[]{:S(2)}, u32[]{:S(2)}) %collective-permute-start.18) | collective-permute-done | bytes 1048608 | tf_op jit(solution)/shard_map/ppermute | solution.py:54
  310.5 11.6 %feed_up.2 = (bf16[2048,2048]{1,0:T(8,128)(2,1)}, bf16[2048,1024]{1,0:T(8,128)(2,1)}, f32[1024,4]{1,0:T(8,128)S(1)}, f32[1024,1024]{1,0:T(8,128)}) custom-call(bf16[512,2048]{1,0:T(8,128)(2,1)} %pad_maximum_fusion.2.refs_0_, bf16[512,2048]{1,0:T(8,128)(2,1)} %collective-permute-done.23.refs_1_, f32[1]{0:T(128)} %copy.205.refs_2_, f32[2048,1]{1,0:T(8,128)S(1)} %copy-done.1, ...), custom_call_target="tpu_custom_call" | custom-call | flops 4294967296 | bytes 16777216 | tf_op jit(solution)/shard_map/feed_up/pallas_call | solution.py:517
  332.6 11.1 %feed_up.3 = (bf16[2048,2048]{1,0:T(8,128)(2,1)}, bf16[2048,1024]{1,0:T(8,128)(2,1)}, f32[1024,4]{1,0:T(8,128)S(1)}, f32[1024,1024]{1,0:T(8,128)}) custom-call(bf16[512,2048]{1,0:T(8,128)(2,1)S(1)} %constant_dynamic-update-slice_fusion.8.refs_0_, bf16[512,2048]{1,0:T(8,128)(2,1)} %copy-done.88, ...), custom_call_target="tpu_custom_call", output_to_operand_aliasing={{0}: (7, {}), {1}: (8, {})} | custom-call | flops 4294967296 | bytes 16777216 | tf_op jit(solution)/shard_map/feed_up/pallas_call | solution.py:517
  344.5 14.6 %all-gather.10.cloned.1.call-done.refs_5_ = bf16[1024,2048]{1,0:T(8,128)(2,1)} async-done(((bf16[256,2048]{1,0:T(8,128)(2,1)}), bf16[1024,2048]{1,0:T(8,128)(2,1)}) %all-gather.10.cloned.1.call-update) | async-done | bytes 4194320 | tf_op jit(solution)/shard_map/all_gather | solution.py:770
  359.1 14.1 %convolution_convert_fusion.1 = bf16[1024,2048]{1,0:T(8,128)(2,1)} fusion(bf16[2048,1024]{1,0:T(8,128)(2,1)} %get-tuple-element.139.refs_3_, bf16[2048,2048]{1,0:T(8,128)(2,1)} %copy-done.107), kind=kOutput, calls=%fused_computation.22 | convolution fusion | flops 8592031744 | bytes 16777216 | tf_op jit(solution)/shard_map/dot_general | solution.py:41
  374.2 21.8 %feed_down.2 = (bf16[2048,1024]{1,0:T(8,128)(2,1)}, f32[512,4]{1,0:T(8,128)S(1)}, f32[512,4]{1,0:T(8,128)S(1)}, bf16[512,2048]{1,0:T(8,128)(2,1)S(1)}, bf16[512,...) custom-call(bf16[2048,2048]{1,0:T(8,128)(2,1)} %copy-done.107, f32[1024,4]{1,0:T(8,128)S(1)} %copy-done.40, ...), custom_call_target="tpu_custom_call" | custom-call | flops 12884901888 | bytes 25165824 | tf_op jit(solution)/shard_map/feed_down/pallas_call | solution.py:556
  410.3 21.7 %feed_down.3 = (bf16[2048,1024]{1,0:T(8,128)(2,1)}, f32[512,4]{1,0:T(8,128)S(1)}, f32[512,4]{1,0:T(8,128)S(1)}, bf16[512,2048]{1,0:T(8,128)(2,1)S(1)}, bf16[512,...) custom-call(bf16[2048,2048]{1,0:T(8,128)(2,1)} %copy-done.107, ...), custom_call_target="tpu_custom_call", output_to_operand_aliasing={{0}: (6, {})} | custom-call | flops 12884901888 | bytes 25165824 | tf_op jit(solution)/shard_map/feed_down/pallas_call | solution.py:556
  453.4 10.2 %collective-permute-done.34 = f32[128,4]{1,0:T(8,128)} collective-permute-done((f32[128,4]{1,0:T(8,128)}, f32[128,4]{1,0:T(8,128)}, u32[]{:S(2)}, u32[]{:S(2)}) %collective-permute-start.34) | collective-permute-done | bytes 2080 | tf_op jit(solution)/shard_map/ppermute | solution.py:115
  479.0 14.0 %convolution_convert_fusion.2 = bf16[2048,1024]{1,0:T(8,128)(2,1)} fusion(bf16[2048,2048]{1,0:T(8,128)(2,1)} %get-tuple-element.169, bf16[2048,1024]{1,0:T(8,128)(2,1)} %get-tuple-element.171), kind=kOutput, calls=%fused_computation.23 | convolution fusion | flops 8592031744 | bytes 16777216 | tf_op jit(solution)/shard_map/dot_general | solution.py:41
  496.0 10.1 %collective-permute-done.43 = bf16[256,2048]{1,0:T(8,128)(2,1)} collective-permute-done((bf16[256,2048]{1,0:T(8,128)(2,1)}, bf16[256,2048]{1,0:T(8,128)(2,1)}, u32[]{:S(2)}, u32[]{:S(2)}) %collective-permute-start.43) | collective-permute-done | bytes 1048608 | tf_op jit(solution)/shard_map/ppermute | solution.py:54
  520.2 12.9 %collective-permute-done.44 = bf16[256,2048]{1,0:T(8,128)(2,1)} collective-permute-done((bf16[256,2048]{1,0:T(8,128)(2,1)}, bf16[256,2048]{1,0:T(8,128)(2,1)}, u32[]{:S(2)}, u32[]{:S(2)}) %collective-permute-start.44) | collective-permute-done | bytes 1048608 | tf_op jit(solution)/shard_map/ppermute | solution.py:54
  542.9 9.3 %collective-permute-done.42 = bf16[128,2048]{1,0:T(8,128)(2,1)S(1)} collective-permute-done((bf16[128,2048]{1,0:T(8,128)(2,1)S(1)}, bf16[128,2048]{1,0:T(8,128)(2,1)S(1)}, u32[]{:S(2)}, u32[]{:S(2)}) %collective-permute-start.42) | collective-permute-done | bytes 524320 | tf_op jit(solution)/shard_map/ppermute | solution.py:115
  556.9 13.6 %collective-permute-done.45 = bf16[256,2048]{1,0:T(8,128)(2,1)} collective-permute-done((bf16[256,2048]{1,0:T(8,128)(2,1)}, bf16[256,2048]{1,0:T(8,128)(2,1)}, u32[]{:S(2)}, u32[]{:S(2)}) %collective-permute-start.45) | collective-permute-done | bytes 1048608 | tf_op jit(solution)/shard_map/ppermute | solution.py:54
  580.2 12.3 %attend_back_far.1 = (f32[4,2,128,512]{3,2,1,0:T(8,128)}, bf16[4,2,128,512]{3,2,1,0:T(8,128)(2,1)}, bf16[4,2,128,512]{3,2,1,0:T(8,128)(2,1)}) custom-call(bf16[2,128,512]{2,1,0:T(8,128)(2,1)S(1)} %copy-done.5, bf16[2,128,512]{2,1,0:T(8,128)(2,1)S(1)} %copy-done.9, bf16[2,128,512]{2,1,0:T(8,128)(2,1)S(1)} %copy-done.13, bf16[2,128,512]{2,1,0:T(8,128)(2,1)S(1)} %copy-done.17, ...), custom_call_target="tpu_custom_call" | custom-call | tf_op jit(solution)/shard_map/attend_back_far/pallas_call | solution.py:396
  604.1 12.7 %attend_back.1 = (f32[4,2,128,512]{3,2,1,0:T(8,128)}, bf16[4,2,128,512]{3,2,1,0:T(8,128)(2,1)S(1)}, bf16[4,2,128,512]{3,2,1,0:T(8,128)(2,1)}) custom-call(bf16[2,128,512]{2,1,0:T(8,128)(2,1)S(1)} %copy-done.6, bf16[2,128,512]{2,1,0:T(8,128)(2,1)S(1)} %copy-done.10, bf16[2,128,512]{2,1,0:T(8,128)(2,1)S(1)} %copy-done.14, bf16[2,128,512]{2,1,0:T(8,128)(2,1)S(1)} %copy-done.18, ...), custom_call_target="tpu_custom_call" | custom-call | tf_op jit(solution)/shard_map/attend_back/pallas_call | solution.py:396
  622.6 17.6 %collective-permute-done.48.refs_2_ = bf16[4,2,128,512]{3,2,1,0:T(8,128)(2,1)} collective-permute-done((bf16[4,2,128,512]{3,2,1,0:T(8,128)(2,1)}, bf16[4,2,128,512]{3,2,1,0:T(8,128)(2,1)}, u32[]{:S(2)}, u32[]{:S(2)}) %collective-permute-start.48) | collective-permute-done | bytes 1048608 | tf_op jit(solution)/shard_map/ppermute | solution.py:54
  640.2 7.9 fusion.76
  655.1 6.6 both_back.1
  667.3 8.9 %convolution_convert_fusion = bf16[2048,1536]{1,0:T(8,128)(2,1)S(1)} fusion(bf16[1024,1536]{1,0:T(8,128)(2,1)S(1)} %bitcast.229, bf16[256,2048]{1,0:T(8,128)(2,1)} %copy-done.96, bf16[256,2048]{1,0:T(8,128)(2,1)} %copy-done.95, bf16[256,2048]{1,0:T(8,128)(2,1)} %copy-done.94, bf16[256,2048]{1,0:T(8,128)(2,1)} %copy-done.93), kind=kOutput, calls=%fused_computation | convolution fusion | flops 6462373888 | bytes 13631488 | tf_op jit(solution)/shard_map/dot_general | solution.py:41
  693.9 13.6 %collective-permute-done.50 = bf16[256,2048]{1,0:T(8,128)(2,1)} collective-permute-done((bf16[256,2048]{1,0:T(8,128)(2,1)}, bf16[256,2048]{1,0:T(8,128)(2,1)}, u32[]{:S(2)}, u32[]{:S(2)}) %collective-permute-start.50) | collective-permute-done | bytes 1048608 | tf_op jit(solution)/shard_map/ppermute | solution.py:54
  726.3 11.0 %collective-permute-done.52 = bf16[256,2048]{1,0:T(8,128)(2,1)} collective-permute-done((bf16[256,2048]{1,0:T(8,128)(2,1)}, bf16[256,2048]{1,0:T(8,128)(2,1)}, u32[]{:S(2)}, u32[]{:S(2)}) %collective-permute-start.52) | collective-permute-done | bytes 1048608 | tf_op jit(solution)/shard_map/ppermute | solution.py:54
  788.7 6.3 collective-permute-done.63.refs_3_
  (595 shorter events, 350.1 us)
Async XLA Ops:
  7.2 118.9 %all-gather.6.cloned.1.call-start = ((), (), s32[]{:S(2)}) async-start(), calls=%async_computation.5 | async-start | bytes 2359296 | tf_op jit(solution)/shard_map/all_gather | solution.py:697
  26.1 100.1 %all-gather.12.cloned.1.call-start = ((), (), s32[]{:S(2)}) async-start(), calls=%async_computation.11 | async-start | bytes 8847360 | tf_op jit(solution)/shard_map/all_gather | solution.py:688
  47.1 162.9 %all-gather.8.cloned.1.call-start = ((), (), s32[]{:S(2)}) async-start(), calls=%async_computation.6 | async-start | bytes 5242880 | tf_op jit(solution)/shard_map/all_gather | solution.py:700
  48.4 26.8 %collective-permute-start = (bf16[256,2048]{1,0:T(8,128)(2,1)S(1)}, bf16[256,2048]{1,0:T(8,128)(2,1)S(1)}, u32[]{:S(2)}, u32[]{:S(2)}) collective-permute-start(bf16[256,2048]{1,0:T(8,128)(2,1)S(1)} %bitcast.218), channel_id=1, source_target_pairs={{0,8},{8,16},{16,24},{24,0},{1,9},{9,17},{17,25},{25,1},{2,10},{10... | collective-permute-start | bytes 3145736 | tf_op jit(solution)/shard_map/ppermute | solution.py:54
  52.4 100.7 %collective-permute-start.11 = (bf16[128,2048]{1,0:T(8,128)(2,1)}, bf16[128,2048]{1,0:T(8,128)(2,1)}, u32[]{:S(2)}, u32[]{:S(2)}) collective-permute-start(bf16[128,2048]{1,0:T(8,128)(2,1)} %get-tuple-element.327), channel_id=1, source_target_pairs={{0,4},{4,0},{1,5},{5,1},{2,6},{6,2},{3,7},{7,3},{8,12},{12,8},{9,1... | collective-permute-start | bytes 1572872 | tf_op jit(solution)/shard_map/ppermute | solution.py:115
  53.5 102.7 %collective-permute-start.10 = (bf16[128,2048]{1,0:T(8,128)(2,1)}, bf16[128,2048]{1,0:T(8,128)(2,1)}, u32[]{:S(2)}, u32[]{:S(2)}) collective-permute-start(bf16[128,2048]{1,0:T(8,128)(2,1)} %get-tuple-element.328), channel_id=1, source_target_pairs={{0,2},{2,0},{1,3},{3,1},{4,6},{6,4},{5,7},{7,5},{8,10},{10,8},{9,1... | collective-permute-start | bytes 1572872 | tf_op jit(solution)/shard_map/ppermute | solution.py:115
  75.2 25.9 %collective-permute-start.1 = (bf16[256,2048]{1,0:T(8,128)(2,1)S(1)}, bf16[256,2048]{1,0:T(8,128)(2,1)S(1)}, u32[]{:S(2)}, u32[]{:S(2)}) collective-permute-start(bf16[256,2048]{1,0:T(8,128)(2,1)S(1)} %collective-permute-done), channel_id=1, source_target_pairs={{0,8},{8,16},{16,24},{24,0},{1,9},{9,17},{17,25},{25,1},{2,10},{10... | collective-permute-start | bytes 3145736 | tf_op jit(solution)/shard_map/ppermute | solution.py:54
  126.1 232.9 %all-gather.10.cloned.1.call-start = ((), (), s32[]{:S(2)}) async-start(), calls=%async_computation.7 | async-start | bytes 5242880 | tf_op jit(solution)/shard_map/all_gather | solution.py:770
  145.8 27.2 %collective-permute-start.8 = (bf16[2,128,1024]{2,1,0:T(8,128)(2,1)S(1)}, bf16[2,128,1024]{2,1,0:T(8,128)(2,1)}, u32[]{:S(2)}, u32[]{:S(2)}) collective-permute-start(bf16[2,128,1024]{2,1,0:T(8,128)(2,1)S(1)} %get-tuple-element.124.refs_7_.refs_15_.refs_6_.refs_10_), channel_id=1, source_target_pairs={{0,4},{4,0},{1,5},{5,1},{2,6},{6,2},{3,7},{7,3},{8,12},{12,8},{9,1... | collective-permute-start | bytes 1572872 | tf_op jit(solution)/shard_map/ppermute | solution.py:54
  153.1 31.1 %collective-permute-start.9 = (bf16[2,128,1024]{2,1,0:T(8,128)(2,1)S(1)}, bf16[2,128,1024]{2,1,0:T(8,128)(2,1)}, u32[]{:S(2)}, u32[]{:S(2)}) collective-permute-start(bf16[2,128,1024]{2,1,0:T(8,128)(2,1)S(1)} %get-tuple-element.127.refs_8_.refs_16_.refs_7_.refs_11_), channel_id=1, source_target_pairs={{0,4},{4,0},{1,5},{5,1},{2,6},{6,2},{3,7},{7,3},{8,12},{12,8},{9,1... | collective-permute-start | bytes 1572872 | tf_op jit(solution)/shard_map/ppermute | solution.py:54
  156.2 51.3 %collective-permute-start.14 = (bf16[256,2048]{1,0:T(8,128)(2,1)S(1)}, bf16[256,2048]{1,0:T(8,128)(2,1)S(1)}, u32[]{:S(2)}, u32[]{:S(2)}) collective-permute-start(bf16[256,2048]{1,0:T(8,128)(2,1)S(1)} %pad_maximum_fusion.4), channel_id=1, source_target_pairs={{0,2},{2,0},{1,3},{3,1},{4,6},{6,4},{5,7},{7,5},{8,10},{10,8},{9,1... | collective-permute-start | bytes 3145736 | tf_op jit(solution)/shard_map/ppermute | solution.py:115
  157.9 49.6 %collective-permute-start.13 = (bf16[256,2048]{1,0:T(8,128)(2,1)S(1)}, bf16[256,2048]{1,0:T(8,128)(2,1)S(1)}, u32[]{:S(2)}, u32[]{:S(2)}) collective-permute-start(bf16[256,2048]{1,0:T(8,128)(2,1)S(1)} %pad_maximum_fusion.3), channel_id=1, source_target_pairs={{0,4},{4,0},{1,5},{5,1},{2,6},{6,2},{3,7},{7,3},{8,12},{12,8},{9,1... | collective-permute-start | bytes 3145736 | tf_op jit(solution)/shard_map/ppermute | solution.py:115
  207.5 45.0 %collective-permute-start.12 = (bf16[512,2048]{1,0:T(8,128)(2,1)}, bf16[512,2048]{1,0:T(8,128)(2,1)}, u32[]{:S(2)}, u32[]{:S(2)}) collective-permute-start(bf16[512,2048]{1,0:T(8,128)(2,1)} %pad_maximum_fusion), channel_id=1, source_target_pairs={{0,1},{1,0},{2,3},{3,2},{4,5},{5,4},{6,7},{7,6},{8,9},{9,8},{10,11... | collective-permute-start | bytes 6291464 | tf_op jit(solution)/shard_map/ppermute | solution.py:115
  209.5 46.2 %collective-permute-start.15 = (bf16[512,2048]{1,0:T(8,128)(2,1)}, bf16[512,2048]{1,0:T(8,128)(2,1)}, u32[]{:S(2)}, u32[]{:S(2)}) collective-permute-start(bf16[512,2048]{1,0:T(8,128)(2,1)} %pad_maximum_fusion.1), channel_id=1, source_target_pairs={{0,1},{1,0},{2,3},{3,2},{4,5},{5,4},{6,7},{7,6},{8,9},{9,8},{10,11... | collective-permute-start | bytes 6291464 | tf_op jit(solution)/shard_map/ppermute | solution.py:115
  281.4 196.6 %reduce-scatter.4.cloned.1.call-start = ((), (), s32[]{:S(2)}) async-start(), calls=%async_computation.8 | async-start | bytes 5242880 | tf_op jit(solution)/shard_map/reduce_scatter | solution.py:818
  294.8 27.3 %collective-permute-start.22 = (bf16[256,2048]{1,0:T(8,128)(2,1)}, bf16[256,2048]{1,0:T(8,128)(2,1)}, u32[]{:S(2)}, u32[]{:S(2)}) collective-permute-start(bf16[256,2048]{1,0:T(8,128)(2,1)} %pad_maximum_fusion.6), channel_id=1, source_target_pairs={{0,2},{2,0},{1,3},{3,1},{4,6},{6,4},{5,7},{7,5},{8,10},{10,8},{9,1... | collective-permute-start | bytes 3145736 | tf_op jit(solution)/shard_map/ppermute | solution.py:115
  298.6 25.6 %collective-permute-start.20 = (bf16[256,2048]{1,0:T(8,128)(2,1)}, bf16[256,2048]{1,0:T(8,128)(2,1)}, u32[]{:S(2)}, u32[]{:S(2)}) collective-permute-start(bf16[256,2048]{1,0:T(8,128)(2,1)} %pad_maximum_fusion.5), channel_id=1, source_target_pairs={{0,4},{4,0},{1,5},{5,1},{2,6},{6,2},{3,7},{7,3},{8,12},{12,8},{9,1... | collective-permute-start | bytes 3145736 | tf_op jit(solution)/shard_map/ppermute | solution.py:115
  398.8 268.5 %reduce-scatter.6.cloned.1.call-start = ((), (), s32[]{:S(2)}) async-start(), calls=%async_computation.9 | async-start | bytes 5242880 | tf_op jit(solution)/shard_map/reduce_scatter | solution.py:932
  407.1 25.4 %collective-permute-start.26 = (bf16[256,2048]{1,0:T(8,128)(2,1)S(1)}, bf16[256,2048]{1,0:T(8,128)(2,1)S(1)}, u32[]{:S(2)}, u32[]{:S(2)}) collective-permute-start(bf16[256,2048]{1,0:T(8,128)(2,1)S(1)} %get-tuple-element.317), channel_id=1, source_target_pairs={{0,4},{4,0},{1,5},{5,1},{2,6},{6,2},{3,7},{7,3},{8,12},{12,8},{9,1... | collective-permute-start | bytes 3145736 | tf_op jit(solution)/shard_map/ppermute | solution.py:115
  478.1 28.1 %collective-permute-start.43 = (bf16[256,2048]{1,0:T(8,128)(2,1)}, bf16[256,2048]{1,0:T(8,128)(2,1)}, u32[]{:S(2)}, u32[]{:S(2)}) collective-permute-start(bf16[256,2048]{1,0:T(8,128)(2,1)} %get-tuple-element.164), channel_id=1, source_target_pairs={{0,8},{8,16},{16,24},{24,0},{1,9},{9,17},{17,25},{25,1},{2,10},{10... | collective-permute-start | bytes 3145736 | tf_op jit(solution)/shard_map/ppermute | solution.py:54
  478.5 37.2 %collective-permute-start.37 = (bf16[512,2048]{1,0:T(8,128)(2,1)}, bf16[512,2048]{1,0:T(8,128)(2,1)}, u32[]{:S(2)}, u32[]{:S(2)}) collective-permute-start(bf16[512,2048]{1,0:T(8,128)(2,1)} %get-tuple-element.166), channel_id=1, source_target_pairs={{0,1},{1,0},{2,3},{3,2},{4,5},{5,4},{6,7},{7,6},{8,9},{9,8},{10,11... | collective-permute-start | bytes 6291464 | tf_op jit(solution)/shard_map/ppermute | solution.py:115
  506.1 26.9 %collective-permute-start.44 = (bf16[256,2048]{1,0:T(8,128)(2,1)}, bf16[256,2048]{1,0:T(8,128)(2,1)}, u32[]{:S(2)}, u32[]{:S(2)}) collective-permute-start(bf16[256,2048]{1,0:T(8,128)(2,1)} %collective-permute-done.43), channel_id=1, source_target_pairs={{0,8},{8,16},{16,24},{24,0},{1,9},{9,17},{17,25},{25,1},{2,10},{10... | collective-permute-start | bytes 3145736 | tf_op jit(solution)/shard_map/ppermute | solution.py:54
  507.6 28.6 %collective-permute-start.39 = (bf16[256,2048]{1,0:T(8,128)(2,1)}, bf16[256,2048]{1,0:T(8,128)(2,1)}, u32[]{:S(2)}, u32[]{:S(2)}) collective-permute-start(bf16[256,2048]{1,0:T(8,128)(2,1)} %get-tuple-element.313), channel_id=1, source_target_pairs={{0,4},{4,0},{1,5},{5,1},{2,6},{6,2},{3,7},{7,3},{8,12},{12,8},{9,1... | collective-permute-start | bytes 3145736 | tf_op jit(solution)/shard_map/ppermute | solution.py:115
  509.1 27.2 %collective-permute-start.41 = (bf16[256,2048]{1,0:T(8,128)(2,1)}, bf16[256,2048]{1,0:T(8,128)(2,1)}, u32[]{:S(2)}, u32[]{:S(2)}) collective-permute-start(bf16[256,2048]{1,0:T(8,128)(2,1)} %get-tuple-element.314), channel_id=1, source_target_pairs={{0,2},{2,0},{1,3},{3,1},{4,6},{6,4},{5,7},{7,5},{8,10},{10,8},{9,1... | collective-permute-start | bytes 3145736 | tf_op jit(solution)/shard_map/ppermute | solution.py:115
  542.8 27.7 %collective-permute-start.45 = (bf16[256,2048]{1,0:T(8,128)(2,1)}, bf16[256,2048]{1,0:T(8,128)(2,1)}, u32[]{:S(2)}, u32[]{:S(2)}) collective-permute-start(bf16[256,2048]{1,0:T(8,128)(2,1)} %collective-permute-done.44), channel_id=1, source_target_pairs={{0,8},{8,16},{16,24},{24,0},{1,9},{9,17},{17,25},{25,1},{2,10},{10... | collective-permute-start | bytes 3145736 | tf_op jit(solution)/shard_map/ppermute | solution.py:54
  570.5 121.6 %reduce-scatter.8.cloned.1.call-start = ((), (), s32[]{:S(2)}) async-start(), calls=%async_computation.10 | async-start | bytes 2359296 | tf_op jit(solution)/shard_map/reduce_scatter | solution.py:999
  592.6 30.0 %collective-permute-start.47 = (bf16[4,2,128,512]{3,2,1,0:T(8,128)(2,1)}, bf16[4,2,128,512]{3,2,1,0:T(8,128)(2,1)}, u32[]{:S(2)}, u32[]{:S(2)}) collective-permute-start(bf16[4,2,128,512]{3,2,1,0:T(8,128)(2,1)} %get-tuple-element.190), channel_id=1, source_target_pairs={{0,4},{4,0},{1,5},{5,1},{2,6},{6,2},{3,7},{7,3},{8,12},{12,8},{9,1... | collective-permute-start | bytes 3145736 | tf_op jit(solution)/shard_map/ppermute | solution.py:54
  593.1 47.1 %collective-permute-start.48 = (bf16[4,2,128,512]{3,2,1,0:T(8,128)(2,1)}, bf16[4,2,128,512]{3,2,1,0:T(8,128)(2,1)}, u32[]{:S(2)}, u32[]{:S(2)}) collective-permute-start(bf16[4,2,128,512]{3,2,1,0:T(8,128)(2,1)} %get-tuple-element.192), channel_id=1, source_target_pairs={{0,4},{4,0},{1,5},{5,1},{2,6},{6,2},{3,7},{7,3},{8,12},{12,8},{9,1... | collective-permute-start | bytes 3145736 | tf_op jit(solution)/shard_map/ppermute | solution.py:54
  679.8 30.6 %collective-permute-start.51 = (bf16[4,2,2,64,1536]{4,3,0,1,2:T(8,128)(2,1)}, bf16[4,2,2,64,1536]{4,3,0,1,2:T(8,128)(2,1)}, u32[]{:S(2)}, u32[]{:S(2)}) collective-permute-start(bf16[4,2,2,64,1536]{4,3,0,1,2:T(8,128)(2,1)} %copy_bitcast_fusion), channel_id=1, source_target_pairs={{0,1},{1,0},{2,3},{3,2},{4,5},{5,4},{6,7},{7,6},{8,9},{9,8},{10,11... | collective-permute-start | bytes 9437192 | tf_op jit(solution)/shard_map/ppermute | solution.py:115
  679.8 27.7 %collective-permute-start.50 = (bf16[256,2048]{1,0:T(8,128)(2,1)}, bf16[256,2048]{1,0:T(8,128)(2,1)}, u32[]{:S(2)}, u32[]{:S(2)}) collective-permute-start(bf16[256,2048]{1,0:T(8,128)(2,1)} %fusion.45), channel_id=1, source_target_pairs={{0,8},{8,16},{16,24},{24,0},{1,9},{9,17},{17,25},{25,1},{2,10},{10... | collective-permute-start | bytes 3145736 | tf_op jit(solution)/shard_map/ppermute | solution.py:54
  710.4 26.9 %collective-permute-start.52 = (bf16[256,2048]{1,0:T(8,128)(2,1)}, bf16[256,2048]{1,0:T(8,128)(2,1)}, u32[]{:S(2)}, u32[]{:S(2)}) collective-permute-start(bf16[256,2048]{1,0:T(8,128)(2,1)} %add_convert_fusion.5), channel_id=1, source_target_pairs={{0,8},{8,16},{16,24},{24,0},{1,9},{9,17},{17,25},{25,1},{2,10},{10... | collective-permute-start | bytes 3145736 | tf_op jit(solution)/shard_map/ppermute | solution.py:54
  715.9 50.5 %all-to-all-start.1 = ((bf16[8,64,1024]{2,1,0:T(8,128)(2,1)}), bf16[8,64,1024]{2,1,0:T(8,128)(2,1)S(1)}, u32[]{:S(2)}, u32[]{:S(2)}) async-start(bf16[8,64,1024]{2,1,0:T(8,128)(2,1)} %bitcast.88), calls=%async_computation.3 | async-start | bytes 2097152 | tf_op jit(solution)/shard_map/all_to_all | solution.py:1019
  (166 other events, 1899.4 us)
Sparse Core Ops, SparseCore 0:
  9.9 36.2 all-gather.5
  48.7 59.3 all-gather.11
  126.3 80.0 all-gather.7
  281.6 77.4 all-gather.9
  398.9 75.4 reduce-scatter.3
  570.6 73.8 reduce-scatter.5
  653.9 38.2 reduce-scatter.7
